TPU v7x, 256 devices: a whole 4x4x8 slice. The times are simulated.
256 devices in a mesh: row: 4 (over x), col: 32 (over y, z), rep: 2 (over core).
Axes of the slice: x: 4, y: 4, z: 8, core: 2. Of those that a mesh axis runs over, the one named last changes fastest.
Arguments:
- amplitudes: bfloat16 [16384, 16384], P(('row', 'col'), 'rep'), may hold values from -6 to 6
- cycle_integrals: bfloat16 [16384, 1024], P('rep', ('row', 'col')), may hold values from -0.046875 to 0.046875
- amp_map: int32 [128, 128], P(('row', 'col'), 'rep'), may hold values 0 or 1
- cycle_map: int32 [128, 128], replicated, may hold values 0 or 1
Outputs:
- dressed: bfloat16 [16384, 1024], P(('row', 'col'), 'rep')
- quadratic: bfloat16 [16384, 16384], P(('row', 'col'), 'rep')
All inputs are finite; a program needn't handle non-finite values. No bound on the sum of `amp_map` on one device may be relied on, other than what follows from the above.
Results may differ from a plain program's by a relative error of at most 0.0049.
Values may be sent and summed in bfloat16 or wider, within the bound.
No kernel may reach another device: no remote copies, remote signals or barrier semaphores. Data moves between devices by JAX's collectives and lax.ppermute only.
A program may use at most 128 MiB of HBM per device.

v0:
```python
import jax
import jax.numpy as jnp
from jax import lax
from jax.sharding import PartitionSpec as P

TB = 128
WD = 8


def expand(tile_map, rows, cols):
    return jnp.repeat(jnp.repeat(tile_map, rows, 0), cols, 1).astype(jnp.bfloat16)


def body(amplitudes, cycle_integrals, amp_map, cycle_map):
    replica = lax.axis_index("rep")
    masked_amp = amplitudes * expand(amp_map, TB, TB)
    half_rows = cycle_integrals.shape[0]
    tile_rows = half_rows // TB
    cycle_rows = lax.dynamic_slice_in_dim(cycle_map, replica * tile_rows, tile_rows, 0)
    cycle_mask = expand(cycle_rows, TB, WD)
    partial_value = jnp.dot(
        masked_amp,
        lax.all_gather(cycle_integrals, ("row", "col"), axis=1, tiled=True) * cycle_mask,
        preferred_element_type=jnp.float32,
    )
    dressed = lax.psum_scatter(partial_value, "rep", scatter_dimension=1, tiled=True).astype(
        jnp.bfloat16
    )
    full_x = lax.all_gather(dressed, "rep", axis=1, tiled=True)
    window_own = masked_amp[:WD]
    window = lax.all_gather(window_own, ("row", "col"), axis=0, tiled=True)
    quadratic = jnp.dot(full_x, window, preferred_element_type=jnp.float32).astype(jnp.bfloat16)
    return (dressed, quadratic)


def solution(mesh):
    placed = (P(("row", "col"), "rep"), P("rep", ("row", "col")), P(("row", "col"), "rep"), P())
    return jax.shard_map(
        body,
        mesh=mesh,
        in_specs=placed,
        out_specs=(P(("row", "col"), "rep"), P(("row", "col"), "rep")),
        check_vma=False,
    )
```

profile of v0, /device:TPU:0, one launch (start us, length us, event | category | flops | bytes accessed | tf_op | source)
XLA Modules:
  0.0 356.9 jit_solution(6451195734484579230)
XLA Ops:
  7.2 0.0 all-gather.3.cloned.1.call-start
  7.2 0.7 all-gather.3.cloned.1.call-update
  7.9 0.0 reduce-scatter.2.cloned.1.call-start
  8.0 0.8 dynamic-slice_convert_fusion
  8.7 0.1 copy.6
  8.8 1.6 broadcast_in_dim.14
  10.5 0.0 copy-start.2
  10.5 0.0 copy-start
  10.5 3.1 copy.9
  13.6 0.1 broadcast_bitcast_fusion
  13.7 0.0 copy-done
  13.7 0.2 broadcast_multiply_fusion
  13.9 149.6 %all-gather.3.cloned.1.call-done = bf16[8192,1024]{0,1:T(8,128)(2,1)} async-done(((bf16[8192,8]{0,1:T(8,128)(2,1)}), bf16[8192,1024]{0,1:T(8,128)(2,1)}) %all-gather.3.cloned.1.call-update) | async-done | bytes 16777232 | tf_op jit(solution)/shard_map/all_gather | solution.py:23
  163.5 10.2 %fusion = f32[128,1024]{1,0:T(8,128)} fusion(bf16[128,8192]{1,0:T(8,128)(2,1)S(1)} %broadcast_multiply_fusion, bf16[8192,1024]{0,1:T(8,128)(2,1)} %all-gather.3.cloned.1.call-done, bf16[8192,128]{0,1:T(8,128)(2,1)} %bitcast.17), kind=kOutput, calls=%fused_computation.1 | convolution fusion | flops 2155872256 | bytes 21495808 | tf_op jit(solution)/shard_map/dot_general | solution.py:21
  173.6 0.0 reduce-scatter.2.cloned.1.call-update
  173.7 0.0 all-gather.5.cloned.1.call-start
  173.7 0.7 slice.4
  174.4 0.0 all-gather.5.cloned.1.call-update
  174.4 9.7 %reduce-scatter.2.cloned.1.call-done = f32[128,512]{1,0:T(8,128)} async-done(((f32[128,1024]{1,0:T(8,128)}), f32[128,512]{1,0:T(8,128)}) %reduce-scatter.2.cloned.1.call-update) | async-done | bytes 262160 | tf_op jit(solution)/shard_map/reduce_scatter | solution.py:26
  184.1 1.0 convert_element_type.34
  185.1 0.0 copy-start.1
  185.1 2.3 all_gather.10
  187.4 153.5 %all-gather.5.cloned.1.call-done = bf16[1024,8192]{1,0:T(8,128)(2,1)} async-done(((bf16[8,8192]{1,0:T(8,128)(2,1)}), bf16[1024,8192]{1,0:T(8,128)(2,1)}) %all-gather.5.cloned.1.call-update) | async-done | bytes 16777232 | tf_op jit(solution)/shard_map/all_gather | solution.py:31
  340.9 9.4 %convolution_convert_fusion = bf16[128,8192]{1,0:T(8,128)(2,1)} fusion(bf16[128,1024]{1,0:T(8,128)(2,1)S(1)} %all_gather.10, bf16[1024,8192]{1,0:T(8,128)(2,1)} %all-gather.5.cloned.1.call-done), kind=kOutput, calls=%fused_computation.2 | convolution fusion | flops 2148532224 | bytes 19136512 | tf_op jit(solution)/shard_map/dot_general | solution.py:32
  (3 shorter events, 0.0 us)
Async XLA Ops:
  7.2 156.3 %all-gather.3.cloned.1.call-start = ((), (), s32[]{:S(2)}) async-start(), calls=%async_computation.1 | async-start | bytes 16908288 | tf_op jit(solution)/shard_map/all_gather | solution.py:23
  7.9 176.2 %reduce-scatter.2.cloned.1.call-start = ((), (), s32[]{:S(2)}) async-start(), calls=%async_computation.2 | async-start | bytes 786432 | tf_op jit(solution)/shard_map/reduce_scatter | solution.py:26
  10.5 3.2 copy-start.2
  10.5 3.2 copy-start
  173.7 167.2 %all-gather.5.cloned.1.call-start = ((), (), s32[]{:S(2)}) async-start(), calls=%async_computation.3 | async-start | bytes 16908288 | tf_op jit(solution)/shard_map/all_gather | solution.py:31
  185.1 165.3 %copy-start.1 = (bf16[128,512]{1,0:T(8,128)(2,1)}, bf16[128,512]{1,0:T(8,128)(2,1)S(1)}, u32[]{:S(2)}) copy-start(bf16[128,512]{1,0:T(8,128)(2,1)S(1)} %convert_element_type.34) | copy-start | bytes 393220
Sparse Core Ops, SparseCore 0:
  11.6 151.7 all-gather.2
  173.8 10.2 reduce-scatter.1
  188.9 151.9 all-gather.4
where the time goes:
time: 359 us; the launch traced here: 357 us
  waiting for transfers between devices  314 us (87%)
  matrix products  19.6 us (5%)
  between operations  13.8 us (4%)
  local copies, waits for them, and re-layouts  5.65 us (2%)
    all_gather x1, waiting for transfers between devices, body(): window = lax.all_gather(window_own, ('row', 'col'), axis=0, tiled=True)  154 us
    all_gather x1, waiting for transfers between devices, body(): lax.all_gather(cycle_integrals, ('row', 'col'), axis=1, tiled=True)  150 us
    dot_general x1, matrix products, body(): jnp.dot(masked_amp, lax.all_gather(cycle_integrals, ('row', 'col'), axis=...  10.2 us
    reduce_scatter x1, waiting for transfers between devices, body(): lax.psum_scatter(partial_value, 'rep', scatter_dimension=1, tiled=True)  9.72 us
    dot_general x1, matrix products, body(): jnp.dot(full_x, window, preferred_element_type=jnp.float32)  9.44 us
  transfers between devices with their start and end apart: 3, of which 3 were waited for; matrix products, arithmetic and copies ran while one was open for 2% of the time, Pallas kernels for 0%

commit v1 on v0

v1 whole, which is shorter than its diff:
```python
import jax
import jax.numpy as jnp
from jax import lax
from jax.sharding import PartitionSpec as P

TB = 128
WD = 8
NX, NY, NZ = 4, 4, 8
AX = ("row", "col", "rep")
F32, BF = jnp.float32, jnp.bfloat16


def ident(x, y, z, c):
    return ((x % NX) * NY * NZ + (y % NY) * NZ + z % NZ) * 2 + c


def every():
    return [(x, y, z, c) for x in range(NX) for y in range(NY) for z in range(NZ) for c in (0, 1)]


def shift_z(value, step):
    return lax.ppermute(value, AX, [(ident(x, y, z, c), ident(x, y, z + step, c)) for x, y, z, c in every()])


def shift_plane(value, step, swapped):
    pairs = []
    for x, y, z, c in every():
        if (c == 0) != swapped:
            pairs.append((ident(x, y, z, c), ident(x + step, y, z, c)))
        else:
            pairs.append((ident(x, y, z, c), ident(x, y + step, z, c)))
    return lax.ppermute(value, AX, pairs)


def shift_g(value, step):
    return shift_plane(value, step, False)


def shift_p(value, step):
    return shift_plane(value, step, True)


def swap_core(value):
    return lax.ppermute(value, AX, [(ident(x, y, z, c), ident(x, y, z, 1 - c)) for x, y, z, c in every()])


def unroll_ring(pieces, place):
    count, rows = len(pieces), pieces[0].shape[0]
    twice = jnp.concatenate(pieces + pieces, 0)
    return lax.dynamic_slice_in_dim(twice, ((count - place) % count) * rows, count * rows, 0)


def body(amplitudes, cycle_integrals, amp_map, cycle_map):
    row, col, core = (lax.axis_index(a) for a in AX)
    x, y, z = row, col // NZ, col % NZ
    g = jnp.where(core == 0, x, y)
    p = jnp.where(core == 0, y, x)
    half = amplitudes.shape[1]
    part = half // 4

    amp_mask = jnp.repeat(amp_map, TB, 1).astype(BF)

    def columns(value, index):
        return lax.dynamic_slice_in_dim(value, (index % 4) * part, part, 1)

    sends = [columns(amplitudes, g + d) * columns(amp_mask, g + d) for d in range(4)]
    blocks = [sends[0]] + [shift_g(sends[d], d) for d in (1, 2, 3)]

    tiles = half // TB
    own_column = lax.dynamic_slice(cycle_map, (core * tiles, row * NY * NZ + col), (tiles, 1))
    cyc = cycle_integrals.T * jnp.repeat(own_column.reshape(1, tiles), TB, 1).astype(BF)
    cyc = cyc.reshape(WD, 4, part).transpose(1, 0, 2)
    send = jnp.where(core == 0, cyc[:, None], cyc[None]).reshape(16 * WD, part)
    plane = [[i * NY * NZ + j * NZ + k for i in range(NX) for j in range(NY)] for k in range(NZ)]
    cyc = lax.all_to_all(send, ("row", "col"), 0, 0, tiled=True, axis_index_groups=plane)
    rings = [[j * NZ + k for k in range(NZ)] for j in range(NY)]
    cyc = lax.all_gather(cyc, "col", axis=0, tiled=True, axis_index_groups=rings)

    win = amplitudes[:WD] * amp_mask
    f, b = shift_z(win, 1), shift_z(win, -1)
    f2, b2 = shift_z(f, 1), shift_z(b, -1)
    f3, b3 = shift_z(f2, 1), shift_z(b2, -1)
    b4 = shift_z(b3, -1)
    win = unroll_ring([win, b, b2, b3, b4, f3, f2, f], z)
    pieces = [columns(win, g)] + [shift_g(columns(win, g - d), -d) for d in (1, 2, 3)]
    win = unroll_ring(pieces, g)
    f, b = shift_p(win, 1), shift_p(win, -1)
    rows = win.shape[0] // 2
    far = jnp.concatenate([shift_p(b[:rows], -1), shift_p(f[rows:], 1)], 0)
    win = unroll_ring([win, b, far, f], p)

    def times(a, b):
        return lax.dot_general(a, b, (((1,), (1,)), ((), ())), preferred_element_type=F32)

    total = times(blocks[0], cyc)
    for d in (2, 1, 3):
        total = total + shift_g(times(blocks[d], cyc).astype(BF), -d).astype(F32)
    full = (total + swap_core(total)).astype(BF)
    width = full.shape[1]
    here = lax.broadcasted_iota(jnp.int32, (width, 1), 0)
    hz, hx, hy, hw = here // 128, here // 32 % 4, here // 8 % 4, here % 8
    there = lax.broadcasted_iota(jnp.int32, (1, width // 2), 1) + core * (width // 2)
    place = hx * 256 + hy * 64 + hz * 8 + hw
    dressed = jnp.dot(full, (place == there).astype(BF), preferred_element_type=F32).astype(BF)
    hg, hp = jnp.where(core == 0, hx, hy), jnp.where(core == 0, hy, hx)
    place = hp * 256 + hg * 64 + hz * 8 + hw
    there = lax.broadcasted_iota(jnp.int32, (1, width), 1)
    inner = jnp.dot(full, (place == there).astype(BF), preferred_element_type=F32).astype(BF)

    inners = [inner] + [shift_g(inner, d) for d in (1, 2, 3)]
    outs = [None] * 4
    for d in (2, 1, 3, 0):
        value = jnp.dot(inners[d], win, preferred_element_type=F32).astype(BF)
        outs[d] = shift_g(value, -d) if d else value
    quadratic = jnp.zeros((inner.shape[0], half), BF)
    for d in range(4):
        quadratic = lax.dynamic_update_slice_in_dim(quadratic, outs[d], ((g + d) % 4) * part, 1)
    return (dressed, quadratic)


def solution(mesh):
    placed = (P(("row", "col"), "rep"), P("rep", ("row", "col")), P(("row", "col"), "rep"), P())
    return jax.shard_map(
        body,
        mesh=mesh,
        in_specs=placed,
        out_specs=(P(("row", "col"), "rep"), P(("row", "col"), "rep")),
        check_vma=False,
    )
```

time: 359 us -> 172 us (0.48)
  waiting for transfers between devices: 314 us -> 60.1 us
  starting transfers between devices: 0.12 us -> 46.7 us
  local copies, waits for them, and re-layouts: 5.65 us -> 24.6 us
  other arithmetic: 1.89 us -> 7.28 us
    all_gather x2 -> x1, waiting for transfers between devices: 303 us -> 0.01 us  [body(): lax.all_gather(cyc, 'col', axis=0, tiled=True, axis_index_groups=rings)]
    ppermute x0 -> x27, waiting for transfers between devices: none -> 60.1 us  [the longest x19 53.5 us: shift_plane(): return lax.ppermute(value, AX, pairs)]
    ppermute x0 -> x27, starting transfers between devices: none -> 39.6 us  [the longest x19 24.6 us: shift_plane(): return lax.ppermute(value, AX, pairs)]
    unnamed x7 -> x40, local copies, waits for them, and re-layouts: 3.16 us -> 20.2 us
    reduce_scatter x1 -> x0, waiting for transfers between devices: 9.72 us -> none  [body(): lax.psum_scatter(partial_value, 'rep', scatter_dimension=1, tiled=True)]
    all_to_all x0 -> x1, starting transfers between devices: none -> 7.03 us  [body(): lax.all_to_all(send, ('row', 'col'), 0, 0, tiled=True, axis_index_groups=...]
    dot_general x2 -> x10, matrix products: 19.6 us -> 17 us  [the longest x4 11.8 us: times(): lax.dot_general(a, b, (((1,), (1,)), ((), ())), preferred_element_type=F32)]
  transfers between devices with their start and end apart: 3 -> 29, of which waited for: 3 -> 16; matrix products, arithmetic and copies ran while one was open for 2% -> 26% of each run, Pallas kernels for 0% -> 0%
where the time goes in v1:
time: 172 us; the launch traced here: 170 us
  waiting for transfers between devices  60.1 us (35%)
  starting transfers between devices  46.7 us (27%)
  local copies, waits for them, and re-layouts  24.6 us (14%)
  matrix products  17 us (10%)
  between operations  14.6 us (8%)
  other arithmetic  7.28 us (4%)
    ppermute x19, waiting for transfers between devices, shift_plane(): return lax.ppermute(value, AX, pairs)  53.5 us
    ppermute x19, starting transfers between devices, shift_plane(): return lax.ppermute(value, AX, pairs)  24.6 us
    unnamed x40, local copies, waits for them, and re-layouts  20.2 us
    ppermute x7, starting transfers between devices, shift_z(): lax.ppermute(value, AX, [(ident(x, y, z, c), ident(x, y, z + step, c)) fo...  14.9 us
    dot_general x4, matrix products, times(): lax.dot_general(a, b, (((1,), (1,)), ((), ())), preferred_element_type=F32)  11.8 us
    all_to_all x1, starting transfers between devices, body(): lax.all_to_all(send, ('row', 'col'), 0, 0, tiled=True, axis_index_groups=...  7.03 us
    ppermute x7, waiting for transfers between devices, shift_z(): lax.ppermute(value, AX, [(ident(x, y, z, c), ident(x, y, z + step, c)) fo...  6.59 us
  transfers between devices with their start and end apart: 29, of which 16 were waited for; matrix products, arithmetic and copies ran while one was open for 26% of the time, Pallas kernels for 0%

profile of v1, /device:TPU:0, one launch (start us, length us, event | category | flops | bytes accessed | tf_op | source)
XLA Modules:
  0.0 170.2 jit_solution(16502726209066530936)
XLA Ops:
  8.8 4.2 %collective-permute-start.7 = (bf16[8,8192]{1,0:T(8,128)(2,1)S(1)}, bf16[8,8192]{1,0:T(8,128)(2,1)S(1)}, u32[]{:S(2)}, u32[]{:S(2)}) collective-permute-start(bf16[8,8192]{1,0:T(8,128)(2,1)S(1)} %get-tuple-element.9), channel_id=1, source_target_pairs={{0,14},{1,15},{2,0},{3,1},{4,2},{5,3},{6,4},{7,5},{8,6},{9,7},{10,... | collective-permute-start | bytes 393224 | tf_op jit(solution)/shard_map/ppermute | solution.py:22
  15.8 7.0 %all-to-all-start = ((bf16[16,8,2048]{2,1,0:T(8,128)(2,1)}), bf16[16,8,2048]{2,1,0:T(8,128)(2,1)S(1)}, u32[]{:S(2)}, u32[]{:S(2)}) async-start(bf16[16,8,2048]{2,1,0:T(8,128)(2,1)} %bitcast.7), calls=%async_computation | async-start | bytes 1048576 | tf_op jit(solution)/shard_map/all_to_all | solution.py:75
  23.1 3.3 %collective-permute-start.8 = (bf16[8,8192]{1,0:T(8,128)(2,1)S(1)}, bf16[8,8192]{1,0:T(8,128)(2,1)S(1)}, u32[]{:S(2)}, u32[]{:S(2)}) collective-permute-start(bf16[8,8192]{1,0:T(8,128)(2,1)S(1)} %collective-permute-done.7), channel_id=1, source_target_pairs={{0,14},{1,15},{2,0},{3,1},{4,2},{5,3},{6,4},{7,5},{8,6},{9,7},{10,... | collective-permute-start | bytes 393224 | tf_op jit(solution)/shard_map/ppermute | solution.py:22
  28.9 3.7 %collective-permute-start.9 = (bf16[8,8192]{1,0:T(8,128)(2,1)S(1)}, bf16[8,8192]{1,0:T(8,128)(2,1)S(1)}, u32[]{:S(2)}, u32[]{:S(2)}) collective-permute-start(bf16[8,8192]{1,0:T(8,128)(2,1)S(1)} %collective-permute-done.8), channel_id=1, source_target_pairs={{0,14},{1,15},{2,0},{3,1},{4,2},{5,3},{6,4},{7,5},{8,6},{9,7},{10,... | collective-permute-start | bytes 393224 | tf_op jit(solution)/shard_map/ppermute | solution.py:22
  35.1 3.7 %collective-permute-start.10 = (bf16[8,8192]{1,0:T(8,128)(2,1)S(1)}, bf16[8,8192]{1,0:T(8,128)(2,1)}, u32[]{:S(2)}, u32[]{:S(2)}) collective-permute-start(bf16[8,8192]{1,0:T(8,128)(2,1)S(1)} %collective-permute-done.9), channel_id=1, source_target_pairs={{0,14},{1,15},{2,0},{3,1},{4,2},{5,3},{6,4},{7,5},{8,6},{9,7},{10,... | collective-permute-start | bytes 393224 | tf_op jit(solution)/shard_map/ppermute | solution.py:22
  44.5 3.1 %collective-permute-start.14 = (bf16[64,2048]{1,0:T(8,128)(2,1)S(1)}, bf16[64,2048]{1,0:T(8,128)(2,1)S(1)}, u32[]{:S(2)}, u32[]{:S(2)}) collective-permute-start(bf16[64,2048]{1,0:T(8,128)(2,1)S(1)} %get-tuple-element.13), channel_id=1, source_target_pairs={{0,192},{1,49},{2,194},{3,51},{4,196},{5,53},{6,198},{7,55},{8,200... | collective-permute-start | bytes 786440 | tf_op jit(solution)/shard_map/ppermute | solution.py:32
  49.4 5.0 %collective-permute-done.14 = bf16[64,2048]{1,0:T(8,128)(2,1)S(1)} collective-permute-done((bf16[64,2048]{1,0:T(8,128)(2,1)S(1)}, bf16[64,2048]{1,0:T(8,128)(2,1)S(1)}, u32[]{:S(2)}, u32[]{:S(2)}) %collective-permute-start.14) | collective-permute-done | bytes 262176 | tf_op jit(solution)/shard_map/ppermute | solution.py:32
  62.1 2.5 %constant_dynamic-update-slice_fusion.31 = (bf16[2048,2048]{1,0:T(8,128)(2,1)}, bf16[256,2048]{1,0:T(8,128)(2,1)S(1)}) fusion(bf16[512,2048]{1,0:T(8,128)(2,1)} %constant_dynamic-update-slice_fusion.16, s32[]{:T(128)S(6)} %select_n.297), kind=kLoop, calls=%fused_computation.69 | loop fusion | bytes 3145732
  64.5 2.7 %collective-permute-start.17 = (bf16[256,2048]{1,0:T(8,128)(2,1)S(1)}, bf16[256,2048]{1,0:T(8,128)(2,1)S(1)}, u32[]{:S(2)}, u32[]{:S(2)}) collective-permute-start(bf16[256,2048]{1,0:T(8,128)(2,1)S(1)} %get-tuple-element.7), channel_id=1, source_target_pairs={{0,48},{1,193},{2,50},{3,195},{4,52},{5,197},{6,54},{7,199},{8,56}... | collective-permute-start | bytes 3145736 | tf_op jit(solution)/shard_map/ppermute | solution.py:32
  67.4 2.8 %dynamic-slice_multiply_fusion.2 = (bf16[128,2048]{1,0:T(8,128)(2,1)}, bf16[128,2048]{1,0:T(8,128)(2,1)}, bf16[128,2048]{1,0:T(8,128)(2,1)}) fusion(bf16[128,8192]{1,0:T(8,128)(2,1)} %param.4, s32[]{:T(128)S(6)} %select_n.268, bf16[2048]{0:T(1024)(128)(2,1)S(1)} %get-tuple-element.2, bf16[2048]{0:T(1024)(128)(2,1)S(1)} %get-tuple-element.4, ...), kind=kLoop, calls=%fused_computation.29 | loop fusion | flops 3145728 | bytes 3158028 | tf_op jit(solution)/shard_map/mul | solution.py:66
  74.3 15.9 %collective-permute-done.17 = bf16[256,2048]{1,0:T(8,128)(2,1)S(1)} collective-permute-done((bf16[256,2048]{1,0:T(8,128)(2,1)S(1)}, bf16[256,2048]{1,0:T(8,128)(2,1)S(1)}, u32[]{:S(2)}, u32[]{:S(2)}) %collective-permute-start.17) | collective-permute-done | bytes 1048608 | tf_op jit(solution)/shard_map/ppermute | solution.py:32
  91.0 3.3 %collective-permute-start.18 = (bf16[128,2048]{1,0:T(8,128)(2,1)}, bf16[128,2048]{1,0:T(8,128)(2,1)}, u32[]{:S(2)}, u32[]{:S(2)}) collective-permute-start(bf16[128,2048]{1,0:T(8,128)(2,1)} %slice.12), channel_id=1, source_target_pairs={{0,48},{1,193},{2,50},{3,195},{4,52},{5,197},{6,54},{7,199},{8,56}... | collective-permute-start | bytes 1572872 | tf_op jit(solution)/shard_map/ppermute | solution.py:32
  96.3 5.0 %collective-permute-done.18 = bf16[128,2048]{1,0:T(8,128)(2,1)} collective-permute-done((bf16[128,2048]{1,0:T(8,128)(2,1)}, bf16[128,2048]{1,0:T(8,128)(2,1)}, u32[]{:S(2)}, u32[]{:S(2)}) %collective-permute-start.18) | collective-permute-done | bytes 524320 | tf_op jit(solution)/shard_map/ppermute | solution.py:32
  103.2 2.7 %collective-permute-done.20 = bf16[128,2048]{1,0:T(8,128)(2,1)} collective-permute-done((bf16[128,2048]{1,0:T(8,128)(2,1)}, bf16[128,2048]{1,0:T(8,128)(2,1)}, u32[]{:S(2)}, u32[]{:S(2)}) %collective-permute-start.20) | collective-permute-done | bytes 524320 | tf_op jit(solution)/shard_map/ppermute | solution.py:32
  110.0 4.0 %convolution_convert_fusion.2 = bf16[128,1024]{1,0:T(8,128)(2,1)S(1)} fusion(bf16[128,2048]{1,0:T(8,128)(2,1)} %collective-permute-done, bf16[1024,2048]{1,0:T(8,128)(2,1)} %all-gather.2.cloned.1.call-done), kind=kOutput, calls=%fused_computation.21 | convolution fusion | flops 537001984 | bytes 4980736 | tf_op jit(solution)/shard_map/dot_general | solution.py:93
  115.5 2.7 %convolution_convert_fusion.1 = bf16[128,1024]{1,0:T(8,128)(2,1)S(1)} fusion(bf16[128,2048]{1,0:T(8,128)(2,1)} %collective-permute-done.2, bf16[1024,2048]{1,0:T(8,128)(2,1)S(1)} %copy-done), kind=kOutput, calls=%fused_computation.20 | convolution fusion | flops 537001984 | bytes 4980736 | tf_op jit(solution)/shard_map/dot_general | solution.py:93
  119.5 2.6 %convolution_convert_fusion = bf16[128,1024]{1,0:T(8,128)(2,1)S(1)} fusion(bf16[128,2048]{1,0:T(8,128)(2,1)} %collective-permute-done.4, bf16[1024,2048]{1,0:T(8,128)(2,1)S(1)} %copy-done), kind=kOutput, calls=%fused_computation.19 | convolution fusion | flops 537001984 | bytes 4980736 | tf_op jit(solution)/shard_map/dot_general | solution.py:93
  123.3 2.6 %fusion.33 = f32[128,1024]{1,0:T(8,128)S(1)} fusion(bf16[1024,2048]{1,0:T(8,128)(2,1)S(1)} %copy-done, bf16[128,8192]{1,0:T(8,128)(2,1)} %param.4, s32[]{:T(128)S(6)} %select_n.261, bf16[2048]{0:T(1024)(128)(2,1)S(1)} %get-tuple-element.5), kind=kOutput, calls=%fused_computation.30 | convolution fusion | flops 537919488 | bytes 5246980 | tf_op jit(solution)/shard_map/dot_general | solution.py:93
  125.9 3.9 %collective-permute-done.5 = bf16[128,1024]{1,0:T(8,128)(2,1)S(1)} collective-permute-done((bf16[128,1024]{1,0:T(8,128)(2,1)S(1)}, bf16[128,1024]{1,0:T(8,128)(2,1)S(1)}, u32[]{:S(2)}, u32[]{:S(2)}) %collective-permute-start.5) | collective-permute-done | bytes 262176 | tf_op jit(solution)/shard_map/ppermute | solution.py:32
  133.5 3.5 %collective-permute-start.25 = (bf16[128,1024]{1,0:T(8,128)(2,1)S(1)}, bf16[128,1024]{1,0:T(8,128)(2,1)S(1)}, u32[]{:S(2)}, u32[]{:S(2)}) collective-permute-start(bf16[128,1024]{1,0:T(8,128)(2,1)S(1)} %fusion.27), channel_id=1, source_target_pairs={{0,192},{1,49},{2,194},{3,51},{4,196},{5,53},{6,198},{7,55},{8,200... | collective-permute-start | bytes 786440 | tf_op jit(solution)/shard_map/ppermute | solution.py:32
  138.0 3.0 %collective-permute-done.21 = bf16[128,1024]{1,0:T(8,128)(2,1)S(1)} collective-permute-done((bf16[128,1024]{1,0:T(8,128)(2,1)S(1)}, bf16[128,1024]{1,0:T(8,128)(2,1)S(1)}, u32[]{:S(2)}, u32[]{:S(2)}) %collective-permute-start.21) | collective-permute-done | bytes 262176 | tf_op jit(solution)/shard_map/ppermute | solution.py:32
  141.8 3.1 %collective-permute-done.23 = bf16[128,1024]{1,0:T(8,128)(2,1)S(1)} collective-permute-done((bf16[128,1024]{1,0:T(8,128)(2,1)S(1)}, bf16[128,1024]{1,0:T(8,128)(2,1)S(1)}, u32[]{:S(2)}, u32[]{:S(2)}) %collective-permute-start.23) | collective-permute-done | bytes 262176 | tf_op jit(solution)/shard_map/ppermute | solution.py:32
  151.0 5.5 %collective-permute-done.24 = bf16[128,2048]{1,0:T(8,128)(2,1)S(1)} collective-permute-done((bf16[128,2048]{1,0:T(8,128)(2,1)S(1)}, bf16[128,2048]{1,0:T(8,128)(2,1)S(1)}, u32[]{:S(2)}, u32[]{:S(2)}) %collective-permute-start.24) | collective-permute-done | bytes 524320 | tf_op jit(solution)/shard_map/ppermute | solution.py:32
  156.6 5.4 %collective-permute-done.26 = bf16[128,2048]{1,0:T(8,128)(2,1)S(1)} collective-permute-done((bf16[128,2048]{1,0:T(8,128)(2,1)S(1)}, bf16[128,2048]{1,0:T(8,128)(2,1)S(1)}, u32[]{:S(2)}, u32[]{:S(2)}) %collective-permute-start.26) | collective-permute-done | bytes 524320 | tf_op jit(solution)/shard_map/ppermute | solution.py:32
  (110 shorter events, 54.7 us)
Async XLA Ops:
  8.8 14.2 %collective-permute-start.7 = (bf16[8,8192]{1,0:T(8,128)(2,1)S(1)}, bf16[8,8192]{1,0:T(8,128)(2,1)S(1)}, u32[]{:S(2)}, u32[]{:S(2)}) collective-permute-start(bf16[8,8192]{1,0:T(8,128)(2,1)S(1)} %get-tuple-element.9), channel_id=1, source_target_pairs={{0,14},{1,15},{2,0},{3,1},{4,2},{5,3},{6,4},{7,5},{8,6},{9,7},{10,... | collective-permute-start | bytes 393224 | tf_op jit(solution)/shard_map/ppermute | solution.py:22
  13.0 13.4 %collective-permute-start.11 = (bf16[8,8192]{1,0:T(8,128)(2,1)S(1)}, bf16[8,8192]{1,0:T(8,128)(2,1)S(1)}, u32[]{:S(2)}, u32[]{:S(2)}) collective-permute-start(bf16[8,8192]{1,0:T(8,128)(2,1)S(1)} %get-tuple-element.9), channel_id=1, source_target_pairs={{0,2},{1,3},{2,4},{3,5},{4,6},{5,7},{6,8},{7,9},{8,10},{9,11},{10,... | collective-permute-start | bytes 393224 | tf_op jit(solution)/shard_map/ppermute | solution.py:22
  15.8 22.9 %all-to-all-start = ((bf16[16,8,2048]{2,1,0:T(8,128)(2,1)}), bf16[16,8,2048]{2,1,0:T(8,128)(2,1)S(1)}, u32[]{:S(2)}, u32[]{:S(2)}) async-start(bf16[16,8,2048]{2,1,0:T(8,128)(2,1)} %bitcast.7), calls=%async_computation | async-start | bytes 1048576 | tf_op jit(solution)/shard_map/all_to_all | solution.py:75
  22.9 87.1 %all-gather.2.cloned.1.call-start = ((), (), s32[]{:S(2)}) async-start(), calls=%async_computation.1 | async-start | bytes 4718592 | tf_op jit(solution)/shard_map/all_gather | solution.py:77
  32.7 9.5 %collective-permute-start.13 = (bf16[8,8192]{1,0:T(8,128)(2,1)S(1)}, bf16[8,8192]{1,0:T(8,128)(2,1)S(1)}, u32[]{:S(2)}, u32[]{:S(2)}) collective-permute-start(bf16[8,8192]{1,0:T(8,128)(2,1)S(1)} %collective-permute-done.12), channel_id=1, source_target_pairs={{0,2},{1,3},{2,4},{3,5},{4,6},{5,7},{6,8},{7,9},{8,10},{9,11},{10,... | collective-permute-start | bytes 393224 | tf_op jit(solution)/shard_map/ppermute | solution.py:22
  44.5 9.8 %collective-permute-start.14 = (bf16[64,2048]{1,0:T(8,128)(2,1)S(1)}, bf16[64,2048]{1,0:T(8,128)(2,1)S(1)}, u32[]{:S(2)}, u32[]{:S(2)}) collective-permute-start(bf16[64,2048]{1,0:T(8,128)(2,1)S(1)} %get-tuple-element.13), channel_id=1, source_target_pairs={{0,192},{1,49},{2,194},{3,51},{4,196},{5,53},{6,198},{7,55},{8,200... | collective-permute-start | bytes 786440 | tf_op jit(solution)/shard_map/ppermute | solution.py:32
  47.6 8.0 %collective-permute-start.15 = (bf16[64,2048]{1,0:T(8,128)(2,1)S(1)}, bf16[64,2048]{1,0:T(8,128)(2,1)S(1)}, u32[]{:S(2)}, u32[]{:S(2)}) collective-permute-start(bf16[64,2048]{1,0:T(8,128)(2,1)S(1)} %get-tuple-element.12), channel_id=1, source_target_pairs={{0,128},{1,33},{2,130},{3,35},{4,132},{5,37},{6,134},{7,39},{8,136... | collective-permute-start | bytes 786440 | tf_op jit(solution)/shard_map/ppermute | solution.py:32
  48.5 9.8 %collective-permute-start.16 = (bf16[64,2048]{1,0:T(8,128)(2,1)S(1)}, bf16[64,2048]{1,0:T(8,128)(2,1)S(1)}, u32[]{:S(2)}, u32[]{:S(2)}) collective-permute-start(bf16[64,2048]{1,0:T(8,128)(2,1)S(1)} %get-tuple-element.10), channel_id=1, source_target_pairs={{0,64},{1,17},{2,66},{3,19},{4,68},{5,21},{6,70},{7,23},{8,72},{9,... | collective-permute-start | bytes 786440 | tf_op jit(solution)/shard_map/ppermute | solution.py:32
  64.5 25.6 %collective-permute-start.17 = (bf16[256,2048]{1,0:T(8,128)(2,1)S(1)}, bf16[256,2048]{1,0:T(8,128)(2,1)S(1)}, u32[]{:S(2)}, u32[]{:S(2)}) collective-permute-start(bf16[256,2048]{1,0:T(8,128)(2,1)S(1)} %get-tuple-element.7), channel_id=1, source_target_pairs={{0,48},{1,193},{2,50},{3,195},{4,52},{5,197},{6,54},{7,199},{8,56}... | collective-permute-start | bytes 3145736 | tf_op jit(solution)/shard_map/ppermute | solution.py:32
  67.2 27.1 %collective-permute-start.19 = (bf16[256,2048]{1,0:T(8,128)(2,1)S(1)}, bf16[256,2048]{1,0:T(8,128)(2,1)S(1)}, u32[]{:S(2)}, u32[]{:S(2)}) collective-permute-start(bf16[256,2048]{1,0:T(8,128)(2,1)S(1)} %get-tuple-element.7), channel_id=1, source_target_pairs={{0,16},{1,65},{2,18},{3,67},{4,20},{5,69},{6,22},{7,71},{8,24},{9,... | collective-permute-start | bytes 3145736 | tf_op jit(solution)/shard_map/ppermute | solution.py:32
  70.1 39.8 %collective-permute-start = (bf16[128,2048]{1,0:T(8,128)(2,1)}, bf16[128,2048]{1,0:T(8,128)(2,1)}, u32[]{:S(2)}, u32[]{:S(2)}) collective-permute-start(bf16[128,2048]{1,0:T(8,128)(2,1)} %get-tuple-element.14), channel_id=1, source_target_pairs={{0,128},{1,33},{2,130},{3,35},{4,132},{5,37},{6,134},{7,39},{8,136... | collective-permute-start | bytes 1572872 | tf_op jit(solution)/shard_map/ppermute | solution.py:32
  71.0 44.5 %collective-permute-start.2 = (bf16[128,2048]{1,0:T(8,128)(2,1)}, bf16[128,2048]{1,0:T(8,128)(2,1)}, u32[]{:S(2)}, u32[]{:S(2)}) collective-permute-start(bf16[128,2048]{1,0:T(8,128)(2,1)} %get-tuple-element.15), channel_id=1, source_target_pairs={{0,64},{1,17},{2,66},{3,19},{4,68},{5,21},{6,70},{7,23},{8,72},{9,... | collective-permute-start | bytes 1572872 | tf_op jit(solution)/shard_map/ppermute | solution.py:32
  72.1 47.4 %collective-permute-start.4 = (bf16[128,2048]{1,0:T(8,128)(2,1)}, bf16[128,2048]{1,0:T(8,128)(2,1)}, u32[]{:S(2)}, u32[]{:S(2)}) collective-permute-start(bf16[128,2048]{1,0:T(8,128)(2,1)} %get-tuple-element.16), channel_id=1, source_target_pairs={{0,192},{1,49},{2,194},{3,51},{4,196},{5,53},{6,198},{7,55},{8,200... | collective-permute-start | bytes 1572872 | tf_op jit(solution)/shard_map/ppermute | solution.py:32
  91.0 10.3 %collective-permute-start.18 = (bf16[128,2048]{1,0:T(8,128)(2,1)}, bf16[128,2048]{1,0:T(8,128)(2,1)}, u32[]{:S(2)}, u32[]{:S(2)}) collective-permute-start(bf16[128,2048]{1,0:T(8,128)(2,1)} %slice.12), channel_id=1, source_target_pairs={{0,48},{1,193},{2,50},{3,195},{4,52},{5,197},{6,54},{7,199},{8,56}... | collective-permute-start | bytes 1572872 | tf_op jit(solution)/shard_map/ppermute | solution.py:32
  95.2 10.7 %collective-permute-start.20 = (bf16[128,2048]{1,0:T(8,128)(2,1)}, bf16[128,2048]{1,0:T(8,128)(2,1)}, u32[]{:S(2)}, u32[]{:S(2)}) collective-permute-start(bf16[128,2048]{1,0:T(8,128)(2,1)} %slice.13), channel_id=1, source_target_pairs={{0,16},{1,65},{2,18},{3,67},{4,20},{5,69},{6,22},{7,71},{8,24},{9,... | collective-permute-start | bytes 1572872 | tf_op jit(solution)/shard_map/ppermute | solution.py:32
  114.0 11.9 %collective-permute-start.1 = (bf16[128,1024]{1,0:T(8,128)(2,1)S(1)}, bf16[128,1024]{1,0:T(8,128)(2,1)S(1)}, u32[]{:S(2)}, u32[]{:S(2)}) collective-permute-start(bf16[128,1024]{1,0:T(8,128)(2,1)S(1)} %convolution_convert_fusion.2), channel_id=1, source_target_pairs={{0,128},{1,33},{2,130},{3,35},{4,132},{5,37},{6,134},{7,39},{8,136... | collective-permute-start | bytes 786440 | tf_op jit(solution)/shard_map/ppermute | solution.py:32
  118.2 7.6 %collective-permute-start.3 = (bf16[128,1024]{1,0:T(8,128)(2,1)S(1)}, bf16[128,1024]{1,0:T(8,128)(2,1)S(1)}, u32[]{:S(2)}, u32[]{:S(2)}) collective-permute-start(bf16[128,1024]{1,0:T(8,128)(2,1)S(1)} %convolution_convert_fusion.1), channel_id=1, source_target_pairs={{0,192},{1,49},{2,194},{3,51},{4,196},{5,53},{6,198},{7,55},{8,200... | collective-permute-start | bytes 786440 | tf_op jit(solution)/shard_map/ppermute | solution.py:32
  122.1 7.7 %collective-permute-start.5 = (bf16[128,1024]{1,0:T(8,128)(2,1)S(1)}, bf16[128,1024]{1,0:T(8,128)(2,1)S(1)}, u32[]{:S(2)}, u32[]{:S(2)}) collective-permute-start(bf16[128,1024]{1,0:T(8,128)(2,1)S(1)} %convolution_convert_fusion), channel_id=1, source_target_pairs={{0,64},{1,17},{2,66},{3,19},{4,68},{5,21},{6,70},{7,23},{8,72},{9,... | collective-permute-start | bytes 786440 | tf_op jit(solution)/shard_map/ppermute | solution.py:32
  133.3 7.7 %collective-permute-start.21 = (bf16[128,1024]{1,0:T(8,128)(2,1)S(1)}, bf16[128,1024]{1,0:T(8,128)(2,1)S(1)}, u32[]{:S(2)}, u32[]{:S(2)}) collective-permute-start(bf16[128,1024]{1,0:T(8,128)(2,1)S(1)} %fusion.27), channel_id=1, source_target_pairs={{0,64},{1,17},{2,66},{3,19},{4,68},{5,21},{6,70},{7,23},{8,72},{9,... | collective-permute-start | bytes 786440 | tf_op jit(solution)/shard_map/ppermute | solution.py:32
  133.5 12.3 %collective-permute-start.25 = (bf16[128,1024]{1,0:T(8,128)(2,1)S(1)}, bf16[128,1024]{1,0:T(8,128)(2,1)S(1)}, u32[]{:S(2)}, u32[]{:S(2)}) collective-permute-start(bf16[128,1024]{1,0:T(8,128)(2,1)S(1)} %fusion.27), channel_id=1, source_target_pairs={{0,192},{1,49},{2,194},{3,51},{4,196},{5,53},{6,198},{7,55},{8,200... | collective-permute-start | bytes 786440 | tf_op jit(solution)/shard_map/ppermute | solution.py:32
  137.0 7.9 %collective-permute-start.23 = (bf16[128,1024]{1,0:T(8,128)(2,1)S(1)}, bf16[128,1024]{1,0:T(8,128)(2,1)S(1)}, u32[]{:S(2)}, u32[]{:S(2)}) collective-permute-start(bf16[128,1024]{1,0:T(8,128)(2,1)S(1)} %fusion.27), channel_id=1, source_target_pairs={{0,128},{1,33},{2,130},{3,35},{4,132},{5,37},{6,134},{7,39},{8,136... | collective-permute-start | bytes 786440 | tf_op jit(solution)/shard_map/ppermute | solution.py:32
  141.7 9.3 %collective-permute-start.22 = (bf16[128,2048]{1,0:T(8,128)(2,1)S(1)}, bf16[128,2048]{1,0:T(8,128)(2,1)S(1)}, u32[]{:S(2)}, u32[]{:S(2)}) collective-permute-start(bf16[128,2048]{1,0:T(8,128)(2,1)S(1)} %fusion.15), channel_id=1, source_target_pairs={{0,192},{1,49},{2,194},{3,51},{4,196},{5,53},{6,198},{7,55},{8,200... | collective-permute-start | bytes 1572872 | tf_op jit(solution)/shard_map/ppermute | solution.py:32
  145.6 10.9 %collective-permute-start.24 = (bf16[128,2048]{1,0:T(8,128)(2,1)S(1)}, bf16[128,2048]{1,0:T(8,128)(2,1)S(1)}, u32[]{:S(2)}, u32[]{:S(2)}) collective-permute-start(bf16[128,2048]{1,0:T(8,128)(2,1)S(1)} %fusion.18), channel_id=1, source_target_pairs={{0,128},{1,33},{2,130},{3,35},{4,132},{5,37},{6,134},{7,39},{8,136... | collective-permute-start | bytes 1572872 | tf_op jit(solution)/shard_map/ppermute | solution.py:32
  146.5 15.5 %collective-permute-start.26 = (bf16[128,2048]{1,0:T(8,128)(2,1)S(1)}, bf16[128,2048]{1,0:T(8,128)(2,1)S(1)}, u32[]{:S(2)}, u32[]{:S(2)}) collective-permute-start(bf16[128,2048]{1,0:T(8,128)(2,1)S(1)} %fusion.21), channel_id=1, source_target_pairs={{0,64},{1,17},{2,66},{3,19},{4,68},{5,21},{6,70},{7,23},{8,72},{9,... | collective-permute-start | bytes 1572872 | tf_op jit(solution)/shard_map/ppermute | solution.py:32
  (10 other events, 60.7 us)
Sparse Core Ops, SparseCore 0:
  39.7 52.2 all-gather.1

commit v2 on v1

v2 whole, which is shorter than its diff:
```python
import functools

import jax
import jax.numpy as jnp
from jax import lax
from jax.experimental import pallas as pl
from jax.experimental.pallas import tpu as pltpu
from jax.sharding import PartitionSpec as P

TB = 128
WD = 8
NX, NY, NZ = 4, 4, 8
AX = ("row", "col", "rep")
F32, BF = jnp.float32, jnp.bfloat16
ROWS = 128
HALF = 8192
PART = HALF // 4
QW = 1024
VMEM = pl.BlockSpec(memory_space=pltpu.VMEM)
PARAMS = pltpu.CompilerParams(vmem_limit_bytes=40 * 2**20)


def ident(x, y, z, c):
    return ((x % NX) * NY * NZ + (y % NY) * NZ + z % NZ) * 2 + c


def every():
    return [(x, y, z, c) for x in range(NX) for y in range(NY) for z in range(NZ) for c in (0, 1)]


def shift_z(value, step):
    return lax.ppermute(value, AX, [(ident(x, y, z, c), ident(x, y, z + step, c)) for x, y, z, c in every()])


def shift_plane(value, step, swapped):
    pairs = []
    for x, y, z, c in every():
        if (c == 0) != swapped:
            pairs.append((ident(x, y, z, c), ident(x + step, y, z, c)))
        else:
            pairs.append((ident(x, y, z, c), ident(x, y + step, z, c)))
    return lax.ppermute(value, AX, pairs)


def shift_g(value, step):
    return shift_plane(value, step, False)


def shift_p(value, step):
    return shift_plane(value, step, True)


def swap_core(value):
    return lax.ppermute(value, AX, [(ident(x, y, z, c), ident(x, y, z, 1 - c)) for x, y, z, c in every()])


def cost(flops, moved):
    return pl.CostEstimate(flops=flops, bytes_accessed=moved, transcendentals=0)


def cycle_kernel(place, cyc_map, cyc, out):
    core, column = place[2], place[3]
    tiles = HALF // TB
    shares = []
    for share in range(4):
        cut = []
        for t in range(share * 16, share * 16 + 16):
            keep = cyc_map[core * tiles + t, column].astype(F32)
            cut.append((cyc[:, t * TB : (t + 1) * TB].astype(F32) * keep))
        shares.append(jnp.concatenate(cut, 1))
    first = core == 0
    for i in range(4):
        for j in range(0, 4, 2):
            top = jnp.where(first, shares[i], shares[j])
            low = jnp.where(first, shares[i], shares[j + 1])
            at = (i * 4 + j) * WD
            out[at : at + 2 * WD, :] = jnp.concatenate([top, low], 0).astype(BF)


def cycle_shares(place, cycle_map, cyc):
    return pl.pallas_call(
        cycle_kernel,
        out_shape=jax.ShapeDtypeStruct((16 * WD, PART), BF),
        grid_spec=pltpu.PrefetchScalarGridSpec(
            num_scalar_prefetch=2, grid=(), in_specs=[VMEM], out_specs=VMEM
        ),
        compiler_params=PARAMS,
        cost_estimate=cost(0, 700_000),
    )(place, cycle_map, cyc)


def amp_kernel(place, amp_map, *refs):
    ins, outs, win = refs[:4], refs[4:8], refs[8]
    step = pl.program_id(0)
    for d in range(4):
        share = lax.rem(place[0] + d, 4)
        for t in range(PART // TB):
            keep = amp_map[0, share * 16 + t].astype(BF)
            outs[d][:, t * TB : (t + 1) * TB] = ins[d][:, t * TB : (t + 1) * TB] * keep

        @pl.when(step == 0)
        def _():
            win[:, pl.ds(pl.multiple_of(share * PART, PART), PART)] = outs[d][:16, :]


def amp_shares(place, amp_map, amplitudes):
    block = 32

    def source(d):
        return pl.BlockSpec((block, PART), lambda i, place, amp_map: (i, lax.rem(place[0] + d, 4)))

    return pl.pallas_call(
        amp_kernel,
        out_shape=[jax.ShapeDtypeStruct((ROWS, PART), BF)] * 4 + [jax.ShapeDtypeStruct((16, HALF), BF)],
        grid_spec=pltpu.PrefetchScalarGridSpec(
            num_scalar_prefetch=2,
            grid=(ROWS // block,),
            in_specs=[source(d) for d in range(4)],
            out_specs=[pl.BlockSpec((block, PART), lambda i, place, amp_map: (i, 0))] * 4
            + [pl.BlockSpec((16, HALF), lambda i, place, amp_map: (0, 0))],
        ),
        compiler_params=PARAMS,
        cost_estimate=cost(0, 4_000_000),
    )(place, amp_map, *[amplitudes] * 4)


def dressed_kernel(first, count, *refs):
    blocks, cyc = refs[:4], refs[4 : 4 + count]
    away, own = refs[-2:]
    left = jnp.concatenate([blocks[d][...] for d in (1, 2, 3, 0)], 0)
    for at in range(0, count, 2):
        right = jnp.concatenate([ref[...] for ref in cyc[at : at + 2]], 0)
        wide = right.shape[0]
        value = lax.dot_general(left, right, (((1,), (1,)), ((), ())), preferred_element_type=F32)
        where = slice(first + at * 128, first + at * 128 + wide)
        away[:, where] = value[: 3 * ROWS].astype(BF)
        own[:, where] = value[3 * ROWS :]


def dressed_first(blocks, cyc):
    return pl.pallas_call(
        functools.partial(dressed_kernel, 0, len(cyc)),
        out_shape=[jax.ShapeDtypeStruct((3 * ROWS, QW), BF), jax.ShapeDtypeStruct((ROWS, QW), F32)],
        in_specs=[VMEM] * (4 + len(cyc)),
        out_specs=[VMEM] * 2,
        compiler_params=PARAMS,
        cost_estimate=cost(2 * 512 * PART * 896, 8_000_000),
    )(*blocks, *cyc)


def dressed_last_kernel(*refs):
    blocks, halves, away_in, own_in = refs[:4], refs[4:6], refs[6], refs[7]
    outs, own = refs[8:11], refs[11]
    edge = 7 * 128
    left = jnp.concatenate([blocks[d][...] for d in (1, 2, 3, 0)], 0)
    right = jnp.concatenate([ref[...] for ref in halves], 0)
    value = lax.dot_general(left, right, (((1,), (1,)), ((), ())), preferred_element_type=F32)
    for d in range(3):
        rows = slice(d * ROWS, (d + 1) * ROWS)
        outs[d][:, :edge] = away_in[rows, :edge]
        outs[d][:, edge:] = value[rows].astype(BF)
    own[:, :edge] = own_in[:, :edge]
    own[:, edge:] = value[3 * ROWS :]


def dressed_last(blocks, halves, away, own):
    return pl.pallas_call(
        dressed_last_kernel,
        out_shape=[jax.ShapeDtypeStruct((ROWS, QW), BF)] * 3 + [jax.ShapeDtypeStruct((ROWS, QW), F32)],
        in_specs=[VMEM] * 8,
        out_specs=[VMEM] * 4,
        compiler_params=PARAMS,
        cost_estimate=cost(2 * 512 * PART * 128, 5_000_000),
    )(*blocks, *halves, away, own)


def window_cut_kernel(place, *refs):
    pieces, outs = refs[:8], refs[8:]
    for d in range(4):
        share = pl.ds(pl.multiple_of(lax.rem(place[0] + 4 - d, 4) * PART, PART), PART)
        for m in range(0, 8, 2):
            pair = jnp.concatenate([pieces[m][:, share], pieces[m + 1][:, share]], 0)
            outs[d][m * WD : (m + 2) * WD, :] = pair


def window_cut(place, pieces):
    return pl.pallas_call(
        window_cut_kernel,
        out_shape=[jax.ShapeDtypeStruct((NZ * WD, PART), BF)] * 4,
        grid_spec=pltpu.PrefetchScalarGridSpec(
            num_scalar_prefetch=1, grid=(), in_specs=[VMEM] * 8, out_specs=[VMEM] * 4
        ),
        compiler_params=PARAMS,
        cost_estimate=cost(0, 2_000_000),
    )(place, *pieces)


def window_order_kernel(place, *refs):
    pieces, out = refs[:4], refs[4]
    for d in range(4):
        at = pl.multiple_of(lax.rem(place[0] + d, 4) * NZ * WD, NZ * WD)
        out[pl.ds(at, NZ * WD), :] = pieces[d][...]


def window_order(place, pieces):
    return pl.pallas_call(
        window_order_kernel,
        out_shape=jax.ShapeDtypeStruct((4 * NZ * WD, PART), BF),
        grid_spec=pltpu.PrefetchScalarGridSpec(
            num_scalar_prefetch=1, grid=(), in_specs=[VMEM] * 4, out_specs=VMEM
        ),
        compiler_params=PARAMS,
        cost_estimate=cost(0, 2_000_000),
    )(place, *pieces)


def inner_kernel(mine, other, order, full, inner):
    value = (mine[...] + other[...]).astype(BF)
    full[...] = value
    inner[...] = jnp.dot(value, order[...], preferred_element_type=F32).astype(BF)


def inner_call(mine, other, order):
    return pl.pallas_call(
        inner_kernel,
        out_shape=[jax.ShapeDtypeStruct((ROWS, QW), BF)] * 2,
        in_specs=[VMEM] * 3,
        out_specs=[VMEM] * 2,
        compiler_params=PARAMS,
        cost_estimate=cost(2 * ROWS * QW * QW, 4_000_000),
    )(mine, other, order)


def quadratic_kernel(count, *refs):
    lefts, rights, outs = refs[:count], refs[count : count + 5], refs[count + 5 :]
    left = jnp.concatenate([ref[...] for ref in lefts], 0)
    wide = 512
    for n in range(0, PART, wide):
        right = jnp.concatenate([ref[:, n : n + wide] for ref in rights], 0)
        value = jnp.dot(left, right, preferred_element_type=F32).astype(BF)
        for d in range(count):
            outs[d][:, n : n + wide] = value[d * ROWS : (d + 1) * ROWS]


def quadratic_blocks(lefts, rights):
    count = len(lefts)
    return pl.pallas_call(
        functools.partial(quadratic_kernel, count),
        out_shape=[jax.ShapeDtypeStruct((ROWS, PART), BF)] * count,
        in_specs=[VMEM] * (count + 5),
        out_specs=[VMEM] * count,
        compiler_params=PARAMS,
        cost_estimate=cost(2 * count * ROWS * QW * PART, 5_000_000),
    )(*lefts, *rights)


def place_kernel(place, *refs):
    ins, out, sem = refs[:4], refs[4], refs[5]
    copies = []
    for d in range(4):
        at = pl.multiple_of(lax.rem(place[0] + d, 4) * PART, PART)
        copies.append(pltpu.make_async_copy(ins[d], out.at[:, pl.ds(at, PART)], sem.at[d]))
    for copy in copies:
        copy.start()
    for copy in copies:
        copy.wait()


def place_blocks(place, blocks):
    anywhere = pl.BlockSpec(memory_space=pl.ANY)
    return pl.pallas_call(
        place_kernel,
        out_shape=jax.ShapeDtypeStruct((ROWS, HALF), BF),
        grid_spec=pltpu.PrefetchScalarGridSpec(
            num_scalar_prefetch=1,
            grid=(),
            in_specs=[anywhere] * 4,
            out_specs=anywhere,
            scratch_shapes=[pltpu.SemaphoreType.DMA((4,))],
        ),
        compiler_params=PARAMS,
        cost_estimate=cost(0, 4_000_000),
    )(place, *blocks)


def body(amplitudes, cycle_integrals, amp_map, cycle_map):
    row, col, core = (lax.axis_index(a) for a in AX)
    x, y, z = row, col // NZ, col % NZ
    g = jnp.where(core == 0, x, y)
    p = jnp.where(core == 0, y, x)
    place = jnp.stack([g, p, core, row * NY * NZ + col]).astype(jnp.int32)

    cyc = cycle_shares(place, cycle_map, cycle_integrals.T)
    plane = [[i * NY * NZ + j * NZ + k for i in range(NX) for j in range(NY)] for k in range(NZ)]
    cyc = lax.all_to_all(cyc, ("row", "col"), 0, 0, tiled=True, axis_index_groups=plane)
    cf, cb = shift_z(cyc, 1), shift_z(cyc, -1)
    cf2, cb2 = shift_z(cf, 1), shift_z(cb, -1)
    cf3, cb3 = shift_z(cf2, 1), shift_z(cb2, -1)
    middle = cyc.shape[0] // 2
    far = [shift_z(cb3[:middle], -1), shift_z(cf3[middle:], 1)]

    *sends, win = amp_shares(place, amp_map, amplitudes)
    blocks = [sends[0]] + [shift_g(sends[d], d) for d in (1, 2, 3)]

    win = win[:WD]
    f, b = shift_z(win, 1), shift_z(win, -1)
    f2, b2 = shift_z(f, 1), shift_z(b, -1)
    f3, b3 = shift_z(f2, 1), shift_z(b2, -1)
    b4 = shift_z(b3, -1)
    cuts = window_cut(place, [win, b, b2, b3, b4, f3, f2, f])
    win = window_order(place, [cuts[0]] + [shift_g(cuts[d], -d) for d in (1, 2, 3)])
    wf, wb = shift_p(win, 1), shift_p(win, -1)
    rows = win.shape[0] // 2
    rights = [win, wb, shift_p(wb[:rows], -1), shift_p(wf[rows:], 1), wf]

    here = lax.broadcasted_iota(jnp.int32, (QW, 1), 0)
    turn = here // 128
    hz = (z + jnp.where(turn % 2 == 1, (turn + 1) // 2, 8 - turn // 2)) % NZ
    hx, hy, hw = here // 32 % 4, here // 8 % 4, here % 8
    hg, hp = jnp.where(core == 0, hx, hy), jnp.where(core == 0, hy, hx)
    there = lax.broadcasted_iota(jnp.int32, (1, QW), 1)
    order = ((hp - p) % 4 * 256 + hg * 64 + (hz - z) % NZ * 8 + hw == there).astype(BF)
    there = lax.broadcasted_iota(jnp.int32, (1, QW // 2), 1) + core * (QW // 2)
    output_order = (hx * 256 + hy * 64 + hz * 8 + hw == there).astype(BF)

    away, own = dressed_first(blocks, [cyc, cb, cf, cb2, cf2, cb3, cf3])
    *away, total = dressed_last(blocks, far, away, own)
    back = [shift_g(away[d - 1], -d) for d in (1, 2, 3)]
    for value in back:
        total = total + value.astype(F32)
    full, inner = inner_call(total, swap_core(total), order)
    dressed = jnp.dot(full, output_order, preferred_element_type=F32).astype(BF)

    inners = [shift_g(inner, d) for d in (1, 2, 3)]
    outs = quadratic_blocks(inners, rights)
    outs = [shift_g(outs[d - 1], -d) for d in (1, 2, 3)]
    outs = list(quadratic_blocks([inner], rights)) + outs
    return (dressed, place_blocks(place, outs))


def solution(mesh):
    placed = (P(("row", "col"), "rep"), P("rep", ("row", "col")), P(("row", "col"), "rep"), P())
    return jax.shard_map(
        body,
        mesh=mesh,
        in_specs=placed,
        out_specs=(P(("row", "col"), "rep"), P(("row", "col"), "rep")),
        check_vma=False,
    )
```

time: 172 us -> 211 us (1.23)
  Pallas kernels: 0 us -> 62.8 us
  local copies, waits for them, and re-layouts: 24.6 us -> 6.42 us
  blocking collectives: 0 us -> 16.6 us
  matrix products: 17 us -> 1.2 us
  between operations: 14.6 us -> 1.08 us
  waiting for transfers between devices: 60.1 us -> 68.5 us
  other arithmetic: 7.28 us -> 1.47 us
  starting transfers between devices: 46.7 us -> 51.7 us
    pallas_call x0 -> x10, Pallas kernels: none -> 62.8 us  [the longest x1 49.3 us: place_blocks(): pl.pallas_call(place_kernel, out_shape=jax.ShapeDtypeStruct((ROWS, HALF),...]
    ppermute x7 -> x15, waiting for transfers between devices: 6.59 us -> 24.5 us  [shift_z(): lax.ppermute(value, AX, [(ident(x, y, z, c), ident(x, y, z + step, c)) fo...]
    all_to_all x0 -> x1, blocking collectives: none -> 16.6 us  [body(): lax.all_to_all(cyc, ('row', 'col'), 0, 0, tiled=True, axis_index_groups=p...]
    dot_general x10 -> x1, matrix products: 17 us -> 1.2 us  [body(): dressed = jnp.dot(full, output_order, preferred_element_type=F32).astype(BF)]
    ppermute x7 -> x15, starting transfers between devices: 14.9 us -> 29.7 us  [shift_z(): lax.ppermute(value, AX, [(ident(x, y, z, c), ident(x, y, z + step, c)) fo...]
    unnamed x40 -> x20, local copies, waits for them, and re-layouts: 20.2 us -> 6.3 us
    ppermute x19, waiting for transfers between devices: 53.5 us -> 44 us  [shift_plane(): return lax.ppermute(value, AX, pairs)]
    all_to_all x1 -> x0, starting transfers between devices: 7.03 us -> none  [body(): lax.all_to_all(send, ('row', 'col'), 0, 0, tiled=True, axis_index_groups=...]
  transfers between devices with their start and end apart: 29 -> 35, of which waited for: 16 -> 18; matrix products, arithmetic and copies ran while one was open for 26% -> 1% of each run, Pallas kernels for 0% -> 4%
where the time goes in v2:
time: 211 us; the launch traced here: 210 us
  waiting for transfers between devices  68.5 us (32%)
  Pallas kernels  62.8 us (30%)
  starting transfers between devices  51.7 us (25%)
  blocking collectives  16.6 us (8%)
  local copies, waits for them, and re-layouts  6.42 us (3%)
    pallas_call x1, Pallas kernels, place_blocks(): pl.pallas_call(place_kernel, out_shape=jax.ShapeDtypeStruct((ROWS, HALF),...  49.3 us
    ppermute x19, waiting for transfers between devices, shift_plane(): return lax.ppermute(value, AX, pairs)  44 us
    ppermute x15, starting transfers between devices, shift_z(): lax.ppermute(value, AX, [(ident(x, y, z, c), ident(x, y, z + step, c)) fo...  29.7 us
    ppermute x15, waiting for transfers between devices, shift_z(): lax.ppermute(value, AX, [(ident(x, y, z, c), ident(x, y, z + step, c)) fo...  24.5 us
    ppermute x19, starting transfers between devices, shift_plane(): return lax.ppermute(value, AX, pairs)  22 us
    all_to_all x1, blocking collectives, body(): lax.all_to_all(cyc, ('row', 'col'), 0, 0, tiled=True, axis_index_groups=p...  16.6 us
    unnamed x20, local copies, waits for them, and re-layouts  6.3 us
  transfers between devices with their start and end apart: 35, of which 18 were waited for; matrix products, arithmetic and copies ran while one was open for 1% of the time, Pallas kernels for 4%

profile of v2, /device:TPU:0, one launch (start us, length us, event | category | flops | bytes accessed | tf_op | source)
XLA Modules:
  0.0 209.7 jit_solution(16105387167995684641)
XLA Ops:
  4.2 16.6 %all_to_all.11 = bf16[16,8,2048]{2,1,0:T(8,128)(2,1)S(1)} all-to-all(bf16[16,8,2048]{2,1,0:T(8,128)(2,1)S(1)} %bitcast.8), channel_id=1, replica_groups={{0,16,32,48,64,80,96,112,128,144,160,176,192,208,224,240},{2,18,34,50,6..., dimensions={0} | all-to-all | bytes 1048576 | tf_op jit(solution)/shard_map/all_to_all | solution.py:295
  20.8 5.9 %collective-permute-start.3 = (bf16[128,2048]{1,0:T(8,128)(2,1)S(1)}, bf16[128,2048]{1,0:T(8,128)(2,1)S(1)}, u32[]{:S(2)}, u32[]{:S(2)}) collective-permute-start(bf16[128,2048]{1,0:T(8,128)(2,1)S(1)} %bitcast.9), channel_id=1, source_target_pairs={{0,14},{1,15},{2,0},{3,1},{4,2},{5,3},{6,4},{7,5},{8,6},{9,7},{10,... | collective-permute-start | bytes 1572872 | tf_op jit(solution)/shard_map/ppermute | solution.py:32
  26.7 9.7 %collective-permute-done.3.refs_5_ = bf16[128,2048]{1,0:T(8,128)(2,1)S(1)} collective-permute-done((bf16[128,2048]{1,0:T(8,128)(2,1)S(1)}, bf16[128,2048]{1,0:T(8,128)(2,1)S(1)}, u32[]{:S(2)}, u32[]{:S(2)}) %collective-permute-start.3) | collective-permute-done | bytes 524320 | tf_op jit(solution)/shard_map/ppermute | solution.py:32
  36.4 3.7 %collective-permute-start.4 = (bf16[128,2048]{1,0:T(8,128)(2,1)S(1)}, bf16[128,2048]{1,0:T(8,128)(2,1)S(1)}, u32[]{:S(2)}, u32[]{:S(2)}) collective-permute-start(bf16[128,2048]{1,0:T(8,128)(2,1)S(1)} %collective-permute-done.3.refs_5_), channel_id=1, source_target_pairs={{0,14},{1,15},{2,0},{3,1},{4,2},{5,3},{6,4},{7,5},{8,6},{9,7},{10,... | collective-permute-start | bytes 1572872 | tf_op jit(solution)/shard_map/ppermute | solution.py:32
  44.4 3.3 %collective-permute-start.15 = (bf16[8,8192]{1,0:T(8,128)(2,1)S(1)}, bf16[8,8192]{1,0:T(8,128)(2,1)S(1)}, u32[]{:S(2)}, u32[]{:S(2)}) collective-permute-start(bf16[8,8192]{1,0:T(8,128)(2,1)S(1)} %slice.17.refs_0_), channel_id=1, source_target_pairs={{0,14},{1,15},{2,0},{3,1},{4,2},{5,3},{6,4},{7,5},{8,6},{9,7},{10,... | collective-permute-start | bytes 393224 | tf_op jit(solution)/shard_map/ppermute | solution.py:32
  47.7 4.0 %collective-permute-done.15.refs_1_ = bf16[8,8192]{1,0:T(8,128)(2,1)S(1)} collective-permute-done((bf16[8,8192]{1,0:T(8,128)(2,1)S(1)}, bf16[8,8192]{1,0:T(8,128)(2,1)S(1)}, u32[]{:S(2)}, u32[]{:S(2)}) %collective-permute-start.15) | collective-permute-done | bytes 131104 | tf_op jit(solution)/shard_map/ppermute | solution.py:32
  51.7 3.7 %collective-permute-start.16 = (bf16[8,8192]{1,0:T(8,128)(2,1)S(1)}, bf16[8,8192]{1,0:T(8,128)(2,1)S(1)}, u32[]{:S(2)}, u32[]{:S(2)}) collective-permute-start(bf16[8,8192]{1,0:T(8,128)(2,1)S(1)} %collective-permute-done.15.refs_1_), channel_id=1, source_target_pairs={{0,14},{1,15},{2,0},{3,1},{4,2},{5,3},{6,4},{7,5},{8,6},{9,7},{10,... | collective-permute-start | bytes 393224 | tf_op jit(solution)/shard_map/ppermute | solution.py:32
  55.4 3.4 %collective-permute-done.16.refs_2_ = bf16[8,8192]{1,0:T(8,128)(2,1)S(1)} collective-permute-done((bf16[8,8192]{1,0:T(8,128)(2,1)S(1)}, bf16[8,8192]{1,0:T(8,128)(2,1)S(1)}, u32[]{:S(2)}, u32[]{:S(2)}) %collective-permute-start.16) | collective-permute-done | bytes 131104 | tf_op jit(solution)/shard_map/ppermute | solution.py:32
  58.7 3.7 %collective-permute-start.17 = (bf16[8,8192]{1,0:T(8,128)(2,1)S(1)}, bf16[8,8192]{1,0:T(8,128)(2,1)S(1)}, u32[]{:S(2)}, u32[]{:S(2)}) collective-permute-start(bf16[8,8192]{1,0:T(8,128)(2,1)S(1)} %collective-permute-done.16.refs_2_), channel_id=1, source_target_pairs={{0,14},{1,15},{2,0},{3,1},{4,2},{5,3},{6,4},{7,5},{8,6},{9,7},{10,... | collective-permute-start | bytes 393224 | tf_op jit(solution)/shard_map/ppermute | solution.py:32
  62.7 3.6 %collective-permute-done.17.refs_3_ = bf16[8,8192]{1,0:T(8,128)(2,1)S(1)} collective-permute-done((bf16[8,8192]{1,0:T(8,128)(2,1)S(1)}, bf16[8,8192]{1,0:T(8,128)(2,1)S(1)}, u32[]{:S(2)}, u32[]{:S(2)}) %collective-permute-start.17) | collective-permute-done | bytes 131104 | tf_op jit(solution)/shard_map/ppermute | solution.py:32
  66.3 3.7 %collective-permute-start.18 = (bf16[8,8192]{1,0:T(8,128)(2,1)S(1)}, bf16[8,8192]{1,0:T(8,128)(2,1)S(1)}, u32[]{:S(2)}, u32[]{:S(2)}) collective-permute-start(bf16[8,8192]{1,0:T(8,128)(2,1)S(1)} %collective-permute-done.17.refs_3_), channel_id=1, source_target_pairs={{0,14},{1,15},{2,0},{3,1},{4,2},{5,3},{6,4},{7,5},{8,6},{9,7},{10,... | collective-permute-start | bytes 393224 | tf_op jit(solution)/shard_map/ppermute | solution.py:32
  76.8 3.1 %collective-permute-done.22.refs_1_ = bf16[64,2048]{1,0:T(8,128)(2,1)S(1)} collective-permute-done((bf16[64,2048]{1,0:T(8,128)(2,1)S(1)}, bf16[64,2048]{1,0:T(8,128)(2,1)S(1)}, u32[]{:S(2)}, u32[]{:S(2)}) %collective-permute-start.22) | collective-permute-done | bytes 262176 | tf_op jit(solution)/shard_map/ppermute | solution.py:42
  83.2 9.2 %collective-permute-done.23.refs_2_ = bf16[64,2048]{1,0:T(8,128)(2,1)S(1)} collective-permute-done((bf16[64,2048]{1,0:T(8,128)(2,1)S(1)}, bf16[64,2048]{1,0:T(8,128)(2,1)S(1)}, u32[]{:S(2)}, u32[]{:S(2)}) %collective-permute-start.23) | collective-permute-done | bytes 262176 | tf_op jit(solution)/shard_map/ppermute | solution.py:42
  92.5 3.7 %collective-permute-start.6 = (bf16[64,2048]{1,0:T(8,128)(2,1)S(1)}, bf16[64,2048]{1,0:T(8,128)(2,1)S(1)}, u32[]{:S(2)}, u32[]{:S(2)}) collective-permute-start(bf16[64,2048]{1,0:T(8,128)(2,1)S(1)} %slice.20), channel_id=1, source_target_pairs={{0,14},{1,15},{2,0},{3,1},{4,2},{5,3},{6,4},{7,5},{8,6},{9,7},{10,... | collective-permute-start | bytes 786440 | tf_op jit(solution)/shard_map/ppermute | solution.py:32
  96.2 3.8 %collective-permute-done.24.refs_3_ = bf16[64,2048]{1,0:T(8,128)(2,1)S(1)} collective-permute-done((bf16[64,2048]{1,0:T(8,128)(2,1)S(1)}, bf16[64,2048]{1,0:T(8,128)(2,1)S(1)}, u32[]{:S(2)}, u32[]{:S(2)}) %collective-permute-start.24) | collective-permute-done | bytes 262176 | tf_op jit(solution)/shard_map/ppermute | solution.py:42
  105.1 2.9 %collective-permute-done.10.refs_5_ = bf16[64,2048]{1,0:T(8,128)(2,1)S(1)} collective-permute-done((bf16[64,2048]{1,0:T(8,128)(2,1)S(1)}, bf16[64,2048]{1,0:T(8,128)(2,1)S(1)}, u32[]{:S(2)}, u32[]{:S(2)}) %collective-permute-start.10) | collective-permute-done | bytes 262176 | tf_op jit(solution)/shard_map/ppermute | solution.py:32
  109.4 4.4 %collective-permute-start.12 = (bf16[128,1024]{1,0:T(8,128)(2,1)S(1)}, bf16[128,1024]{1,0:T(8,128)(2,1)S(1)}, u32[]{:S(2)}, u32[]{:S(2)}) collective-permute-start(bf16[128,1024]{1,0:T(8,128)(2,1)S(1)} %get-tuple-element.30), channel_id=1, source_target_pairs={{0,128},{1,33},{2,130},{3,35},{4,132},{5,37},{6,134},{7,39},{8,136... | collective-permute-start | bytes 786440 | tf_op jit(solution)/shard_map/ppermute | solution.py:42
  116.7 4.3 %collective-permute-done.12 = bf16[128,1024]{1,0:T(8,128)(2,1)S(1)} collective-permute-done((bf16[128,1024]{1,0:T(8,128)(2,1)S(1)}, bf16[128,1024]{1,0:T(8,128)(2,1)S(1)}, u32[]{:S(2)}, u32[]{:S(2)}) %collective-permute-start.12) | collective-permute-done | bytes 262176 | tf_op jit(solution)/shard_map/ppermute | solution.py:42
  126.7 3.6 %collective-permute-start.30 = (bf16[128,1024]{1,0:T(8,128)(2,1)S(1)}, bf16[128,1024]{1,0:T(8,128)(2,1)S(1)}, u32[]{:S(2)}, u32[]{:S(2)}) collective-permute-start(bf16[128,1024]{1,0:T(8,128)(2,1)S(1)} %get-tuple-element.33.refs_0_), channel_id=1, source_target_pairs={{0,128},{1,33},{2,130},{3,35},{4,132},{5,37},{6,134},{7,39},{8,136... | collective-permute-start | bytes 786440 | tf_op jit(solution)/shard_map/ppermute | solution.py:42
  131.3 3.7 %collective-permute-done.28.refs_4_.refs_6_ = bf16[128,2048]{1,0:T(8,128)(2,1)S(1)} collective-permute-done((bf16[128,2048]{1,0:T(8,128)(2,1)S(1)}, bf16[128,2048]{1,0:T(8,128)(2,1)S(1)}, u32[]{:S(2)}, u32[]{:S(2)}) %collective-permute-start.28) | collective-permute-done | bytes 524320 | tf_op jit(solution)/shard_map/ppermute | solution.py:42
  135.0 4.9 %collective-permute-done.29.refs_0_ = bf16[128,1024]{1,0:T(8,128)(2,1)S(1)} collective-permute-done((bf16[128,1024]{1,0:T(8,128)(2,1)S(1)}, bf16[128,1024]{1,0:T(8,128)(2,1)S(1)}, u32[]{:S(2)}, u32[]{:S(2)}) %collective-permute-start.29) | collective-permute-done | bytes 262176 | tf_op jit(solution)/shard_map/ppermute | solution.py:42
  149.2 3.2 %collective-permute-done.32.refs_1_ = bf16[128,2048]{1,0:T(8,128)(2,1)} collective-permute-done((bf16[128,2048]{1,0:T(8,128)(2,1)}, bf16[128,2048]{1,0:T(8,128)(2,1)}, u32[]{:S(2)}, u32[]{:S(2)}) %collective-permute-start.32) | collective-permute-done | bytes 524320 | tf_op jit(solution)/shard_map/ppermute | solution.py:42
  154.7 5.5 %collective-permute-done.34.refs_3_ = bf16[128,2048]{1,0:T(8,128)(2,1)} collective-permute-done((bf16[128,2048]{1,0:T(8,128)(2,1)}, bf16[128,2048]{1,0:T(8,128)(2,1)}, u32[]{:S(2)}, u32[]{:S(2)}) %collective-permute-start.34) | collective-permute-done | bytes 524320 | tf_op jit(solution)/shard_map/ppermute | solution.py:42
  160.2 49.3 %shard_map.68 = bf16[128,8192]{1,0:T(8,128)(2,1)} custom-call(s32[4]{0:T(128)S(1)} %pad_add_fusion.place, bf16[128,2048]{1,0:T(8,128)(2,1)S(1)} %shard_map.66.refs_0_, bf16[128,2048]{1,0:T(8,128)(2,1)} %collective-permute-done.32.refs_1_, bf16[128,2048]{1,0:T(8,128)(2,1)} %collective-permute-done.33.refs_2_, bf16[128,2048]{1,0:T(8,128)(2,1)} %collective-permute-done.34.refs_3_), custom_call_target="tpu_custom_call" | custom-call | bytes 4000000 | tf_op jit(solution)/shard_map/pallas_call | solution.py:271
  (89 shorter events, 45.7 us)
Async XLA Ops:
  20.8 15.6 %collective-permute-start.3 = (bf16[128,2048]{1,0:T(8,128)(2,1)S(1)}, bf16[128,2048]{1,0:T(8,128)(2,1)S(1)}, u32[]{:S(2)}, u32[]{:S(2)}) collective-permute-start(bf16[128,2048]{1,0:T(8,128)(2,1)S(1)} %bitcast.9), channel_id=1, source_target_pairs={{0,14},{1,15},{2,0},{3,1},{4,2},{5,3},{6,4},{7,5},{8,6},{9,7},{10,... | collective-permute-start | bytes 1572872 | tf_op jit(solution)/shard_map/ppermute | solution.py:32
  26.7 13.4 %collective-permute-start.7 = (bf16[128,2048]{1,0:T(8,128)(2,1)S(1)}, bf16[128,2048]{1,0:T(8,128)(2,1)S(1)}, u32[]{:S(2)}, u32[]{:S(2)}) collective-permute-start(bf16[128,2048]{1,0:T(8,128)(2,1)S(1)} %bitcast.10), channel_id=1, source_target_pairs={{0,2},{1,3},{2,4},{3,5},{4,6},{5,7},{6,8},{7,9},{8,10},{9,11},{10,... | collective-permute-start | bytes 1572872 | tf_op jit(solution)/shard_map/ppermute | solution.py:32
  36.4 33.6 %collective-permute-start.4 = (bf16[128,2048]{1,0:T(8,128)(2,1)S(1)}, bf16[128,2048]{1,0:T(8,128)(2,1)S(1)}, u32[]{:S(2)}, u32[]{:S(2)}) collective-permute-start(bf16[128,2048]{1,0:T(8,128)(2,1)S(1)} %collective-permute-done.3.refs_5_), channel_id=1, source_target_pairs={{0,14},{1,15},{2,0},{3,1},{4,2},{5,3},{6,4},{7,5},{8,6},{9,7},{10,... | collective-permute-start | bytes 1572872 | tf_op jit(solution)/shard_map/ppermute | solution.py:32
  40.1 29.9 %collective-permute-start.8 = (bf16[128,2048]{1,0:T(8,128)(2,1)S(1)}, bf16[128,2048]{1,0:T(8,128)(2,1)S(1)}, u32[]{:S(2)}, u32[]{:S(2)}) collective-permute-start(bf16[128,2048]{1,0:T(8,128)(2,1)S(1)} %collective-permute-done.7.refs_6_), channel_id=1, source_target_pairs={{0,2},{1,3},{2,4},{3,5},{4,6},{5,7},{6,8},{7,9},{8,10},{9,11},{10,... | collective-permute-start | bytes 1572872 | tf_op jit(solution)/shard_map/ppermute | solution.py:32
  62.6 9.4 %collective-permute-start.21 = (bf16[8,8192]{1,0:T(8,128)(2,1)S(1)}, bf16[8,8192]{1,0:T(8,128)(2,1)S(1)}, u32[]{:S(2)}, u32[]{:S(2)}) collective-permute-start(bf16[8,8192]{1,0:T(8,128)(2,1)S(1)} %collective-permute-done.20.refs_6_), channel_id=1, source_target_pairs={{0,2},{1,3},{2,4},{3,5},{4,6},{5,7},{6,8},{7,9},{8,10},{9,11},{10,... | collective-permute-start | bytes 393224 | tf_op jit(solution)/shard_map/ppermute | solution.py:32
  70.0 12.3 %collective-permute-start.5 = (bf16[128,2048]{1,0:T(8,128)(2,1)S(1)}, bf16[128,2048]{1,0:T(8,128)(2,1)S(1)}, u32[]{:S(2)}, u32[]{:S(2)}) collective-permute-start(bf16[128,2048]{1,0:T(8,128)(2,1)S(1)} %collective-permute-done.4.refs_7_), channel_id=1, source_target_pairs={{0,14},{1,15},{2,0},{3,1},{4,2},{5,3},{6,4},{7,5},{8,6},{9,7},{10,... | collective-permute-start | bytes 1572872 | tf_op jit(solution)/shard_map/ppermute | solution.py:32
  70.0 12.3 %collective-permute-start.9 = (bf16[128,2048]{1,0:T(8,128)(2,1)S(1)}, bf16[128,2048]{1,0:T(8,128)(2,1)S(1)}, u32[]{:S(2)}, u32[]{:S(2)}) collective-permute-start(bf16[128,2048]{1,0:T(8,128)(2,1)S(1)} %collective-permute-done.8.refs_8_), channel_id=1, source_target_pairs={{0,2},{1,3},{2,4},{3,5},{4,6},{5,7},{6,8},{7,9},{8,10},{9,11},{10,... | collective-permute-start | bytes 1572872 | tf_op jit(solution)/shard_map/ppermute | solution.py:32
  74.7 25.9 %collective-permute-start = (bf16[128,2048]{1,0:T(8,128)(2,1)S(1)}, bf16[128,2048]{1,0:T(8,128)(2,1)S(1)}, u32[]{:S(2)}, u32[]{:S(2)}) collective-permute-start(bf16[128,2048]{1,0:T(8,128)(2,1)S(1)} %get-tuple-element.23), channel_id=1, source_target_pairs={{0,64},{1,17},{2,66},{3,19},{4,68},{5,21},{6,70},{7,23},{8,72},{9,... | collective-permute-start | bytes 1572872 | tf_op jit(solution)/shard_map/ppermute | solution.py:42
  75.5 25.2 %collective-permute-start.1 = (bf16[128,2048]{1,0:T(8,128)(2,1)S(1)}, bf16[128,2048]{1,0:T(8,128)(2,1)S(1)}, u32[]{:S(2)}, u32[]{:S(2)}) collective-permute-start(bf16[128,2048]{1,0:T(8,128)(2,1)S(1)} %get-tuple-element.24), channel_id=1, source_target_pairs={{0,128},{1,33},{2,130},{3,35},{4,132},{5,37},{6,134},{7,39},{8,136... | collective-permute-start | bytes 1572872 | tf_op jit(solution)/shard_map/ppermute | solution.py:42
  79.9 22.9 %collective-permute-start.2 = (bf16[128,2048]{1,0:T(8,128)(2,1)S(1)}, bf16[128,2048]{1,0:T(8,128)(2,1)S(1)}, u32[]{:S(2)}, u32[]{:S(2)}) collective-permute-start(bf16[128,2048]{1,0:T(8,128)(2,1)S(1)} %get-tuple-element.25), channel_id=1, source_target_pairs={{0,192},{1,49},{2,194},{3,51},{4,196},{5,53},{6,198},{7,55},{8,200... | collective-permute-start | bytes 1572872 | tf_op jit(solution)/shard_map/ppermute | solution.py:42
  82.3 10.2 %collective-permute-start.23 = (bf16[64,2048]{1,0:T(8,128)(2,1)S(1)}, bf16[64,2048]{1,0:T(8,128)(2,1)S(1)}, u32[]{:S(2)}, u32[]{:S(2)}) collective-permute-start(bf16[64,2048]{1,0:T(8,128)(2,1)S(1)} %get-tuple-element.37), channel_id=1, source_target_pairs={{0,128},{1,33},{2,130},{3,35},{4,132},{5,37},{6,134},{7,39},{8,136... | collective-permute-start | bytes 786440 | tf_op jit(solution)/shard_map/ppermute | solution.py:42
  82.3 17.7 %collective-permute-start.24 = (bf16[64,2048]{1,0:T(8,128)(2,1)S(1)}, bf16[64,2048]{1,0:T(8,128)(2,1)S(1)}, u32[]{:S(2)}, u32[]{:S(2)}) collective-permute-start(bf16[64,2048]{1,0:T(8,128)(2,1)S(1)} %get-tuple-element.38), channel_id=1, source_target_pairs={{0,64},{1,17},{2,66},{3,19},{4,68},{5,21},{6,70},{7,23},{8,72},{9,... | collective-permute-start | bytes 786440 | tf_op jit(solution)/shard_map/ppermute | solution.py:42
  92.5 12.7 %collective-permute-start.6 = (bf16[64,2048]{1,0:T(8,128)(2,1)S(1)}, bf16[64,2048]{1,0:T(8,128)(2,1)S(1)}, u32[]{:S(2)}, u32[]{:S(2)}) collective-permute-start(bf16[64,2048]{1,0:T(8,128)(2,1)S(1)} %slice.20), channel_id=1, source_target_pairs={{0,14},{1,15},{2,0},{3,1},{4,2},{5,3},{6,4},{7,5},{8,6},{9,7},{10,... | collective-permute-start | bytes 786440 | tf_op jit(solution)/shard_map/ppermute | solution.py:32
  100.7 21.3 %collective-permute-start.25 = (bf16[256,2048]{1,0:T(8,128)(2,1)S(1)}, bf16[256,2048]{1,0:T(8,128)(2,1)S(1)}, u32[]{:S(2)}, u32[]{:S(2)}) collective-permute-start(bf16[256,2048]{1,0:T(8,128)(2,1)S(1)} %shard_map.65.refs_1_.refs_3_), channel_id=1, source_target_pairs={{0,48},{1,193},{2,50},{3,195},{4,52},{5,197},{6,54},{7,199},{8,56}... | collective-permute-start | bytes 3145736 | tf_op jit(solution)/shard_map/ppermute | solution.py:42
  100.8 21.4 %collective-permute-start.27 = (bf16[256,2048]{1,0:T(8,128)(2,1)S(1)}, bf16[256,2048]{1,0:T(8,128)(2,1)S(1)}, u32[]{:S(2)}, u32[]{:S(2)}) collective-permute-start(bf16[256,2048]{1,0:T(8,128)(2,1)S(1)} %shard_map.65.refs_1_.refs_3_), channel_id=1, source_target_pairs={{0,16},{1,65},{2,18},{3,67},{4,20},{5,69},{6,22},{7,71},{8,24},{9,... | collective-permute-start | bytes 3145736 | tf_op jit(solution)/shard_map/ppermute | solution.py:42
  109.4 11.6 %collective-permute-start.12 = (bf16[128,1024]{1,0:T(8,128)(2,1)S(1)}, bf16[128,1024]{1,0:T(8,128)(2,1)S(1)}, u32[]{:S(2)}, u32[]{:S(2)}) collective-permute-start(bf16[128,1024]{1,0:T(8,128)(2,1)S(1)} %get-tuple-element.30), channel_id=1, source_target_pairs={{0,128},{1,33},{2,130},{3,35},{4,132},{5,37},{6,134},{7,39},{8,136... | collective-permute-start | bytes 786440 | tf_op jit(solution)/shard_map/ppermute | solution.py:42
  122.0 9.3 %collective-permute-start.26 = (bf16[128,2048]{1,0:T(8,128)(2,1)S(1)}, bf16[128,2048]{1,0:T(8,128)(2,1)S(1)}, u32[]{:S(2)}, u32[]{:S(2)}) collective-permute-start(bf16[128,2048]{1,0:T(8,128)(2,1)S(1)} %slice.22), channel_id=1, source_target_pairs={{0,48},{1,193},{2,50},{3,195},{4,52},{5,197},{6,54},{7,199},{8,56}... | collective-permute-start | bytes 1572872 | tf_op jit(solution)/shard_map/ppermute | solution.py:42
  122.2 12.8 %collective-permute-start.28 = (bf16[128,2048]{1,0:T(8,128)(2,1)S(1)}, bf16[128,2048]{1,0:T(8,128)(2,1)S(1)}, u32[]{:S(2)}, u32[]{:S(2)}) collective-permute-start(bf16[128,2048]{1,0:T(8,128)(2,1)S(1)} %slice.23), channel_id=1, source_target_pairs={{0,16},{1,65},{2,18},{3,67},{4,20},{5,69},{6,22},{7,71},{8,24},{9,... | collective-permute-start | bytes 1572872 | tf_op jit(solution)/shard_map/ppermute | solution.py:42
  126.6 13.3 %collective-permute-start.29 = (bf16[128,1024]{1,0:T(8,128)(2,1)S(1)}, bf16[128,1024]{1,0:T(8,128)(2,1)S(1)}, u32[]{:S(2)}, u32[]{:S(2)}) collective-permute-start(bf16[128,1024]{1,0:T(8,128)(2,1)S(1)} %get-tuple-element.33.refs_0_), channel_id=1, source_target_pairs={{0,64},{1,17},{2,66},{3,19},{4,68},{5,21},{6,70},{7,23},{8,72},{9,... | collective-permute-start | bytes 786440 | tf_op jit(solution)/shard_map/ppermute | solution.py:42
  126.7 13.2 %collective-permute-start.30 = (bf16[128,1024]{1,0:T(8,128)(2,1)S(1)}, bf16[128,1024]{1,0:T(8,128)(2,1)S(1)}, u32[]{:S(2)}, u32[]{:S(2)}) collective-permute-start(bf16[128,1024]{1,0:T(8,128)(2,1)S(1)} %get-tuple-element.33.refs_0_), channel_id=1, source_target_pairs={{0,128},{1,33},{2,130},{3,35},{4,132},{5,37},{6,134},{7,39},{8,136... | collective-permute-start | bytes 786440 | tf_op jit(solution)/shard_map/ppermute | solution.py:42
  130.3 9.6 %collective-permute-start.31 = (bf16[128,1024]{1,0:T(8,128)(2,1)S(1)}, bf16[128,1024]{1,0:T(8,128)(2,1)S(1)}, u32[]{:S(2)}, u32[]{:S(2)}) collective-permute-start(bf16[128,1024]{1,0:T(8,128)(2,1)S(1)} %get-tuple-element.33.refs_0_), channel_id=1, source_target_pairs={{0,192},{1,49},{2,194},{3,51},{4,196},{5,53},{6,198},{7,55},{8,200... | collective-permute-start | bytes 786440 | tf_op jit(solution)/shard_map/ppermute | solution.py:42
  142.8 9.6 %collective-permute-start.32 = (bf16[128,2048]{1,0:T(8,128)(2,1)}, bf16[128,2048]{1,0:T(8,128)(2,1)}, u32[]{:S(2)}, u32[]{:S(2)}) collective-permute-start(bf16[128,2048]{1,0:T(8,128)(2,1)} %get-tuple-element.39), channel_id=1, source_target_pairs={{0,192},{1,49},{2,194},{3,51},{4,196},{5,53},{6,198},{7,55},{8,200... | collective-permute-start | bytes 1572872 | tf_op jit(solution)/shard_map/ppermute | solution.py:42
  143.6 11.1 %collective-permute-start.33 = (bf16[128,2048]{1,0:T(8,128)(2,1)}, bf16[128,2048]{1,0:T(8,128)(2,1)}, u32[]{:S(2)}, u32[]{:S(2)}) collective-permute-start(bf16[128,2048]{1,0:T(8,128)(2,1)} %get-tuple-element.40), channel_id=1, source_target_pairs={{0,128},{1,33},{2,130},{3,35},{4,132},{5,37},{6,134},{7,39},{8,136... | collective-permute-start | bytes 1572872 | tf_op jit(solution)/shard_map/ppermute | solution.py:42
  143.6 16.6 %collective-permute-start.34 = (bf16[128,2048]{1,0:T(8,128)(2,1)}, bf16[128,2048]{1,0:T(8,128)(2,1)}, u32[]{:S(2)}, u32[]{:S(2)}) collective-permute-start(bf16[128,2048]{1,0:T(8,128)(2,1)} %get-tuple-element.41), channel_id=1, source_target_pairs={{0,64},{1,17},{2,66},{3,19},{4,68},{5,21},{6,70},{7,23},{8,72},{9,... | collective-permute-start | bytes 1572872 | tf_op jit(solution)/shard_map/ppermute | solution.py:42
  (21 other events, 118.4 us)

commit v3 on v2

--- a/solution.py
+++ b/solution.py
@@ -58,35 +58,67 @@
     return pl.CostEstimate(flops=flops, bytes_accessed=moved, transcendentals=0)
 
 
-def cycle_kernel(place, cyc_map, cyc, out):
+def cycle_kernel(place, cyc_map, cyc, *outs):
     core, column = place[2], place[3]
     tiles = HALF // TB
-    shares = []
-    for share in range(4):
-        cut = []
-        for t in range(share * 16, share * 16 + 16):
-            keep = cyc_map[core * tiles + t, column].astype(F32)
-            cut.append((cyc[:, t * TB : (t + 1) * TB].astype(F32) * keep))
-        shares.append(jnp.concatenate(cut, 1))
-    first = core == 0
-    for i in range(4):
-        for j in range(0, 4, 2):
-            top = jnp.where(first, shares[i], shares[j])
-            low = jnp.where(first, shares[i], shares[j + 1])
-            at = (i * 4 + j) * WD
-            out[at : at + 2 * WD, :] = jnp.concatenate([top, low], 0).astype(BF)
+    for d in range(4):
+        share = lax.rem(place[0] + d, 4)
+        for t in range(PART // TB):
+            keep = cyc_map[core * tiles + share * 16 + t, column].astype(F32)
+            at = pl.multiple_of(share * PART + t * TB, TB)
+            outs[d][:, t * TB : (t + 1) * TB] = (cyc[:, pl.ds(at, TB)].astype(F32) * keep).astype(BF)
 
 
 def cycle_shares(place, cycle_map, cyc):
     return pl.pallas_call(
         cycle_kernel,
+        out_shape=[jax.ShapeDtypeStruct((WD, PART), BF)] * 4,
+        grid_spec=pltpu.PrefetchScalarGridSpec(
+            num_scalar_prefetch=2, grid=(), in_specs=[VMEM], out_specs=[VMEM] * 4
+        ),
+        compiler_params=PARAMS,
+        cost_estimate=cost(0, 300_000),
+    )(place, cycle_map, cyc)
+
+
+def stack_kernel(*refs):
+    refs[4][...] = jnp.concatenate([ref[...] for ref in refs[:4]], 0)
+
+
+def stack(pieces):
+    return pl.pallas_call(
+        stack_kernel,
+        out_shape=jax.ShapeDtypeStruct((4 * pieces[0].shape[0], PART), BF),
+        in_specs=[VMEM] * 4,
+        out_specs=VMEM,
+        compiler_params=PARAMS,
+        cost_estimate=cost(0, 300_000),
+    )(*pieces)
+
+
+def plane_kernel(place, *refs):
+    pieces, out = refs[:4], refs[4]
+    rows = 16 * WD
+    here = lax.broadcasted_iota(jnp.int32, (rows, rows), 1)
+    there = lax.broadcasted_iota(jnp.int32, (rows, rows), 0)
+    hp, hg, hw = (here // 32 + place[1]) % 4, (here // 8 + place[0]) % 4, here % 8
+    first = place[2] == 0
+    at = jnp.where(first, hg * 32 + hp * 8, hp * 32 + hg * 8) + hw
+    order = (at == there).astype(F32).astype(BF)
+    value = jnp.concatenate([ref[...] for ref in pieces], 0)
+    out[...] = jnp.dot(order, value, preferred_element_type=F32).astype(BF)
+
+
+def plane_order(place, pieces):
+    return pl.pallas_call(
+        plane_kernel,
         out_shape=jax.ShapeDtypeStruct((16 * WD, PART), BF),
         grid_spec=pltpu.PrefetchScalarGridSpec(
-            num_scalar_prefetch=2, grid=(), in_specs=[VMEM], out_specs=VMEM
-        ),
-        compiler_params=PARAMS,
-        cost_estimate=cost(0, 700_000),
-    )(place, cycle_map, cyc)
+            num_scalar_prefetch=1, grid=(), in_specs=[VMEM] * 4, out_specs=VMEM
+        ),
+        compiler_params=PARAMS,
+        cost_estimate=cost(2 * 128 * 128 * PART, 1_000_000),
+    )(place, *pieces)
 
 
 def amp_kernel(place, amp_map, *refs):
@@ -255,32 +287,31 @@
 
 
 def place_kernel(place, *refs):
-    ins, out, sem = refs[:4], refs[4], refs[5]
-    copies = []
+    ins, out = refs[:4], refs[4]
     for d in range(4):
         at = pl.multiple_of(lax.rem(place[0] + d, 4) * PART, PART)
-        copies.append(pltpu.make_async_copy(ins[d], out.at[:, pl.ds(at, PART)], sem.at[d]))
-    for copy in copies:
-        copy.start()
-    for copy in copies:
-        copy.wait()
+        out[:, pl.ds(at, PART)] = ins[d][...]
 
 
 def place_blocks(place, blocks):
-    anywhere = pl.BlockSpec(memory_space=pl.ANY)
+    block = 32
     return pl.pallas_call(
         place_kernel,
         out_shape=jax.ShapeDtypeStruct((ROWS, HALF), BF),
         grid_spec=pltpu.PrefetchScalarGridSpec(
             num_scalar_prefetch=1,
-            grid=(),
-            in_specs=[anywhere] * 4,
-            out_specs=anywhere,
-            scratch_shapes=[pltpu.SemaphoreType.DMA((4,))],
+            grid=(ROWS // block,),
+            in_specs=[pl.BlockSpec((block, PART), lambda i, place: (i, 0))] * 4,
+            out_specs=pl.BlockSpec((block, HALF), lambda i, place: (i, 0)),
         ),
         compiler_params=PARAMS,
         cost_estimate=cost(0, 4_000_000),
     )(place, *blocks)
+
+
+def after(values, *others):
+    count = len(values)
+    return lax.optimization_barrier(tuple(values) + others)[:count]
 
 
 def body(amplitudes, cycle_integrals, amp_map, cycle_map):
@@ -290,28 +321,37 @@
     p = jnp.where(core == 0, y, x)
     place = jnp.stack([g, p, core, row * NY * NZ + col]).astype(jnp.int32)
 
-    cyc = cycle_shares(place, cycle_map, cycle_integrals.T)
-    plane = [[i * NY * NZ + j * NZ + k for i in range(NX) for j in range(NY)] for k in range(NZ)]
-    cyc = lax.all_to_all(cyc, ("row", "col"), 0, 0, tiled=True, axis_index_groups=plane)
+    shares = cycle_shares(place, cycle_map, cycle_integrals.T)
+    shares = [shares[0]] + [shift_g(shares[4 - d], -d) for d in (1, 2, 3)]
+    *sends, win = amp_shares(place, amp_map, amplitudes)
+    win = win[:WD]
+    cyc = stack(after(shares, win))
+    sends[1:2] = after(sends[1:2], cyc)
+    block1 = shift_g(sends[1], 1)
+    wf, wb = shift_z(win, 1), shift_z(win, -1)
+    cyc = plane_order(place, after([cyc] + [shift_p(cyc, -e) for e in (1, 2, 3)], wf, wb))
+
     cf, cb = shift_z(cyc, 1), shift_z(cyc, -1)
+    wf, wb, sends[3] = after([wf, wb, sends[3]], cyc)
+    wf2, wb2 = shift_z(wf, 1), shift_z(wb, -1)
+    block3 = shift_g(sends[3], 3)
+    wf3, wb3 = shift_z(wf2, 1), shift_z(wb2, -1)
+    cf, cb, wb3, sends[2], block1 = after([cf, cb, wb3, sends[2], block1], wf3)
+
     cf2, cb2 = shift_z(cf, 1), shift_z(cb, -1)
+    wb4 = shift_z(wb3, -1)
+    block2 = shift_g(sends[2], 2)
+    cuts = window_cut(place, [win, wb, wb2, wb3, wb4, wf3, wf2, wf])
+    cf2, cb2, block3, *cuts = after([cf2, cb2, block3, *cuts])
+
     cf3, cb3 = shift_z(cf2, 1), shift_z(cb2, -1)
+    win = window_order(place, [cuts[0]] + [shift_g(cuts[d], -d) for d in (1, 2, 3)])
+    cf3, cb3, block2, win = after([cf3, cb3, block2, win])
+
     middle = cyc.shape[0] // 2
     far = [shift_z(cb3[:middle], -1), shift_z(cf3[middle:], 1)]
-
-    *sends, win = amp_shares(place, amp_map, amplitudes)
-    blocks = [sends[0]] + [shift_g(sends[d], d) for d in (1, 2, 3)]
-
-    win = win[:WD]
-    f, b = shift_z(win, 1), shift_z(win, -1)
-    f2, b2 = shift_z(f, 1), shift_z(b, -1)
-    f3, b3 = shift_z(f2, 1), shift_z(b2, -1)
-    b4 = shift_z(b3, -1)
-    cuts = window_cut(place, [win, b, b2, b3, b4, f3, f2, f])
-    win = window_order(place, [cuts[0]] + [shift_g(cuts[d], -d) for d in (1, 2, 3)])
     wf, wb = shift_p(win, 1), shift_p(win, -1)
-    rows = win.shape[0] // 2
-    rights = [win, wb, shift_p(wb[:rows], -1), shift_p(wf[rows:], 1), wf]
+    blocks = [sends[0], block1, block2, block3]
 
     here = lax.broadcasted_iota(jnp.int32, (QW, 1), 0)
     turn = here // 128
@@ -326,9 +366,13 @@
     away, own = dressed_first(blocks, [cyc, cb, cf, cb2, cf2, cb3, cf3])
     *away, total = dressed_last(blocks, far, away, own)
     back = [shift_g(away[d - 1], -d) for d in (1, 2, 3)]
+    wf, wb, *back = after([wf, wb, *back])
     for value in back:
         total = total + value.astype(F32)
-    full, inner = inner_call(total, swap_core(total), order)
+    other = swap_core(total)
+    rows = win.shape[0] // 2
+    rights = [win, wb, shift_p(wb[:rows], -1), shift_p(wf[rows:], 1), wf]
+    full, inner = inner_call(total, other, order)
     dressed = jnp.dot(full, output_order, preferred_element_type=F32).astype(BF)
 
     inners = [shift_g(inner, d) for d in (1, 2, 3)]

time: 211 us -> 169 us (0.80)
  Pallas kernels: 62.8 us -> 18.6 us
  blocking collectives: 16.6 us -> 0 us
  starting transfers between devices: 51.7 us -> 67.9 us
  waiting for transfers between devices: 68.5 us -> 70.9 us
    pallas_call x1, Pallas kernels: 49.3 us -> 4.29 us  [place_blocks(): pl.pallas_call(place_kernel, out_shape=jax.ShapeDtypeStruct((ROWS, HALF),...]
    ppermute x19 -> x25, starting transfers between devices: 22 us -> 42 us  [shift_plane(): return lax.ppermute(value, AX, pairs)]
    all_to_all x1 -> x0, blocking collectives: 16.6 us -> none  [body(): lax.all_to_all(cyc, ('row', 'col'), 0, 0, tiled=True, axis_index_groups=p...]
    ppermute x15, waiting for transfers between devices: 24.5 us -> 30.3 us  [shift_z(): lax.ppermute(value, AX, [(ident(x, y, z, c), ident(x, y, z + step, c)) fo...]
    ppermute x15, starting transfers between devices: 29.7 us -> 25.9 us  [shift_z(): lax.ppermute(value, AX, [(ident(x, y, z, c), ident(x, y, z + step, c)) fo...]
    ppermute x19 -> x25, waiting for transfers between devices: 44 us -> 40.6 us  [shift_plane(): return lax.ppermute(value, AX, pairs)]
  transfers between devices with their start and end apart: 35 -> 41, of which waited for: 18 -> 19; matrix products, arithmetic and copies ran while one was open for 1% -> 1% of each run, Pallas kernels for 4% -> 6%
where the time goes in v3:
time: 169 us; the launch traced here: 167 us
  waiting for transfers between devices  70.9 us (42%)
  starting transfers between devices  67.9 us (40%)
  Pallas kernels  18.6 us (11%)
  local copies, waits for them, and re-layouts  6.42 us (4%)
    ppermute x25, starting transfers between devices, shift_plane(): return lax.ppermute(value, AX, pairs)  42 us
    ppermute x25, waiting for transfers between devices, shift_plane(): return lax.ppermute(value, AX, pairs)  40.6 us
    ppermute x15, waiting for transfers between devices, shift_z(): lax.ppermute(value, AX, [(ident(x, y, z, c), ident(x, y, z + step, c)) fo...  30.3 us
    ppermute x15, starting transfers between devices, shift_z(): lax.ppermute(value, AX, [(ident(x, y, z, c), ident(x, y, z + step, c)) fo...  25.9 us
    unnamed x20, local copies, waits for them, and re-layouts  6.3 us
    pallas_call x1, Pallas kernels, place_blocks(): pl.pallas_call(place_kernel, out_shape=jax.ShapeDtypeStruct((ROWS, HALF),...  4.29 us
    pallas_call x2, Pallas kernels, quadratic_blocks(): pl.pallas_call(functools.partial(quadratic_kernel, count), out_shape=[jax...  3.62 us
  transfers between devices with their start and end apart: 41, of which 19 were waited for; matrix products, arithmetic and copies ran while one was open for 1% of the time, Pallas kernels for 6%

profile of v3, /device:TPU:0, one launch (start us, length us, event | category | flops | bytes accessed | tf_op | source)
XLA Modules:
  0.0 167.4 jit_solution(10247613275697951297)
XLA Ops:
  13.4 4.0 %collective-permute-start.7 = (bf16[8,8192]{1,0:T(8,128)(2,1)S(1)}, bf16[8,8192]{1,0:T(8,128)(2,1)S(1)}, u32[]{:S(2)}, u32[]{:S(2)}) collective-permute-start(bf16[8,8192]{1,0:T(8,128)(2,1)S(1)} %slice.15.refs_0_), channel_id=1, source_target_pairs={{0,14},{1,15},{2,0},{3,1},{4,2},{5,3},{6,4},{7,5},{8,6},{9,7},{10,... | collective-permute-start | bytes 393224 | tf_op jit(solution)/shard_map/ppermute | solution.py:32
  17.5 3.1 %collective-permute-start.3 = (bf16[32,2048]{1,0:T(8,128)(2,1)S(1)}, bf16[32,2048]{1,0:T(8,128)(2,1)S(1)}, u32[]{:S(2)}, u32[]{:S(2)}) collective-permute-start(bf16[32,2048]{1,0:T(8,128)(2,1)S(1)} %shard_map.61.refs_0_), channel_id=1, source_target_pairs={{0,48},{1,193},{2,50},{3,195},{4,52},{5,197},{6,54},{7,199},{8,56}... | collective-permute-start | bytes 393224 | tf_op jit(solution)/shard_map/ppermute | solution.py:42
  24.5 4.0 %collective-permute-done.4.refs_2_ = bf16[32,2048]{1,0:T(8,128)(2,1)S(1)} collective-permute-done((bf16[32,2048]{1,0:T(8,128)(2,1)S(1)}, bf16[32,2048]{1,0:T(8,128)(2,1)S(1)}, u32[]{:S(2)}, u32[]{:S(2)}) %collective-permute-start.4) | collective-permute-done | bytes 131104 | tf_op jit(solution)/shard_map/ppermute | solution.py:42
  31.0 3.2 %collective-permute-start.9 = (bf16[128,2048]{1,0:T(8,128)(2,1)S(1)}, bf16[128,2048]{1,0:T(8,128)(2,1)S(1)}, u32[]{:S(2)}, u32[]{:S(2)}) collective-permute-start(bf16[128,2048]{1,0:T(8,128)(2,1)S(1)} %shard_map.62.refs_4_), channel_id=1, source_target_pairs={{0,14},{1,15},{2,0},{3,1},{4,2},{5,3},{6,4},{7,5},{8,6},{9,7},{10,... | collective-permute-start | bytes 1572872 | tf_op jit(solution)/shard_map/ppermute | solution.py:32
  36.3 9.1 %collective-permute-done.10.refs_2_ = bf16[8,8192]{1,0:T(8,128)(2,1)S(1)} collective-permute-done((bf16[8,8192]{1,0:T(8,128)(2,1)S(1)}, bf16[8,8192]{1,0:T(8,128)(2,1)S(1)}, u32[]{:S(2)}, u32[]{:S(2)}) %collective-permute-start.10) | collective-permute-done | bytes 131104 | tf_op jit(solution)/shard_map/ppermute | solution.py:32
  45.3 3.7 %collective-permute-start.11 = (bf16[8,8192]{1,0:T(8,128)(2,1)S(1)}, bf16[8,8192]{1,0:T(8,128)(2,1)S(1)}, u32[]{:S(2)}, u32[]{:S(2)}) collective-permute-start(bf16[8,8192]{1,0:T(8,128)(2,1)S(1)} %collective-permute-done.10.refs_2_), channel_id=1, source_target_pairs={{0,14},{1,15},{2,0},{3,1},{4,2},{5,3},{6,4},{7,5},{8,6},{9,7},{10,... | collective-permute-start | bytes 393224 | tf_op jit(solution)/shard_map/ppermute | solution.py:32
  49.0 2.9 %collective-permute-done.11.refs_3_ = bf16[8,8192]{1,0:T(8,128)(2,1)S(1)} collective-permute-done((bf16[8,8192]{1,0:T(8,128)(2,1)S(1)}, bf16[8,8192]{1,0:T(8,128)(2,1)S(1)}, u32[]{:S(2)}, u32[]{:S(2)}) %collective-permute-start.11) | collective-permute-done | bytes 131104 | tf_op jit(solution)/shard_map/ppermute | solution.py:32
  53.7 3.0 %collective-permute-done.14.refs_5_ = bf16[8,8192]{1,0:T(8,128)(2,1)S(1)} collective-permute-done((bf16[8,8192]{1,0:T(8,128)(2,1)S(1)}, bf16[8,8192]{1,0:T(8,128)(2,1)S(1)}, u32[]{:S(2)}, u32[]{:S(2)}) %collective-permute-start.14) | collective-permute-done | bytes 131104 | tf_op jit(solution)/shard_map/ppermute | solution.py:32
  56.8 3.2 %collective-permute-start.16 = (bf16[128,2048]{1,0:T(8,128)(2,1)S(1)}, bf16[128,2048]{1,0:T(8,128)(2,1)S(1)}, u32[]{:S(2)}, u32[]{:S(2)}) collective-permute-start(bf16[128,2048]{1,0:T(8,128)(2,1)S(1)} %collective-permute-done.9.refs_5_), channel_id=1, source_target_pairs={{0,14},{1,15},{2,0},{3,1},{4,2},{5,3},{6,4},{7,5},{8,6},{9,7},{10,... | collective-permute-start | bytes 1572872 | tf_op jit(solution)/shard_map/ppermute | solution.py:32
  60.0 10.1 %collective-permute-done.18.refs_4_ = bf16[8,8192]{1,0:T(8,128)(2,1)S(1)} collective-permute-done((bf16[8,8192]{1,0:T(8,128)(2,1)S(1)}, bf16[8,8192]{1,0:T(8,128)(2,1)S(1)}, u32[]{:S(2)}, u32[]{:S(2)}) %collective-permute-start.18) | collective-permute-done | bytes 131104 | tf_op jit(solution)/shard_map/ppermute | solution.py:32
  71.3 3.2 %collective-permute-start.21 = (bf16[128,2048]{1,0:T(8,128)(2,1)S(1)}, bf16[128,2048]{1,0:T(8,128)(2,1)S(1)}, u32[]{:S(2)}, u32[]{:S(2)}) collective-permute-start(bf16[128,2048]{1,0:T(8,128)(2,1)S(1)} %get-tuple-element.90), channel_id=1, source_target_pairs={{0,128},{1,33},{2,130},{3,35},{4,132},{5,37},{6,134},{7,39},{8,136... | collective-permute-start | bytes 1572872 | tf_op jit(solution)/shard_map/ppermute | solution.py:42
  74.6 3.7 %collective-permute-start.20 = (bf16[128,2048]{1,0:T(8,128)(2,1)S(1)}, bf16[128,2048]{1,0:T(8,128)(2,1)S(1)}, u32[]{:S(2)}, u32[]{:S(2)}) collective-permute-start(bf16[128,2048]{1,0:T(8,128)(2,1)S(1)} %collective-permute-done.16.refs_7_), channel_id=1, source_target_pairs={{0,14},{1,15},{2,0},{3,1},{4,2},{5,3},{6,4},{7,5},{8,6},{9,7},{10,... | collective-permute-start | bytes 1572872 | tf_op jit(solution)/shard_map/ppermute | solution.py:32
  78.6 9.4 %collective-permute-start.24 = (bf16[64,2048]{1,0:T(8,128)(2,1)S(1)}, bf16[64,2048]{1,0:T(8,128)(2,1)S(1)}, u32[]{:S(2)}, u32[]{:S(2)}) collective-permute-start(bf16[64,2048]{1,0:T(8,128)(2,1)S(1)} %get-tuple-element.94), channel_id=1, source_target_pairs={{0,64},{1,17},{2,66},{3,19},{4,68},{5,21},{6,70},{7,23},{8,72},{9,... | collective-permute-start | bytes 786440 | tf_op jit(solution)/shard_map/ppermute | solution.py:42
  89.0 5.7 %collective-permute-done.24.refs_3_ = bf16[64,2048]{1,0:T(8,128)(2,1)S(1)} collective-permute-done((bf16[64,2048]{1,0:T(8,128)(2,1)S(1)}, bf16[64,2048]{1,0:T(8,128)(2,1)S(1)}, u32[]{:S(2)}, u32[]{:S(2)}) %collective-permute-start.24) | collective-permute-done | bytes 262176 | tf_op jit(solution)/shard_map/ppermute | solution.py:42
  95.4 4.2 %collective-permute-start.27 = (bf16[256,2048]{1,0:T(8,128)(2,1)S(1)}, bf16[256,2048]{1,0:T(8,128)(2,1)S(1)}, u32[]{:S(2)}, u32[]{:S(2)}) collective-permute-start(bf16[256,2048]{1,0:T(8,128)(2,1)S(1)} %shard_map.64.refs_1_.refs_3_), channel_id=1, source_target_pairs={{0,16},{1,65},{2,18},{3,67},{4,20},{5,69},{6,22},{7,71},{8,24},{9,... | collective-permute-start | bytes 3145736 | tf_op jit(solution)/shard_map/ppermute | solution.py:42
  99.6 3.5 %collective-permute-start.25 = (bf16[64,2048]{1,0:T(8,128)(2,1)S(1)}, bf16[64,2048]{1,0:T(8,128)(2,1)S(1)}, u32[]{:S(2)}, u32[]{:S(2)}) collective-permute-start(bf16[64,2048]{1,0:T(8,128)(2,1)S(1)} %slice.16), channel_id=1, source_target_pairs={{0,14},{1,15},{2,0},{3,1},{4,2},{5,3},{6,4},{7,5},{8,6},{9,7},{10,... | collective-permute-start | bytes 786440 | tf_op jit(solution)/shard_map/ppermute | solution.py:32
  107.0 4.0 %collective-permute-done.26.refs_5_ = bf16[64,2048]{1,0:T(8,128)(2,1)S(1)} collective-permute-done((bf16[64,2048]{1,0:T(8,128)(2,1)S(1)}, bf16[64,2048]{1,0:T(8,128)(2,1)S(1)}, u32[]{:S(2)}, u32[]{:S(2)}) %collective-permute-start.26) | collective-permute-done | bytes 262176 | tf_op jit(solution)/shard_map/ppermute | solution.py:32
  118.2 2.9 %collective-permute-done.30 = bf16[128,1024]{1,0:T(8,128)(2,1)S(1)} collective-permute-done((bf16[128,1024]{1,0:T(8,128)(2,1)S(1)}, bf16[128,1024]{1,0:T(8,128)(2,1)S(1)}, u32[]{:S(2)}, u32[]{:S(2)}) %collective-permute-start.30) | collective-permute-done | bytes 262176 | tf_op jit(solution)/shard_map/ppermute | solution.py:42
  121.0 2.8 %collective-permute-done.31 = bf16[128,1024]{1,0:T(8,128)(2,1)S(1)} collective-permute-done((bf16[128,1024]{1,0:T(8,128)(2,1)S(1)}, bf16[128,1024]{1,0:T(8,128)(2,1)S(1)}, u32[]{:S(2)}, u32[]{:S(2)}) %collective-permute-start.31) | collective-permute-done | bytes 262176 | tf_op jit(solution)/shard_map/ppermute | solution.py:42
  136.3 6.5 %collective-permute-done.34.refs_4_.refs_6_ = bf16[128,2048]{1,0:T(8,128)(2,1)S(1)} collective-permute-done((bf16[128,2048]{1,0:T(8,128)(2,1)S(1)}, bf16[128,2048]{1,0:T(8,128)(2,1)S(1)}, u32[]{:S(2)}, u32[]{:S(2)}) %collective-permute-start.34) | collective-permute-done | bytes 524320 | tf_op jit(solution)/shard_map/ppermute | solution.py:42
  142.9 2.9 %shard_map.69 = (bf16[128,2048]{1,0:T(8,128)(2,1)}, bf16[128,2048]{1,0:T(8,128)(2,1)}, bf16[128,2048]{1,0:T(8,128)(2,1)}) custom-call(bf16[128,1024]{1,0:T(8,128)(2,1)S(1)} %collective-permute-done.35.refs_0_, bf16[128,1024]{1,0:T(8,128)(2,1)S(1)} %collective-permute-done.36.refs_1_, bf16[128,1024]{1,0:T(8,128)(2,1)S(1)} %collective-permute-done.37.refs_2_, ...), custom_call_target="tpu_custom_call" | custom-call | flops 1610612736 | bytes 5000000 | tf_op jit(solution)/shard_map/pallas_call | solution.py:279
  152.4 3.0 %collective-permute-done.38.refs_1_ = bf16[128,2048]{1,0:T(8,128)(2,1)} collective-permute-done((bf16[128,2048]{1,0:T(8,128)(2,1)}, bf16[128,2048]{1,0:T(8,128)(2,1)}, u32[]{:S(2)}, u32[]{:S(2)}) %collective-permute-start.38) | collective-permute-done | bytes 524320 | tf_op jit(solution)/shard_map/ppermute | solution.py:42
  157.6 5.5 %collective-permute-done.40.refs_3_ = bf16[128,2048]{1,0:T(8,128)(2,1)} collective-permute-done((bf16[128,2048]{1,0:T(8,128)(2,1)}, bf16[128,2048]{1,0:T(8,128)(2,1)}, u32[]{:S(2)}, u32[]{:S(2)}) %collective-permute-start.40) | collective-permute-done | bytes 524320 | tf_op jit(solution)/shard_map/ppermute | solution.py:42
  163.1 4.3 %shard_map.70 = bf16[128,8192]{1,0:T(8,128)(2,1)} custom-call(s32[4]{0:T(128)S(1)} %pad_add_fusion.place, bf16[128,2048]{1,0:T(8,128)(2,1)S(1)} %shard_map.68.refs_0_, bf16[128,2048]{1,0:T(8,128)(2,1)} %collective-permute-done.38.refs_1_, bf16[128,2048]{1,0:T(8,128)(2,1)} %collective-permute-done.39.refs_2_, bf16[128,2048]{1,0:T(8,128)(2,1)} %collective-permute-done.40.refs_3_), custom_call_target="tpu_custom_call" | custom-call | bytes 4000000 | tf_op jit(solution)/shard_map/pallas_call | solution.py:298
  (102 shorter events, 58.5 us)
Async XLA Ops:
  4.3 13.1 %collective-permute-start = (bf16[8,2048]{1,0:T(8,128)(2,1)S(1)}, bf16[8,2048]{1,0:T(8,128)(2,1)S(1)}, u32[]{:S(2)}, u32[]{:S(2)}) collective-permute-start(bf16[8,2048]{1,0:T(8,128)(2,1)S(1)} %get-tuple-element.61), channel_id=1, source_target_pairs={{0,192},{1,49},{2,194},{3,51},{4,196},{5,53},{6,198},{7,55},{8,200... | collective-permute-start | bytes 98312 | tf_op jit(solution)/shard_map/ppermute | solution.py:42
  5.4 12.0 %collective-permute-start.1 = (bf16[8,2048]{1,0:T(8,128)(2,1)S(1)}, bf16[8,2048]{1,0:T(8,128)(2,1)S(1)}, u32[]{:S(2)}, u32[]{:S(2)}) collective-permute-start(bf16[8,2048]{1,0:T(8,128)(2,1)S(1)} %get-tuple-element.62), channel_id=1, source_target_pairs={{0,128},{1,33},{2,130},{3,35},{4,132},{5,37},{6,134},{7,39},{8,136... | collective-permute-start | bytes 98312 | tf_op jit(solution)/shard_map/ppermute | solution.py:42
  6.2 11.2 %collective-permute-start.2 = (bf16[8,2048]{1,0:T(8,128)(2,1)S(1)}, bf16[8,2048]{1,0:T(8,128)(2,1)S(1)}, u32[]{:S(2)}, u32[]{:S(2)}) collective-permute-start(bf16[8,2048]{1,0:T(8,128)(2,1)S(1)} %get-tuple-element.63), channel_id=1, source_target_pairs={{0,64},{1,17},{2,66},{3,19},{4,68},{5,21},{6,70},{7,23},{8,72},{9,... | collective-permute-start | bytes 98312 | tf_op jit(solution)/shard_map/ppermute | solution.py:42
  22.2 34.5 %collective-permute-start.12 = (bf16[128,2048]{1,0:T(8,128)(2,1)S(1)}, bf16[128,2048]{1,0:T(8,128)(2,1)S(1)}, u32[]{:S(2)}, u32[]{:S(2)}) collective-permute-start(bf16[128,2048]{1,0:T(8,128)(2,1)S(1)} %get-tuple-element.77), channel_id=1, source_target_pairs={{0,64},{1,17},{2,66},{3,19},{4,68},{5,21},{6,70},{7,23},{8,72},{9,... | collective-permute-start | bytes 1572872 | tf_op jit(solution)/shard_map/ppermute | solution.py:42
  30.9 25.8 %collective-permute-start.8 = (bf16[128,2048]{1,0:T(8,128)(2,1)S(1)}, bf16[128,2048]{1,0:T(8,128)(2,1)S(1)}, u32[]{:S(2)}, u32[]{:S(2)}) collective-permute-start(bf16[128,2048]{1,0:T(8,128)(2,1)S(1)} %shard_map.62.refs_4_), channel_id=1, source_target_pairs={{0,2},{1,3},{2,4},{3,5},{4,6},{5,7},{6,8},{7,9},{8,10},{9,11},{10,... | collective-permute-start | bytes 1572872 | tf_op jit(solution)/shard_map/ppermute | solution.py:32
  31.0 25.7 %collective-permute-start.9 = (bf16[128,2048]{1,0:T(8,128)(2,1)S(1)}, bf16[128,2048]{1,0:T(8,128)(2,1)S(1)}, u32[]{:S(2)}, u32[]{:S(2)}) collective-permute-start(bf16[128,2048]{1,0:T(8,128)(2,1)S(1)} %shard_map.62.refs_4_), channel_id=1, source_target_pairs={{0,14},{1,15},{2,0},{3,1},{4,2},{5,3},{6,4},{7,5},{8,6},{9,7},{10,... | collective-permute-start | bytes 1572872 | tf_op jit(solution)/shard_map/ppermute | solution.py:32
  34.2 11.1 %collective-permute-start.10 = (bf16[8,8192]{1,0:T(8,128)(2,1)S(1)}, bf16[8,8192]{1,0:T(8,128)(2,1)S(1)}, u32[]{:S(2)}, u32[]{:S(2)}) collective-permute-start(bf16[8,8192]{1,0:T(8,128)(2,1)S(1)} %collective-permute-done.7.refs_1_), channel_id=1, source_target_pairs={{0,14},{1,15},{2,0},{3,1},{4,2},{5,3},{6,4},{7,5},{8,6},{9,7},{10,... | collective-permute-start | bytes 393224 | tf_op jit(solution)/shard_map/ppermute | solution.py:32
  35.0 14.1 %collective-permute-start.13 = (bf16[8,8192]{1,0:T(8,128)(2,1)S(1)}, bf16[8,8192]{1,0:T(8,128)(2,1)S(1)}, u32[]{:S(2)}, u32[]{:S(2)}) collective-permute-start(bf16[8,8192]{1,0:T(8,128)(2,1)S(1)} %collective-permute-done.6.refs_7_), channel_id=1, source_target_pairs={{0,2},{1,3},{2,4},{3,5},{4,6},{5,7},{6,8},{7,9},{8,10},{9,11},{10,... | collective-permute-start | bytes 393224 | tf_op jit(solution)/shard_map/ppermute | solution.py:32
  51.9 18.9 %collective-permute-start.17 = (bf16[128,2048]{1,0:T(8,128)(2,1)S(1)}, bf16[128,2048]{1,0:T(8,128)(2,1)S(1)}, u32[]{:S(2)}, u32[]{:S(2)}) collective-permute-start(bf16[128,2048]{1,0:T(8,128)(2,1)S(1)} %get-tuple-element.82), channel_id=1, source_target_pairs={{0,192},{1,49},{2,194},{3,51},{4,196},{5,53},{6,198},{7,55},{8,200... | collective-permute-start | bytes 1572872 | tf_op jit(solution)/shard_map/ppermute | solution.py:42
  56.7 14.1 %collective-permute-start.15 = (bf16[128,2048]{1,0:T(8,128)(2,1)S(1)}, bf16[128,2048]{1,0:T(8,128)(2,1)S(1)}, u32[]{:S(2)}, u32[]{:S(2)}) collective-permute-start(bf16[128,2048]{1,0:T(8,128)(2,1)S(1)} %collective-permute-done.8.refs_6_), channel_id=1, source_target_pairs={{0,2},{1,3},{2,4},{3,5},{4,6},{5,7},{6,8},{7,9},{8,10},{9,11},{10,... | collective-permute-start | bytes 1572872 | tf_op jit(solution)/shard_map/ppermute | solution.py:32
  56.8 14.1 %collective-permute-start.16 = (bf16[128,2048]{1,0:T(8,128)(2,1)S(1)}, bf16[128,2048]{1,0:T(8,128)(2,1)S(1)}, u32[]{:S(2)}, u32[]{:S(2)}) collective-permute-start(bf16[128,2048]{1,0:T(8,128)(2,1)S(1)} %collective-permute-done.9.refs_5_), channel_id=1, source_target_pairs={{0,14},{1,15},{2,0},{3,1},{4,2},{5,3},{6,4},{7,5},{8,6},{9,7},{10,... | collective-permute-start | bytes 1572872 | tf_op jit(solution)/shard_map/ppermute | solution.py:32
  71.3 24.1 %collective-permute-start.21 = (bf16[128,2048]{1,0:T(8,128)(2,1)S(1)}, bf16[128,2048]{1,0:T(8,128)(2,1)S(1)}, u32[]{:S(2)}, u32[]{:S(2)}) collective-permute-start(bf16[128,2048]{1,0:T(8,128)(2,1)S(1)} %get-tuple-element.90), channel_id=1, source_target_pairs={{0,128},{1,33},{2,130},{3,35},{4,132},{5,37},{6,134},{7,39},{8,136... | collective-permute-start | bytes 1572872 | tf_op jit(solution)/shard_map/ppermute | solution.py:42
  74.6 20.8 %collective-permute-start.19 = (bf16[128,2048]{1,0:T(8,128)(2,1)S(1)}, bf16[128,2048]{1,0:T(8,128)(2,1)S(1)}, u32[]{:S(2)}, u32[]{:S(2)}) collective-permute-start(bf16[128,2048]{1,0:T(8,128)(2,1)S(1)} %collective-permute-done.15.refs_8_), channel_id=1, source_target_pairs={{0,2},{1,3},{2,4},{3,5},{4,6},{5,7},{6,8},{7,9},{8,10},{9,11},{10,... | collective-permute-start | bytes 1572872 | tf_op jit(solution)/shard_map/ppermute | solution.py:32
  74.6 20.8 %collective-permute-start.20 = (bf16[128,2048]{1,0:T(8,128)(2,1)S(1)}, bf16[128,2048]{1,0:T(8,128)(2,1)S(1)}, u32[]{:S(2)}, u32[]{:S(2)}) collective-permute-start(bf16[128,2048]{1,0:T(8,128)(2,1)S(1)} %collective-permute-done.16.refs_7_), channel_id=1, source_target_pairs={{0,14},{1,15},{2,0},{3,1},{4,2},{5,3},{6,4},{7,5},{8,6},{9,7},{10,... | collective-permute-start | bytes 1572872 | tf_op jit(solution)/shard_map/ppermute | solution.py:32
  78.6 16.2 %collective-permute-start.24 = (bf16[64,2048]{1,0:T(8,128)(2,1)S(1)}, bf16[64,2048]{1,0:T(8,128)(2,1)S(1)}, u32[]{:S(2)}, u32[]{:S(2)}) collective-permute-start(bf16[64,2048]{1,0:T(8,128)(2,1)S(1)} %get-tuple-element.94), channel_id=1, source_target_pairs={{0,64},{1,17},{2,66},{3,19},{4,68},{5,21},{6,70},{7,23},{8,72},{9,... | collective-permute-start | bytes 786440 | tf_op jit(solution)/shard_map/ppermute | solution.py:42
  95.4 28.4 %collective-permute-start.27 = (bf16[256,2048]{1,0:T(8,128)(2,1)S(1)}, bf16[256,2048]{1,0:T(8,128)(2,1)S(1)}, u32[]{:S(2)}, u32[]{:S(2)}) collective-permute-start(bf16[256,2048]{1,0:T(8,128)(2,1)S(1)} %shard_map.64.refs_1_.refs_3_), channel_id=1, source_target_pairs={{0,16},{1,65},{2,18},{3,67},{4,20},{5,69},{6,22},{7,71},{8,24},{9,... | collective-permute-start | bytes 3145736 | tf_op jit(solution)/shard_map/ppermute | solution.py:42
  99.6 24.2 %collective-permute-start.28 = (bf16[256,2048]{1,0:T(8,128)(2,1)S(1)}, bf16[256,2048]{1,0:T(8,128)(2,1)S(1)}, u32[]{:S(2)}, u32[]{:S(2)}) collective-permute-start(bf16[256,2048]{1,0:T(8,128)(2,1)S(1)} %shard_map.64.refs_1_.refs_3_), channel_id=1, source_target_pairs={{0,48},{1,193},{2,50},{3,195},{4,52},{5,197},{6,54},{7,199},{8,56}... | collective-permute-start | bytes 3145736 | tf_op jit(solution)/shard_map/ppermute | solution.py:42
  124.8 11.5 %collective-permute-start.33 = (bf16[128,2048]{1,0:T(8,128)(2,1)S(1)}, bf16[128,2048]{1,0:T(8,128)(2,1)S(1)}, u32[]{:S(2)}, u32[]{:S(2)}) collective-permute-start(bf16[128,2048]{1,0:T(8,128)(2,1)S(1)} %slice.18), channel_id=1, source_target_pairs={{0,48},{1,193},{2,50},{3,195},{4,52},{5,197},{6,54},{7,199},{8,56}... | collective-permute-start | bytes 1572872 | tf_op jit(solution)/shard_map/ppermute | solution.py:42
  126.8 16.1 %collective-permute-start.34 = (bf16[128,2048]{1,0:T(8,128)(2,1)S(1)}, bf16[128,2048]{1,0:T(8,128)(2,1)S(1)}, u32[]{:S(2)}, u32[]{:S(2)}) collective-permute-start(bf16[128,2048]{1,0:T(8,128)(2,1)S(1)} %slice.19), channel_id=1, source_target_pairs={{0,16},{1,65},{2,18},{3,67},{4,20},{5,69},{6,22},{7,71},{8,24},{9,... | collective-permute-start | bytes 1572872 | tf_op jit(solution)/shard_map/ppermute | solution.py:42
  129.1 13.7 %collective-permute-start.35 = (bf16[128,1024]{1,0:T(8,128)(2,1)S(1)}, bf16[128,1024]{1,0:T(8,128)(2,1)S(1)}, u32[]{:S(2)}, u32[]{:S(2)}) collective-permute-start(bf16[128,1024]{1,0:T(8,128)(2,1)S(1)} %get-tuple-element.110.refs_0_), channel_id=1, source_target_pairs={{0,64},{1,17},{2,66},{3,19},{4,68},{5,21},{6,70},{7,23},{8,72},{9,... | collective-permute-start | bytes 786440 | tf_op jit(solution)/shard_map/ppermute | solution.py:42
  130.4 12.5 %collective-permute-start.36 = (bf16[128,1024]{1,0:T(8,128)(2,1)S(1)}, bf16[128,1024]{1,0:T(8,128)(2,1)S(1)}, u32[]{:S(2)}, u32[]{:S(2)}) collective-permute-start(bf16[128,1024]{1,0:T(8,128)(2,1)S(1)} %get-tuple-element.110.refs_0_), channel_id=1, source_target_pairs={{0,128},{1,33},{2,130},{3,35},{4,132},{5,37},{6,134},{7,39},{8,136... | collective-permute-start | bytes 786440 | tf_op jit(solution)/shard_map/ppermute | solution.py:42
  131.3 11.6 %collective-permute-start.37 = (bf16[128,1024]{1,0:T(8,128)(2,1)S(1)}, bf16[128,1024]{1,0:T(8,128)(2,1)S(1)}, u32[]{:S(2)}, u32[]{:S(2)}) collective-permute-start(bf16[128,1024]{1,0:T(8,128)(2,1)S(1)} %get-tuple-element.110.refs_0_), channel_id=1, source_target_pairs={{0,192},{1,49},{2,194},{3,51},{4,196},{5,53},{6,198},{7,55},{8,200... | collective-permute-start | bytes 786440 | tf_op jit(solution)/shard_map/ppermute | solution.py:42
  146.5 11.1 %collective-permute-start.39 = (bf16[128,2048]{1,0:T(8,128)(2,1)}, bf16[128,2048]{1,0:T(8,128)(2,1)}, u32[]{:S(2)}, u32[]{:S(2)}) collective-permute-start(bf16[128,2048]{1,0:T(8,128)(2,1)} %get-tuple-element.114), channel_id=1, source_target_pairs={{0,128},{1,33},{2,130},{3,35},{4,132},{5,37},{6,134},{7,39},{8,136... | collective-permute-start | bytes 1572872 | tf_op jit(solution)/shard_map/ppermute | solution.py:42
  146.9 16.2 %collective-permute-start.40 = (bf16[128,2048]{1,0:T(8,128)(2,1)}, bf16[128,2048]{1,0:T(8,128)(2,1)}, u32[]{:S(2)}, u32[]{:S(2)}) collective-permute-start(bf16[128,2048]{1,0:T(8,128)(2,1)} %get-tuple-element.115), channel_id=1, source_target_pairs={{0,64},{1,17},{2,66},{3,19},{4,68},{5,21},{6,70},{7,23},{8,72},{9,... | collective-permute-start | bytes 1572872 | tf_op jit(solution)/shard_map/ppermute | solution.py:42
  (27 other events, 174.0 us)

commit v4 on v3

v4 whole, which is shorter than its diff:
```python
import functools

import jax
import jax.numpy as jnp
from jax import lax
from jax.experimental import pallas as pl
from jax.experimental.pallas import tpu as pltpu
from jax.sharding import PartitionSpec as P

TB = 128
WD = 8
NX, NY, NZ = 4, 4, 8
AX = ("row", "col", "rep")
F32, BF = jnp.float32, jnp.bfloat16
ROWS = 128
HALF = 8192
PART = HALF // 4
QW = 1024
VMEM = pl.BlockSpec(memory_space=pltpu.VMEM)
PARAMS = pltpu.CompilerParams(vmem_limit_bytes=40 * 2**20)


def ident(x, y, z, c):
    return ((x % NX) * NY * NZ + (y % NY) * NZ + z % NZ) * 2 + c


def every():
    return [(x, y, z, c) for x in range(NX) for y in range(NY) for z in range(NZ) for c in (0, 1)]


def shift_z(value, step):
    return lax.ppermute(value, AX, [(ident(x, y, z, c), ident(x, y, z + step, c)) for x, y, z, c in every()])


def shift_plane(value, step, swapped):
    pairs = []
    for x, y, z, c in every():
        if (c == 0) != swapped:
            pairs.append((ident(x, y, z, c), ident(x + step, y, z, c)))
        else:
            pairs.append((ident(x, y, z, c), ident(x, y + step, z, c)))
    return lax.ppermute(value, AX, pairs)


def shift_g(value, step):
    return shift_plane(value, step, False)


def shift_p(value, step):
    return shift_plane(value, step, True)


def swap_core(value):
    return lax.ppermute(value, AX, [(ident(x, y, z, c), ident(x, y, z, 1 - c)) for x, y, z, c in every()])


def cost(flops, moved):
    return pl.CostEstimate(flops=flops, bytes_accessed=moved, transcendentals=0)


def shares_kernel(cyc_map, amp_map, cyc, amp, *refs):
    outs, rows, both, sem = refs[:4], refs[4], refs[5], refs[6]
    row, col, core = (lax.axis_index(a) for a in AX)
    g = jnp.where(core == 0, row, col // NZ)
    copy = pltpu.make_async_copy(amp.at[0:16, :], rows, sem)
    copy.start()
    tiles = HALF // TB
    half_map = cyc_map[pl.ds(pl.multiple_of(core * tiles, tiles), tiles), :].astype(F32)
    lane = lax.broadcasted_iota(jnp.int32, half_map.shape, 1)
    keep = jnp.sum(jnp.where(lane == row * NY * NZ + col, half_map, 0.0), axis=1, keepdims=True)
    keep_window = amp_map[...].astype(F32)
    copy.wait()
    for t in range(tiles):
        at = slice(t * TB, (t + 1) * TB)
        top = cyc[:, at].astype(F32) * keep[t : t + 1, :]
        low = rows[:WD, at].astype(F32) * keep_window[:, t : t + 1]
        both[:, at] = jnp.concatenate([top, low], 0).astype(BF)
    for d in range(4):
        share = pl.multiple_of(lax.rem(g + d, 4) * PART, PART)
        outs[d][...] = both[:, pl.ds(share, PART)]


def small_shares(cycle_map, amp_map, cyc, amplitudes):
    return pl.pallas_call(
        shares_kernel,
        out_shape=[jax.ShapeDtypeStruct((2 * WD, PART), BF)] * 4,
        in_specs=[VMEM] * 3 + [pl.BlockSpec(memory_space=pl.ANY)],
        out_specs=[VMEM] * 4,
        scratch_shapes=[
            pltpu.VMEM((16, HALF), BF),
            pltpu.VMEM((16, HALF), BF),
            pltpu.SemaphoreType.DMA,
        ],
        compiler_params=pltpu.CompilerParams(vmem_limit_bytes=60 * 2**20),
        cost_estimate=cost(0, 600_000),
    )(cycle_map, amp_map, cyc, amplitudes)


def group_kernel(place, *refs):
    pieces, outs = refs[:4], refs[4:]
    rows = 8 * WD
    here = lax.broadcasted_iota(jnp.int32, (rows, rows), 1)
    there = lax.broadcasted_iota(jnp.int32, (rows, rows), 0)
    member = jnp.where(here // 8 % 2 == 0, (here // 16 + place[0]) % 4, 4 + here // 16)
    order = (member * 8 + here % 8 == there).astype(F32).astype(BF)
    value = jnp.concatenate([ref[...] for ref in pieces], 0)
    value = jnp.dot(order, value, preferred_element_type=F32).astype(BF)
    outs[0][...] = value[: rows // 2]
    outs[1][...] = value[rows // 2 :]


def group_order(place, pieces):
    return pl.pallas_call(
        group_kernel,
        out_shape=[jax.ShapeDtypeStruct((4 * WD, PART), BF)] * 2,
        grid_spec=pltpu.PrefetchScalarGridSpec(
            num_scalar_prefetch=1, grid=(), in_specs=[VMEM] * 4, out_specs=[VMEM] * 2
        ),
        compiler_params=PARAMS,
        cost_estimate=cost(2 * 64 * 64 * PART, 600_000),
    )(place, *pieces)


def stack_kernel(*refs):
    refs[-1][...] = jnp.concatenate([ref[...] for ref in refs[:-1]], 0)


def stack(pieces):
    return pl.pallas_call(
        stack_kernel,
        out_shape=jax.ShapeDtypeStruct((sum(piece.shape[0] for piece in pieces), PART), BF),
        in_specs=[VMEM] * len(pieces),
        out_specs=VMEM,
        compiler_params=PARAMS,
        cost_estimate=cost(0, 2_000_000),
    )(*pieces)


def plane_kernel(place, *refs):
    pieces, out = refs[:4], refs[4]
    rows = 16 * WD
    here = lax.broadcasted_iota(jnp.int32, (rows, rows), 1)
    there = lax.broadcasted_iota(jnp.int32, (rows, rows), 0)
    hp, hg, hw = (here // 32 + place[1]) % 4, (here // 8 + place[0]) % 4, here % 8
    first = place[2] == 0
    at = jnp.where(first, hg * 32 + hp * 8, hp * 32 + hg * 8) + hw
    order = (at == there).astype(F32).astype(BF)
    value = jnp.concatenate([ref[...] for ref in pieces], 0)
    out[...] = jnp.dot(order, value, preferred_element_type=F32).astype(BF)


def plane_order(place, pieces):
    return pl.pallas_call(
        plane_kernel,
        out_shape=jax.ShapeDtypeStruct((16 * WD, PART), BF),
        grid_spec=pltpu.PrefetchScalarGridSpec(
            num_scalar_prefetch=1, grid=(), in_specs=[VMEM] * 4, out_specs=VMEM
        ),
        compiler_params=PARAMS,
        cost_estimate=cost(2 * 128 * 128 * PART, 1_000_000),
    )(place, *pieces)


def amp_kernel(place, amp_map, *refs):
    ins, outs = refs[:4], refs[4:]
    for d in range(4):
        share = lax.rem(place[0] + d, 4)
        for t in range(PART // TB):
            keep = amp_map[0, share * 16 + t].astype(BF)
            outs[d][:, t * TB : (t + 1) * TB] = ins[d][:, t * TB : (t + 1) * TB] * keep


def amp_shares(place, amp_map, amplitudes):
    block = 32

    def source(d):
        return pl.BlockSpec((block, PART), lambda i, place, amp_map: (i, lax.rem(place[0] + d, 4)))

    return pl.pallas_call(
        amp_kernel,
        out_shape=[jax.ShapeDtypeStruct((ROWS, PART), BF)] * 4,
        grid_spec=pltpu.PrefetchScalarGridSpec(
            num_scalar_prefetch=2,
            grid=(ROWS // block,),
            in_specs=[source(d) for d in range(4)],
            out_specs=[pl.BlockSpec((block, PART), lambda i, place, amp_map: (i, 0))] * 4,
        ),
        compiler_params=PARAMS,
        cost_estimate=cost(0, 4_000_000),
    )(place, amp_map, *[amplitudes] * 4)


def dressed_kernel(count, *refs):
    blocks, cyc = refs[:4], refs[4 : 4 + count]
    away, own = refs[-2:]
    left = jnp.concatenate([blocks[d][...] for d in (1, 2, 3, 0)], 0)
    for at in range(count):
        value = lax.dot_general(left, cyc[at][...], (((1,), (1,)), ((), ())), preferred_element_type=F32)
        where = slice(at * 256, at * 256 + 256)
        away[:, where] = value[: 3 * ROWS].astype(BF)
        own[:, where] = value[3 * ROWS :]


def dressed_first(blocks, cyc):
    return pl.pallas_call(
        functools.partial(dressed_kernel, len(cyc)),
        out_shape=[jax.ShapeDtypeStruct((3 * ROWS, QW), BF), jax.ShapeDtypeStruct((ROWS, QW), F32)],
        in_specs=[VMEM] * (4 + len(cyc)),
        out_specs=[VMEM] * 2,
        compiler_params=PARAMS,
        cost_estimate=cost(2 * 512 * PART * 768, 8_000_000),
    )(*blocks, *cyc)


def dressed_last_kernel(*refs):
    blocks, halves, away_in, own_in = refs[:4], refs[4:6], refs[6], refs[7]
    outs, own = refs[8:11], refs[11]
    edge = 3 * 256
    left = jnp.concatenate([blocks[d][...] for d in (1, 2, 3, 0)], 0)
    right = jnp.concatenate([ref[...] for ref in halves], 0)
    value = lax.dot_general(left, right, (((1,), (1,)), ((), ())), preferred_element_type=F32)
    for d in range(3):
        rows = slice(d * ROWS, (d + 1) * ROWS)
        outs[d][:, :edge] = away_in[rows, :edge]
        outs[d][:, edge:] = value[rows].astype(BF)
    own[:, :edge] = own_in[:, :edge]
    own[:, edge:] = value[3 * ROWS :]


def dressed_last(blocks, halves, away, own):
    return pl.pallas_call(
        dressed_last_kernel,
        out_shape=[jax.ShapeDtypeStruct((ROWS, QW), BF)] * 3 + [jax.ShapeDtypeStruct((ROWS, QW), F32)],
        in_specs=[VMEM] * 8,
        out_specs=[VMEM] * 4,
        compiler_params=PARAMS,
        cost_estimate=cost(2 * 512 * PART * 256, 5_000_000),
    )(*blocks, *halves, away, own)


def sum_kernel(own, one, two, three, order, out):
    value = own[...] + one[...].astype(F32) + two[...].astype(F32) + three[...].astype(F32)
    high = value.astype(BF)
    rest = value - high.astype(F32)
    middle = rest.astype(BF)
    low = (rest - middle.astype(F32)).astype(BF)
    moved = jnp.dot(jnp.concatenate([high, middle, low], 0), order[...], preferred_element_type=F32)
    out[...] = moved[:ROWS] + moved[ROWS : 2 * ROWS] + moved[2 * ROWS :]


def group_sum(own, back, order):
    return pl.pallas_call(
        sum_kernel,
        out_shape=jax.ShapeDtypeStruct((ROWS, QW), F32),
        in_specs=[VMEM] * 5,
        out_specs=VMEM,
        compiler_params=PARAMS,
        cost_estimate=cost(6 * ROWS * QW * QW, 4_000_000),
    )(own, *back, order)


def quadratic_kernel(count, *refs):
    lefts, rights, outs = refs[:count], refs[count : count + 9], refs[count + 9 :]
    left = jnp.concatenate([ref[...] for ref in lefts], 0)
    wide = 512
    for n in range(0, PART, wide):
        right = jnp.concatenate([ref[:, n : n + wide] for ref in rights], 0)
        value = jnp.dot(left, right, preferred_element_type=F32).astype(BF)
        for d in range(count):
            outs[d][:, n : n + wide] = value[d * ROWS : (d + 1) * ROWS]


def quadratic_blocks(lefts, rights):
    count = len(lefts)
    return pl.pallas_call(
        functools.partial(quadratic_kernel, count),
        out_shape=[jax.ShapeDtypeStruct((ROWS, PART), BF)] * count,
        in_specs=[VMEM] * (count + 9),
        out_specs=[VMEM] * count,
        compiler_params=PARAMS,
        cost_estimate=cost(2 * count * ROWS * QW * PART, 5_000_000),
    )(*lefts, *rights)


def place_kernel(place, *refs):
    ins, out, sem = refs[:4], refs[4], refs[5]
    copies = []
    for d in range(4):
        at = pl.multiple_of(lax.rem(place[0] + d, 4) * PART, PART)
        for i in range(4):
            rows = slice(i * 32, i * 32 + 32)
            copies.append(
                pltpu.make_async_copy(ins[d].at[rows, :], out.at[rows, pl.ds(at, PART)], sem.at[d * 4 + i])
            )
    for copy in copies:
        copy.start()
    for copy in copies:
        copy.wait()


def place_blocks(place, blocks):
    return pl.pallas_call(
        place_kernel,
        out_shape=jax.ShapeDtypeStruct((ROWS, HALF), BF),
        grid_spec=pltpu.PrefetchScalarGridSpec(
            num_scalar_prefetch=1,
            grid=(),
            in_specs=[VMEM] * 4,
            out_specs=pl.BlockSpec(memory_space=pl.ANY),
            scratch_shapes=[pltpu.SemaphoreType.DMA((16,))],
        ),
        compiler_params=PARAMS,
        cost_estimate=cost(0, 4_000_000),
    )(place, *blocks)


def after(values, *others):
    count = len(values)
    return lax.optimization_barrier(tuple(values) + others)[:count]


def body(amplitudes, cycle_integrals, amp_map, cycle_map):
    row, col, core = (lax.axis_index(a) for a in AX)
    x, y, z = row, col // NZ, col % NZ
    g = jnp.where(core == 0, x, y)
    p = jnp.where(core == 0, y, x)
    place = jnp.stack([g, p, core, row * NY * NZ + col]).astype(jnp.int32)

    shares = small_shares(cycle_map, amp_map, cycle_integrals.T, amplitudes)
    shares = [shares[0]] + [shift_g(shares[4 - d], -d) for d in (1, 2, 3)]
    cyc, win = group_order(place, shares)

    cf, cb = shift_z(cyc, 1), shift_z(cyc, -1)
    window = [win] + [shift_p(win, -e) for e in (1, 2, 3)]
    cf2, cb2 = shift_z(cf, 1), shift_z(cb, -1)
    [amplitudes] = after([amplitudes], cyc)
    mine, *sends = amp_shares(place, amp_map, amplitudes)
    sends = after(sends, cf2, cb2, *window[1:])
    blocks = [mine] + [shift_g(sends[d - 1], d) for d in (1, 2, 3)]
    cf3, cb3 = shift_z(cf2, 1), shift_z(cb2, -1)
    half = cyc.shape[0] // 2
    far = [shift_z(cb3[:half], -1), shift_z(cf3[half:], 1)]
    win = plane_order(place, after(window, *far))
    cyc = stack([cyc, cb, cb2, cb3, *far, cf3, cf2, cf])
    [cyc] = after([cyc], *blocks)

    cf, cb = shift_p(cyc, 1), shift_p(cyc, -1)
    wf, wb = shift_z(win, 1), shift_z(win, -1)
    half = cyc.shape[0] // 2
    far = [shift_p(cb[:half], -1), shift_p(cf[half:], 1)]

    here = lax.broadcasted_iota(jnp.int32, (QW, 1), 0)
    turn, hg = here // 256, here // 8 % 4
    hp = (p + jnp.where(turn == 2, 3, jnp.where(turn == 3, 2, turn))) % 4
    at = jnp.where(core == 0, hg * 32 + hp * 8, hp * 32 + hg * 8)
    there = lax.broadcasted_iota(jnp.int32, (1, QW), 1)
    order = (here // 32 % 8 * 128 + at + here % 8 == there).astype(BF)
    there = lax.broadcasted_iota(jnp.int32, (1, QW // 2), 1) + core * (QW // 2)
    final = (here // 8 % 16 * 64 + (z + here // 128) % NZ * 8 + here % 8 == there).astype(BF)

    away, own = dressed_first(blocks, [cyc, cb, cf])
    wf, wb = after([wf, wb], own)
    wf2, wb2 = shift_z(wf, 1), shift_z(wb, -1)
    *away, own = dressed_last(blocks, far, away, own)
    back = [shift_g(away[d - 1], -d) for d in (1, 2, 3)]
    wf2, wb2 = after([wf2, wb2], back[0])
    wf3, wb3 = shift_z(wf2, 1), shift_z(wb2, -1)
    total = group_sum(own, back, order)
    inner = (total + swap_core(total)).astype(BF)
    inners = [shift_g(inner, d) for d in (1, 2, 3)]
    wf3, wb3 = after([wf3, wb3], inners[0])
    half = win.shape[0] // 2
    far = [shift_z(wb3[:half], -1), shift_z(wf3[half:], 1)]
    rights = [win, wb, wb2, wb3, *far, wf3, wf2, wf]
    dressed = jnp.dot(inner, final, preferred_element_type=F32).astype(BF)

    outs = quadratic_blocks(inners, rights)
    outs = [shift_g(outs[d - 1], -d) for d in (1, 2, 3)]
    outs = list(quadratic_blocks([inner], rights)) + outs
    return (dressed, place_blocks(place, outs))


def solution(mesh):
    placed = (P(("row", "col"), "rep"), P("rep", ("row", "col")), P(("row", "col"), "rep"), P())
    return jax.shard_map(
        body,
        mesh=mesh,
        in_specs=placed,
        out_specs=(P(("row", "col"), "rep"), P(("row", "col"), "rep")),
        check_vma=False,
    )
```

time: 169 us -> 148 us (0.88)
  waiting for transfers between devices: 70.9 us -> 62.2 us
  starting transfers between devices: 67.9 us -> 60.4 us
  local copies, waits for them, and re-layouts: 6.42 us -> 3.92 us
    ppermute x25 -> x22, starting transfers between devices: 42 us -> 30.5 us  [shift_plane(): return lax.ppermute(value, AX, pairs)]
    ppermute x15 -> x16, waiting for transfers between devices: 30.3 us -> 23.7 us  [shift_z(): lax.ppermute(value, AX, [(ident(x, y, z, c), ident(x, y, z + step, c)) fo...]
    ppermute x15 -> x16, starting transfers between devices: 25.9 us -> 29.8 us  [shift_z(): lax.ppermute(value, AX, [(ident(x, y, z, c), ident(x, y, z + step, c)) fo...]
    unnamed x20 -> x18, local copies, waits for them, and re-layouts: 6.3 us -> 3.8 us
    ppermute x25 -> x22, waiting for transfers between devices: 40.6 us -> 38.5 us  [shift_plane(): return lax.ppermute(value, AX, pairs)]
    pallas_call x6 -> x5, Pallas kernels: 7.14 us -> 6.61 us  [the longest x1 2.99 us: small_shares(): pl.pallas_call(shares_kernel, out_shape=[jax.ShapeDtypeStruct((2 * WD, PA...]
  transfers between devices with their start and end apart: 41 -> 39, of which waited for: 19 -> 19; matrix products, arithmetic and copies ran while one was open for 1% -> 1% of each run, Pallas kernels for 6% -> 5%
where the time goes in v4:
time: 148 us; the launch traced here: 146 us
  waiting for transfers between devices  62.2 us (42%)
  starting transfers between devices  60.4 us (41%)
  Pallas kernels  17 us (11%)
  local copies, waits for them, and re-layouts  3.92 us (3%)
    ppermute x22, waiting for transfers between devices, shift_plane(): return lax.ppermute(value, AX, pairs)  38.5 us
    ppermute x22, starting transfers between devices, shift_plane(): return lax.ppermute(value, AX, pairs)  30.5 us
    ppermute x16, starting transfers between devices, shift_z(): lax.ppermute(value, AX, [(ident(x, y, z, c), ident(x, y, z + step, c)) fo...  29.8 us
    ppermute x16, waiting for transfers between devices, shift_z(): lax.ppermute(value, AX, [(ident(x, y, z, c), ident(x, y, z + step, c)) fo...  23.7 us
    unnamed x18, local copies, waits for them, and re-layouts  3.8 us
    pallas_call x2, Pallas kernels, quadratic_blocks(): pl.pallas_call(functools.partial(quadratic_kernel, count), out_shape=[jax...  3.62 us
    pallas_call x1, Pallas kernels, place_blocks(): pl.pallas_call(place_kernel, out_shape=jax.ShapeDtypeStruct((ROWS, HALF),...  3.33 us
    pallas_call x1, Pallas kernels, small_shares(): pl.pallas_call(shares_kernel, out_shape=[jax.ShapeDtypeStruct((2 * WD, PA...  2.99 us
  transfers between devices with their start and end apart: 39, of which 19 were waited for; matrix products, arithmetic and copies ran while one was open for 1% of the time, Pallas kernels for 5%

profile of v4, /device:TPU:0, one launch (start us, length us, event | category | flops | bytes accessed | tf_op | source)
XLA Modules:
  0.0 146.4 jit_solution(7533789517553646002)
XLA Ops:
  0.7 3.0 %shard_map.59 = (bf16[16,2048]{1,0:T(8,128)(2,1)}, bf16[16,2048]{1,0:T(8,128)(2,1)}, bf16[16,2048]{1,0:T(8,128)(2,1)}, bf16[16,2048]{1,0:T(8,128)(2,1)}) custom-call(s32[128,128]{1,0:T(8,128)} %cyc_map.1, s32[1,64]{1,0:T(1,128)} %amp_map.3, bf16[8,8192]{1,0:T(8,128)(2,1)} %bitcast.6, bf16[128,8192]{1,0:T(8,128)(2,1)} %refs_3_), custom_call_target="tpu_custom_call" | custom-call | bytes 600000 | tf_op jit(solution)/shard_map/pallas_call | solution.py:84
  15.0 4.0 %collective-permute-start.5 = (bf16[32,2048]{1,0:T(8,128)(2,1)S(1)}, bf16[32,2048]{1,0:T(8,128)(2,1)S(1)}, u32[]{:S(2)}, u32[]{:S(2)}) collective-permute-start(bf16[32,2048]{1,0:T(8,128)(2,1)S(1)} %get-tuple-element.40.refs_0_), channel_id=1, source_target_pairs={{0,14},{1,15},{2,0},{3,1},{4,2},{5,3},{6,4},{7,5},{8,6},{9,7},{10,... | collective-permute-start | bytes 393224 | tf_op jit(solution)/shard_map/ppermute | solution.py:32
  19.1 3.0 %collective-permute-start.7 = (bf16[32,2048]{1,0:T(8,128)(2,1)S(1)}, bf16[32,2048]{1,0:T(8,128)(2,1)S(1)}, u32[]{:S(2)}, u32[]{:S(2)}) collective-permute-start(bf16[32,2048]{1,0:T(8,128)(2,1)S(1)} %get-tuple-element.57.refs_0_), channel_id=1, source_target_pairs={{0,48},{1,193},{2,50},{3,195},{4,52},{5,197},{6,54},{7,199},{8,56}... | collective-permute-start | bytes 393224 | tf_op jit(solution)/shard_map/ppermute | solution.py:42
  23.7 3.2 %collective-permute-start.6 = (bf16[32,2048]{1,0:T(8,128)(2,1)S(1)}, bf16[32,2048]{1,0:T(8,128)(2,1)S(1)}, u32[]{:S(2)}, u32[]{:S(2)}) collective-permute-start(bf16[32,2048]{1,0:T(8,128)(2,1)S(1)} %collective-permute-done.5.refs_1_), channel_id=1, source_target_pairs={{0,14},{1,15},{2,0},{3,1},{4,2},{5,3},{6,4},{7,5},{8,6},{9,7},{10,... | collective-permute-start | bytes 393224 | tf_op jit(solution)/shard_map/ppermute | solution.py:32
  33.9 3.1 %collective-permute-start.13 = (bf16[32,2048]{1,0:T(8,128)(2,1)S(1)}, bf16[32,2048]{1,0:T(8,128)(2,1)S(1)}, u32[]{:S(2)}, u32[]{:S(2)}) collective-permute-start(bf16[32,2048]{1,0:T(8,128)(2,1)S(1)} %collective-permute-done.6.refs_2_), channel_id=1, source_target_pairs={{0,14},{1,15},{2,0},{3,1},{4,2},{5,3},{6,4},{7,5},{8,6},{9,7},{10,... | collective-permute-start | bytes 393224 | tf_op jit(solution)/shard_map/ppermute | solution.py:32
  39.6 3.7 %collective-permute-start.14 = (bf16[16,2048]{1,0:T(8,128)(2,1)S(1)}, bf16[16,2048]{1,0:T(8,128)(2,1)S(1)}, u32[]{:S(2)}, u32[]{:S(2)}) collective-permute-start(bf16[16,2048]{1,0:T(8,128)(2,1)S(1)} %slice.24), channel_id=1, source_target_pairs={{0,14},{1,15},{2,0},{3,1},{4,2},{5,3},{6,4},{7,5},{8,6},{9,7},{10,... | collective-permute-start | bytes 196616 | tf_op jit(solution)/shard_map/ppermute | solution.py:32
  45.2 3.7 %collective-permute-done.16.refs_5_ = bf16[16,2048]{1,0:T(8,128)(2,1)S(1)} collective-permute-done((bf16[16,2048]{1,0:T(8,128)(2,1)S(1)}, bf16[16,2048]{1,0:T(8,128)(2,1)S(1)}, u32[]{:S(2)}, u32[]{:S(2)}) %collective-permute-start.16) | collective-permute-done | bytes 65568 | tf_op jit(solution)/shard_map/ppermute | solution.py:32
  51.4 12.8 %collective-permute-done.17.refs_5_ = bf16[256,2048]{1,0:T(8,128)(2,1)S(1)} collective-permute-done((bf16[256,2048]{1,0:T(8,128)(2,1)S(1)}, bf16[256,2048]{1,0:T(8,128)(2,1)S(1)}, u32[]{:S(2)}, u32[]{:S(2)}) %collective-permute-start.17) | collective-permute-done | bytes 1048608 | tf_op jit(solution)/shard_map/ppermute | solution.py:42
  64.2 3.2 %collective-permute-start.18 = (bf16[128,2048]{1,0:T(8,128)(2,1)S(1)}, bf16[128,2048]{1,0:T(8,128)(2,1)S(1)}, u32[]{:S(2)}, u32[]{:S(2)}) collective-permute-start(bf16[128,2048]{1,0:T(8,128)(2,1)S(1)} %slice.26), channel_id=1, source_target_pairs={{0,48},{1,193},{2,50},{3,195},{4,52},{5,197},{6,54},{7,199},{8,56}... | collective-permute-start | bytes 1572872 | tf_op jit(solution)/shard_map/ppermute | solution.py:42
  68.4 3.2 %collective-permute-start.26 = (bf16[128,2048]{1,0:T(8,128)(2,1)S(1)}, bf16[128,2048]{1,0:T(8,128)(2,1)S(1)}, u32[]{:S(2)}, u32[]{:S(2)}) collective-permute-start(bf16[128,2048]{1,0:T(8,128)(2,1)S(1)} %shard_map.66.refs_1_.refs_3_), channel_id=1, source_target_pairs={{0,14},{1,15},{2,0},{3,1},{4,2},{5,3},{6,4},{7,5},{8,6},{9,7},{10,... | collective-permute-start | bytes 1572872 | tf_op jit(solution)/shard_map/ppermute | solution.py:32
  74.6 6.6 %collective-permute-done.20.refs_5_ = bf16[128,2048]{1,0:T(8,128)(2,1)S(1)} collective-permute-done((bf16[128,2048]{1,0:T(8,128)(2,1)S(1)}, bf16[128,2048]{1,0:T(8,128)(2,1)S(1)}, u32[]{:S(2)}, u32[]{:S(2)}) %collective-permute-start.20) | collective-permute-done | bytes 524320 | tf_op jit(solution)/shard_map/ppermute | solution.py:42
  84.1 2.6 %collective-permute-start.22 = (bf16[128,1024]{1,0:T(8,128)(2,1)S(1)}, bf16[128,1024]{1,0:T(8,128)(2,1)S(1)}, u32[]{:S(2)}, u32[]{:S(2)}) collective-permute-start(bf16[128,1024]{1,0:T(8,128)(2,1)S(1)} %get-tuple-element.55), channel_id=1, source_target_pairs={{0,128},{1,33},{2,130},{3,35},{4,132},{5,37},{6,134},{7,39},{8,136... | collective-permute-start | bytes 786440 | tf_op jit(solution)/shard_map/ppermute | solution.py:42
  88.5 3.2 %collective-permute-start.28 = (bf16[128,2048]{1,0:T(8,128)(2,1)S(1)}, bf16[128,2048]{1,0:T(8,128)(2,1)S(1)}, u32[]{:S(2)}, u32[]{:S(2)}) collective-permute-start(bf16[128,2048]{1,0:T(8,128)(2,1)S(1)} %collective-permute-done.26.refs_2_.refs_4_), channel_id=1, source_target_pairs={{0,14},{1,15},{2,0},{3,1},{4,2},{5,3},{6,4},{7,5},{8,6},{9,7},{10,... | collective-permute-start | bytes 1572872 | tf_op jit(solution)/shard_map/ppermute | solution.py:32
  92.0 2.8 %collective-permute-done.23.three = bf16[128,1024]{1,0:T(8,128)(2,1)S(1)} collective-permute-done((bf16[128,1024]{1,0:T(8,128)(2,1)S(1)}, bf16[128,1024]{1,0:T(8,128)(2,1)S(1)}, u32[]{:S(2)}, u32[]{:S(2)}) %collective-permute-start.23) | collective-permute-done | bytes 262176 | tf_op jit(solution)/shard_map/ppermute | solution.py:42
  95.8 3.0 %collective-permute-done.27.refs_8_.refs_10_ = bf16[128,2048]{1,0:T(8,128)(2,1)S(1)} collective-permute-done((bf16[128,2048]{1,0:T(8,128)(2,1)S(1)}, bf16[128,2048]{1,0:T(8,128)(2,1)S(1)}, u32[]{:S(2)}, u32[]{:S(2)}) %collective-permute-start.27) | collective-permute-done | bytes 524320 | tf_op jit(solution)/shard_map/ppermute | solution.py:32
  102.4 3.4 %collective-permute-start.34 = (bf16[128,1024]{1,0:T(8,128)(2,1)S(1)}, bf16[128,1024]{1,0:T(8,128)(2,1)S(1)}, u32[]{:S(2)}, u32[]{:S(2)}) collective-permute-start(bf16[128,1024]{1,0:T(8,128)(2,1)S(1)} %add_convert_fusion.refs_0_), channel_id=1, source_target_pairs={{0,128},{1,33},{2,130},{3,35},{4,132},{5,37},{6,134},{7,39},{8,136... | collective-permute-start | bytes 786440 | tf_op jit(solution)/shard_map/ppermute | solution.py:42
  105.8 5.7 %collective-permute-done.29.refs_7_.refs_9_ = bf16[128,2048]{1,0:T(8,128)(2,1)S(1)} collective-permute-done((bf16[128,2048]{1,0:T(8,128)(2,1)S(1)}, bf16[128,2048]{1,0:T(8,128)(2,1)S(1)}, u32[]{:S(2)}, u32[]{:S(2)}) %collective-permute-start.29) | collective-permute-done | bytes 524320 | tf_op jit(solution)/shard_map/ppermute | solution.py:32
  111.5 3.1 %collective-permute-start.32 = (bf16[64,2048]{1,0:T(8,128)(2,1)S(1)}, bf16[64,2048]{1,0:T(8,128)(2,1)S(1)}, u32[]{:S(2)}, u32[]{:S(2)}) collective-permute-start(bf16[64,2048]{1,0:T(8,128)(2,1)S(1)} %slice.22), channel_id=1, source_target_pairs={{0,14},{1,15},{2,0},{3,1},{4,2},{5,3},{6,4},{7,5},{8,6},{9,7},{10,... | collective-permute-start | bytes 786440 | tf_op jit(solution)/shard_map/ppermute | solution.py:32
  115.3 4.2 %collective-permute-done.32.refs_5_.refs_7_ = bf16[64,2048]{1,0:T(8,128)(2,1)S(1)} collective-permute-done((bf16[64,2048]{1,0:T(8,128)(2,1)S(1)}, bf16[64,2048]{1,0:T(8,128)(2,1)S(1)}, u32[]{:S(2)}, u32[]{:S(2)}) %collective-permute-start.32) | collective-permute-done | bytes 262176 | tf_op jit(solution)/shard_map/ppermute | solution.py:32
  119.5 2.7 %collective-permute-done.33.refs_6_.refs_8_ = bf16[64,2048]{1,0:T(8,128)(2,1)S(1)} collective-permute-done((bf16[64,2048]{1,0:T(8,128)(2,1)S(1)}, bf16[64,2048]{1,0:T(8,128)(2,1)S(1)}, u32[]{:S(2)}, u32[]{:S(2)}) %collective-permute-start.33) | collective-permute-done | bytes 262176 | tf_op jit(solution)/shard_map/ppermute | solution.py:32
  122.2 2.9 %shard_map.68 = (bf16[128,2048]{1,0:T(8,128)(2,1)}, bf16[128,2048]{1,0:T(8,128)(2,1)}, bf16[128,2048]{1,0:T(8,128)(2,1)}) custom-call(bf16[128,1024]{1,0:T(8,128)(2,1)S(1)} %collective-permute-done.31.refs_0_, bf16[128,1024]{1,0:T(8,128)(2,1)S(1)} %collective-permute-done.34.refs_1_, bf16[128,1024]{1,0:T(8,128)(2,1)S(1)} %collective-permute-done.35.refs_2_, ...), custom_call_target="tpu_custom_call" | custom-call | flops 1610612736 | bytes 5000000 | tf_op jit(solution)/shard_map/pallas_call | solution.py:275
  134.7 2.6 %collective-permute-done.37.refs_2_ = bf16[128,2048]{1,0:T(8,128)(2,1)} collective-permute-done((bf16[128,2048]{1,0:T(8,128)(2,1)}, bf16[128,2048]{1,0:T(8,128)(2,1)}, u32[]{:S(2)}, u32[]{:S(2)}) %collective-permute-start.37) | collective-permute-done | bytes 524320 | tf_op jit(solution)/shard_map/ppermute | solution.py:42
  137.4 5.5 %collective-permute-done.38.refs_3_ = bf16[128,2048]{1,0:T(8,128)(2,1)} collective-permute-done((bf16[128,2048]{1,0:T(8,128)(2,1)}, bf16[128,2048]{1,0:T(8,128)(2,1)}, u32[]{:S(2)}, u32[]{:S(2)}) %collective-permute-start.38) | collective-permute-done | bytes 524320 | tf_op jit(solution)/shard_map/ppermute | solution.py:42
  142.9 3.3 %shard_map.69 = bf16[128,8192]{1,0:T(8,128)(2,1)} custom-call(s32[4]{0:T(128)S(1)} %pad_add_fusion.place, bf16[128,2048]{1,0:T(8,128)(2,1)S(1)} %shard_map.67.refs_0_, bf16[128,2048]{1,0:T(8,128)(2,1)} %collective-permute-done.36.refs_1_, bf16[128,2048]{1,0:T(8,128)(2,1)} %collective-permute-done.37.refs_2_, bf16[128,2048]{1,0:T(8,128)(2,1)} %collective-permute-done.38.refs_3_), custom_call_target="tpu_custom_call" | custom-call | bytes 4000000 | tf_op jit(solution)/shard_map/pallas_call | solution.py:302
  (96 shorter events, 50.7 us)
Async XLA Ops:
  13.0 10.6 %collective-permute-start.3 = (bf16[32,2048]{1,0:T(8,128)(2,1)S(1)}, bf16[32,2048]{1,0:T(8,128)(2,1)S(1)}, u32[]{:S(2)}, u32[]{:S(2)}) collective-permute-start(bf16[32,2048]{1,0:T(8,128)(2,1)S(1)} %get-tuple-element.40.refs_0_), channel_id=1, source_target_pairs={{0,2},{1,3},{2,4},{3,5},{4,6},{5,7},{6,8},{7,9},{8,10},{9,11},{10,... | collective-permute-start | bytes 393224 | tf_op jit(solution)/shard_map/ppermute | solution.py:32
  15.0 8.6 %collective-permute-start.5 = (bf16[32,2048]{1,0:T(8,128)(2,1)S(1)}, bf16[32,2048]{1,0:T(8,128)(2,1)S(1)}, u32[]{:S(2)}, u32[]{:S(2)}) collective-permute-start(bf16[32,2048]{1,0:T(8,128)(2,1)S(1)} %get-tuple-element.40.refs_0_), channel_id=1, source_target_pairs={{0,14},{1,15},{2,0},{3,1},{4,2},{5,3},{6,4},{7,5},{8,6},{9,7},{10,... | collective-permute-start | bytes 393224 | tf_op jit(solution)/shard_map/ppermute | solution.py:32
  19.1 9.8 %collective-permute-start.7 = (bf16[32,2048]{1,0:T(8,128)(2,1)S(1)}, bf16[32,2048]{1,0:T(8,128)(2,1)S(1)}, u32[]{:S(2)}, u32[]{:S(2)}) collective-permute-start(bf16[32,2048]{1,0:T(8,128)(2,1)S(1)} %get-tuple-element.57.refs_0_), channel_id=1, source_target_pairs={{0,48},{1,193},{2,50},{3,195},{4,52},{5,197},{6,54},{7,199},{8,56}... | collective-permute-start | bytes 393224 | tf_op jit(solution)/shard_map/ppermute | solution.py:42
  30.0 19.0 %collective-permute-start.10 = (bf16[128,2048]{1,0:T(8,128)(2,1)S(1)}, bf16[128,2048]{1,0:T(8,128)(2,1)S(1)}, u32[]{:S(2)}, u32[]{:S(2)}) collective-permute-start(bf16[128,2048]{1,0:T(8,128)(2,1)S(1)} %get-tuple-element.47), channel_id=1, source_target_pairs={{0,64},{1,17},{2,66},{3,19},{4,68},{5,21},{6,70},{7,23},{8,72},{9,... | collective-permute-start | bytes 1572872 | tf_op jit(solution)/shard_map/ppermute | solution.py:42
  30.0 19.0 %collective-permute-start.11 = (bf16[128,2048]{1,0:T(8,128)(2,1)S(1)}, bf16[128,2048]{1,0:T(8,128)(2,1)S(1)}, u32[]{:S(2)}, u32[]{:S(2)}) collective-permute-start(bf16[128,2048]{1,0:T(8,128)(2,1)S(1)} %get-tuple-element.48), channel_id=1, source_target_pairs={{0,128},{1,33},{2,130},{3,35},{4,132},{5,37},{6,134},{7,39},{8,136... | collective-permute-start | bytes 1572872 | tf_op jit(solution)/shard_map/ppermute | solution.py:42
  32.0 16.9 %collective-permute-start.12 = (bf16[128,2048]{1,0:T(8,128)(2,1)S(1)}, bf16[128,2048]{1,0:T(8,128)(2,1)S(1)}, u32[]{:S(2)}, u32[]{:S(2)}) collective-permute-start(bf16[128,2048]{1,0:T(8,128)(2,1)S(1)} %get-tuple-element.49), channel_id=1, source_target_pairs={{0,192},{1,49},{2,194},{3,51},{4,196},{5,53},{6,198},{7,55},{8,200... | collective-permute-start | bytes 1572872 | tf_op jit(solution)/shard_map/ppermute | solution.py:42
  48.9 15.2 %collective-permute-start.17 = (bf16[256,2048]{1,0:T(8,128)(2,1)S(1)}, bf16[256,2048]{1,0:T(8,128)(2,1)S(1)}, u32[]{:S(2)}, u32[]{:S(2)}) collective-permute-start(bf16[256,2048]{1,0:T(8,128)(2,1)S(1)} %shard_map.62.refs_4_), channel_id=1, source_target_pairs={{0,48},{1,193},{2,50},{3,195},{4,52},{5,197},{6,54},{7,199},{8,56}... | collective-permute-start | bytes 3145736 | tf_op jit(solution)/shard_map/ppermute | solution.py:42
  51.2 16.1 %collective-permute-start.19 = (bf16[256,2048]{1,0:T(8,128)(2,1)S(1)}, bf16[256,2048]{1,0:T(8,128)(2,1)S(1)}, u32[]{:S(2)}, u32[]{:S(2)}) collective-permute-start(bf16[256,2048]{1,0:T(8,128)(2,1)S(1)} %shard_map.62.refs_4_), channel_id=1, source_target_pairs={{0,16},{1,65},{2,18},{3,67},{4,20},{5,69},{6,22},{7,71},{8,24},{9,... | collective-permute-start | bytes 3145736 | tf_op jit(solution)/shard_map/ppermute | solution.py:42
  64.2 10.4 %collective-permute-start.18 = (bf16[128,2048]{1,0:T(8,128)(2,1)S(1)}, bf16[128,2048]{1,0:T(8,128)(2,1)S(1)}, u32[]{:S(2)}, u32[]{:S(2)}) collective-permute-start(bf16[128,2048]{1,0:T(8,128)(2,1)S(1)} %slice.26), channel_id=1, source_target_pairs={{0,48},{1,193},{2,50},{3,195},{4,52},{5,197},{6,54},{7,199},{8,56}... | collective-permute-start | bytes 1572872 | tf_op jit(solution)/shard_map/ppermute | solution.py:42
  67.4 13.8 %collective-permute-start.20 = (bf16[128,2048]{1,0:T(8,128)(2,1)S(1)}, bf16[128,2048]{1,0:T(8,128)(2,1)S(1)}, u32[]{:S(2)}, u32[]{:S(2)}) collective-permute-start(bf16[128,2048]{1,0:T(8,128)(2,1)S(1)} %slice.27), channel_id=1, source_target_pairs={{0,16},{1,65},{2,18},{3,67},{4,20},{5,69},{6,22},{7,71},{8,24},{9,... | collective-permute-start | bytes 1572872 | tf_op jit(solution)/shard_map/ppermute | solution.py:42
  68.3 20.0 %collective-permute-start.25 = (bf16[128,2048]{1,0:T(8,128)(2,1)S(1)}, bf16[128,2048]{1,0:T(8,128)(2,1)S(1)}, u32[]{:S(2)}, u32[]{:S(2)}) collective-permute-start(bf16[128,2048]{1,0:T(8,128)(2,1)S(1)} %shard_map.66.refs_1_.refs_3_), channel_id=1, source_target_pairs={{0,2},{1,3},{2,4},{3,5},{4,6},{5,7},{6,8},{7,9},{8,10},{9,11},{10,... | collective-permute-start | bytes 1572872 | tf_op jit(solution)/shard_map/ppermute | solution.py:32
  68.4 20.0 %collective-permute-start.26 = (bf16[128,2048]{1,0:T(8,128)(2,1)S(1)}, bf16[128,2048]{1,0:T(8,128)(2,1)S(1)}, u32[]{:S(2)}, u32[]{:S(2)}) collective-permute-start(bf16[128,2048]{1,0:T(8,128)(2,1)S(1)} %shard_map.66.refs_1_.refs_3_), channel_id=1, source_target_pairs={{0,14},{1,15},{2,0},{3,1},{4,2},{5,3},{6,4},{7,5},{8,6},{9,7},{10,... | collective-permute-start | bytes 1572872 | tf_op jit(solution)/shard_map/ppermute | solution.py:32
  82.0 9.7 %collective-permute-start.21 = (bf16[128,1024]{1,0:T(8,128)(2,1)S(1)}, bf16[128,1024]{1,0:T(8,128)(2,1)S(1)}, u32[]{:S(2)}, u32[]{:S(2)}) collective-permute-start(bf16[128,1024]{1,0:T(8,128)(2,1)S(1)} %get-tuple-element.54), channel_id=1, source_target_pairs={{0,192},{1,49},{2,194},{3,51},{4,196},{5,53},{6,198},{7,55},{8,200... | collective-permute-start | bytes 786440 | tf_op jit(solution)/shard_map/ppermute | solution.py:42
  86.7 8.1 %collective-permute-start.23 = (bf16[128,1024]{1,0:T(8,128)(2,1)S(1)}, bf16[128,1024]{1,0:T(8,128)(2,1)S(1)}, u32[]{:S(2)}, u32[]{:S(2)}) collective-permute-start(bf16[128,1024]{1,0:T(8,128)(2,1)S(1)} %get-tuple-element.56), channel_id=1, source_target_pairs={{0,64},{1,17},{2,66},{3,19},{4,68},{5,21},{6,70},{7,23},{8,72},{9,... | collective-permute-start | bytes 786440 | tf_op jit(solution)/shard_map/ppermute | solution.py:42
  88.4 10.5 %collective-permute-start.27 = (bf16[128,2048]{1,0:T(8,128)(2,1)S(1)}, bf16[128,2048]{1,0:T(8,128)(2,1)S(1)}, u32[]{:S(2)}, u32[]{:S(2)}) collective-permute-start(bf16[128,2048]{1,0:T(8,128)(2,1)S(1)} %collective-permute-done.25.refs_9_.refs_11_), channel_id=1, source_target_pairs={{0,2},{1,3},{2,4},{3,5},{4,6},{5,7},{6,8},{7,9},{8,10},{9,11},{10,... | collective-permute-start | bytes 1572872 | tf_op jit(solution)/shard_map/ppermute | solution.py:32
  88.5 10.4 %collective-permute-start.28 = (bf16[128,2048]{1,0:T(8,128)(2,1)S(1)}, bf16[128,2048]{1,0:T(8,128)(2,1)S(1)}, u32[]{:S(2)}, u32[]{:S(2)}) collective-permute-start(bf16[128,2048]{1,0:T(8,128)(2,1)S(1)} %collective-permute-done.26.refs_2_.refs_4_), channel_id=1, source_target_pairs={{0,14},{1,15},{2,0},{3,1},{4,2},{5,3},{6,4},{7,5},{8,6},{9,7},{10,... | collective-permute-start | bytes 1572872 | tf_op jit(solution)/shard_map/ppermute | solution.py:32
  98.9 12.6 %collective-permute-start.29 = (bf16[128,2048]{1,0:T(8,128)(2,1)S(1)}, bf16[128,2048]{1,0:T(8,128)(2,1)S(1)}, u32[]{:S(2)}, u32[]{:S(2)}) collective-permute-start(bf16[128,2048]{1,0:T(8,128)(2,1)S(1)} %collective-permute-done.27.refs_8_.refs_10_), channel_id=1, source_target_pairs={{0,2},{1,3},{2,4},{3,5},{4,6},{5,7},{6,8},{7,9},{8,10},{9,11},{10,... | collective-permute-start | bytes 1572872 | tf_op jit(solution)/shard_map/ppermute | solution.py:32
  99.7 11.8 %collective-permute-start.30 = (bf16[128,2048]{1,0:T(8,128)(2,1)S(1)}, bf16[128,2048]{1,0:T(8,128)(2,1)S(1)}, u32[]{:S(2)}, u32[]{:S(2)}) collective-permute-start(bf16[128,2048]{1,0:T(8,128)(2,1)S(1)} %collective-permute-done.28.refs_3_.refs_5_), channel_id=1, source_target_pairs={{0,14},{1,15},{2,0},{3,1},{4,2},{5,3},{6,4},{7,5},{8,6},{9,7},{10,... | collective-permute-start | bytes 1572872 | tf_op jit(solution)/shard_map/ppermute | solution.py:32
  102.2 9.3 %collective-permute-start.31 = (bf16[128,1024]{1,0:T(8,128)(2,1)S(1)}, bf16[128,1024]{1,0:T(8,128)(2,1)S(1)}, u32[]{:S(2)}, u32[]{:S(2)}) collective-permute-start(bf16[128,1024]{1,0:T(8,128)(2,1)S(1)} %add_convert_fusion.refs_0_), channel_id=1, source_target_pairs={{0,64},{1,17},{2,66},{3,19},{4,68},{5,21},{6,70},{7,23},{8,72},{9,... | collective-permute-start | bytes 786440 | tf_op jit(solution)/shard_map/ppermute | solution.py:42
  102.4 12.9 %collective-permute-start.34 = (bf16[128,1024]{1,0:T(8,128)(2,1)S(1)}, bf16[128,1024]{1,0:T(8,128)(2,1)S(1)}, u32[]{:S(2)}, u32[]{:S(2)}) collective-permute-start(bf16[128,1024]{1,0:T(8,128)(2,1)S(1)} %add_convert_fusion.refs_0_), channel_id=1, source_target_pairs={{0,128},{1,33},{2,130},{3,35},{4,132},{5,37},{6,134},{7,39},{8,136... | collective-permute-start | bytes 786440 | tf_op jit(solution)/shard_map/ppermute | solution.py:42
  105.8 9.5 %collective-permute-start.35 = (bf16[128,1024]{1,0:T(8,128)(2,1)S(1)}, bf16[128,1024]{1,0:T(8,128)(2,1)S(1)}, u32[]{:S(2)}, u32[]{:S(2)}) collective-permute-start(bf16[128,1024]{1,0:T(8,128)(2,1)S(1)} %add_convert_fusion.refs_0_), channel_id=1, source_target_pairs={{0,192},{1,49},{2,194},{3,51},{4,196},{5,53},{6,198},{7,55},{8,200... | collective-permute-start | bytes 786440 | tf_op jit(solution)/shard_map/ppermute | solution.py:42
  125.1 9.6 %collective-permute-start.36 = (bf16[128,2048]{1,0:T(8,128)(2,1)}, bf16[128,2048]{1,0:T(8,128)(2,1)}, u32[]{:S(2)}, u32[]{:S(2)}) collective-permute-start(bf16[128,2048]{1,0:T(8,128)(2,1)} %get-tuple-element.67), channel_id=1, source_target_pairs={{0,192},{1,49},{2,194},{3,51},{4,196},{5,53},{6,198},{7,55},{8,200... | collective-permute-start | bytes 1572872 | tf_op jit(solution)/shard_map/ppermute | solution.py:42
  126.3 11.1 %collective-permute-start.37 = (bf16[128,2048]{1,0:T(8,128)(2,1)}, bf16[128,2048]{1,0:T(8,128)(2,1)}, u32[]{:S(2)}, u32[]{:S(2)}) collective-permute-start(bf16[128,2048]{1,0:T(8,128)(2,1)} %get-tuple-element.68), channel_id=1, source_target_pairs={{0,128},{1,33},{2,130},{3,35},{4,132},{5,37},{6,134},{7,39},{8,136... | collective-permute-start | bytes 1572872 | tf_op jit(solution)/shard_map/ppermute | solution.py:42
  128.4 14.5 %collective-permute-start.38 = (bf16[128,2048]{1,0:T(8,128)(2,1)}, bf16[128,2048]{1,0:T(8,128)(2,1)}, u32[]{:S(2)}, u32[]{:S(2)}) collective-permute-start(bf16[128,2048]{1,0:T(8,128)(2,1)} %get-tuple-element.69), channel_id=1, source_target_pairs={{0,64},{1,17},{2,66},{3,19},{4,68},{5,21},{6,70},{7,23},{8,72},{9,... | collective-permute-start | bytes 1572872 | tf_op jit(solution)/shard_map/ppermute | solution.py:42
  (24 other events, 187.2 us)

commit v5 on v4

--- a/solution.py
+++ b/solution.py
@@ -17,7 +17,7 @@
 PART = HALF // 4
 QW = 1024
 VMEM = pl.BlockSpec(memory_space=pltpu.VMEM)
-PARAMS = pltpu.CompilerParams(vmem_limit_bytes=40 * 2**20)
+PARAMS = pltpu.CompilerParams(vmem_limit_bytes=24 * 2**20)
 
 
 def ident(x, y, z, c):
@@ -97,68 +97,48 @@
 
 
 def group_kernel(place, *refs):
-    pieces, outs = refs[:4], refs[4:]
+    pieces, out = refs[:4], refs[4]
     rows = 8 * WD
     here = lax.broadcasted_iota(jnp.int32, (rows, rows), 1)
     there = lax.broadcasted_iota(jnp.int32, (rows, rows), 0)
-    member = jnp.where(here // 8 % 2 == 0, (here // 16 + place[0]) % 4, 4 + here // 16)
-    order = (member * 8 + here % 8 == there).astype(F32).astype(BF)
-    value = jnp.concatenate([ref[...] for ref in pieces], 0)
-    value = jnp.dot(order, value, preferred_element_type=F32).astype(BF)
-    outs[0][...] = value[: rows // 2]
-    outs[1][...] = value[rows // 2 :]
-
-
-def group_order(place, pieces):
-    return pl.pallas_call(
-        group_kernel,
-        out_shape=[jax.ShapeDtypeStruct((4 * WD, PART), BF)] * 2,
-        grid_spec=pltpu.PrefetchScalarGridSpec(
-            num_scalar_prefetch=1, grid=(), in_specs=[VMEM] * 4, out_specs=[VMEM] * 2
-        ),
-        compiler_params=PARAMS,
-        cost_estimate=cost(2 * 64 * 64 * PART, 600_000),
-    )(place, *pieces)
-
-
-def stack_kernel(*refs):
-    refs[-1][...] = jnp.concatenate([ref[...] for ref in refs[:-1]], 0)
-
-
-def stack(pieces):
-    return pl.pallas_call(
-        stack_kernel,
-        out_shape=jax.ShapeDtypeStruct((sum(piece.shape[0] for piece in pieces), PART), BF),
-        in_specs=[VMEM] * len(pieces),
-        out_specs=VMEM,
-        compiler_params=PARAMS,
-        cost_estimate=cost(0, 2_000_000),
-    )(*pieces)
-
-
-def plane_kernel(place, *refs):
-    pieces, out = refs[:4], refs[4]
-    rows = 16 * WD
-    here = lax.broadcasted_iota(jnp.int32, (rows, rows), 1)
-    there = lax.broadcasted_iota(jnp.int32, (rows, rows), 0)
-    hp, hg, hw = (here // 32 + place[1]) % 4, (here // 8 + place[0]) % 4, here % 8
-    first = place[2] == 0
-    at = jnp.where(first, hg * 32 + hp * 8, hp * 32 + hg * 8) + hw
+    member = (here // 16 + place[0]) % 4
+    at = member // 2 * 32 + here // 8 % 2 * 16 + member % 2 * 8 + here % 8
     order = (at == there).astype(F32).astype(BF)
     value = jnp.concatenate([ref[...] for ref in pieces], 0)
     out[...] = jnp.dot(order, value, preferred_element_type=F32).astype(BF)
 
 
-def plane_order(place, pieces):
-    return pl.pallas_call(
-        plane_kernel,
-        out_shape=jax.ShapeDtypeStruct((16 * WD, PART), BF),
+def group_order(place, pieces):
+    return pl.pallas_call(
+        group_kernel,
+        out_shape=jax.ShapeDtypeStruct((8 * WD, PART), BF),
         grid_spec=pltpu.PrefetchScalarGridSpec(
             num_scalar_prefetch=1, grid=(), in_specs=[VMEM] * 4, out_specs=VMEM
         ),
         compiler_params=PARAMS,
-        cost_estimate=cost(2 * 128 * 128 * PART, 1_000_000),
+        cost_estimate=cost(2 * 64 * 64 * PART, 600_000),
     )(place, *pieces)
+
+
+def part_kernel(*refs):
+    pieces, outs = refs[:9], refs[9:]
+    at = 0
+    for ref in pieces:
+        for rows in range(0, ref.shape[0], 32):
+            outs[0][at : at + 16, :] = ref[rows : rows + 16, :]
+            outs[1][at : at + 16, :] = ref[rows + 16 : rows + 32, :]
+            at += 16
+
+
+def part(pieces):
+    return pl.pallas_call(
+        part_kernel,
+        out_shape=[jax.ShapeDtypeStruct((32 * WD, PART), BF)] * 2,
+        in_specs=[VMEM] * 9,
+        out_specs=[VMEM] * 2,
+        compiler_params=PARAMS,
+        cost_estimate=cost(0, 4_000_000),
+    )(*pieces)
 
 
 def amp_kernel(place, amp_map, *refs):
@@ -238,29 +218,30 @@
     )(*blocks, *halves, away, own)
 
 
-def sum_kernel(own, one, two, three, order, out):
-    value = own[...] + one[...].astype(F32) + two[...].astype(F32) + three[...].astype(F32)
+def inner_kernel(mine, other, order, out):
+    value = other[...]
     high = value.astype(BF)
     rest = value - high.astype(F32)
     middle = rest.astype(BF)
     low = (rest - middle.astype(F32)).astype(BF)
     moved = jnp.dot(jnp.concatenate([high, middle, low], 0), order[...], preferred_element_type=F32)
-    out[...] = moved[:ROWS] + moved[ROWS : 2 * ROWS] + moved[2 * ROWS :]
-
-
-def group_sum(own, back, order):
-    return pl.pallas_call(
-        sum_kernel,
-        out_shape=jax.ShapeDtypeStruct((ROWS, QW), F32),
-        in_specs=[VMEM] * 5,
+    moved = moved[:ROWS] + moved[ROWS : 2 * ROWS] + moved[2 * ROWS :]
+    out[...] = (mine[...] + moved).astype(BF)
+
+
+def inner_call(mine, other, order):
+    return pl.pallas_call(
+        inner_kernel,
+        out_shape=jax.ShapeDtypeStruct((ROWS, QW), BF),
+        in_specs=[VMEM] * 3,
         out_specs=VMEM,
         compiler_params=PARAMS,
         cost_estimate=cost(6 * ROWS * QW * QW, 4_000_000),
-    )(own, *back, order)
+    )(mine, other, order)
 
 
 def quadratic_kernel(count, *refs):
-    lefts, rights, outs = refs[:count], refs[count : count + 9], refs[count + 9 :]
+    lefts, rights, outs = refs[:count], refs[count : count + 5], refs[count + 5 :]
     left = jnp.concatenate([ref[...] for ref in lefts], 0)
     wide = 512
     for n in range(0, PART, wide):
@@ -275,7 +256,7 @@
     return pl.pallas_call(
         functools.partial(quadratic_kernel, count),
         out_shape=[jax.ShapeDtypeStruct((ROWS, PART), BF)] * count,
-        in_specs=[VMEM] * (count + 9),
+        in_specs=[VMEM] * (count + 5),
         out_specs=[VMEM] * count,
         compiler_params=PARAMS,
         cost_estimate=cost(2 * count * ROWS * QW * PART, 5_000_000),
@@ -327,51 +308,48 @@
     place = jnp.stack([g, p, core, row * NY * NZ + col]).astype(jnp.int32)
 
     shares = small_shares(cycle_map, amp_map, cycle_integrals.T, amplitudes)
+    [amplitudes] = after([amplitudes], shares[0])
     shares = [shares[0]] + [shift_g(shares[4 - d], -d) for d in (1, 2, 3)]
-    cyc, win = group_order(place, shares)
-
-    cf, cb = shift_z(cyc, 1), shift_z(cyc, -1)
-    window = [win] + [shift_p(win, -e) for e in (1, 2, 3)]
-    cf2, cb2 = shift_z(cf, 1), shift_z(cb, -1)
-    [amplitudes] = after([amplitudes], cyc)
     mine, *sends = amp_shares(place, amp_map, amplitudes)
-    sends = after(sends, cf2, cb2, *window[1:])
+    both = group_order(place, after(shares, mine))
+
+    f, b = shift_z(both, 1), shift_z(both, -1)
+    f2, b2 = shift_z(f, 1), shift_z(b, -1)
+    sends[:2] = after(sends[:2], f)
+    f3, b3 = shift_z(f2, 1), shift_z(b2, -1)
+    sends[2:] = after(sends[2:], f2)
+    half = both.shape[0] // 2
+    far = [shift_z(b3[:half], -1), shift_z(f3[half:], 1)]
     blocks = [mine] + [shift_g(sends[d - 1], d) for d in (1, 2, 3)]
-    cf3, cb3 = shift_z(cf2, 1), shift_z(cb2, -1)
-    half = cyc.shape[0] // 2
-    far = [shift_z(cb3[:half], -1), shift_z(cf3[half:], 1)]
-    win = plane_order(place, after(window, *far))
-    cyc = stack([cyc, cb, cb2, cb3, *far, cf3, cf2, cf])
+    cyc, win = part([both, b, b2, b3, *far, f3, f2, f])
     [cyc] = after([cyc], *blocks)
 
     cf, cb = shift_p(cyc, 1), shift_p(cyc, -1)
-    wf, wb = shift_z(win, 1), shift_z(win, -1)
     half = cyc.shape[0] // 2
     far = [shift_p(cb[:half], -1), shift_p(cf[half:], 1)]
 
     here = lax.broadcasted_iota(jnp.int32, (QW, 1), 0)
-    turn, hg = here // 256, here // 8 % 4
-    hp = (p + jnp.where(turn == 2, 3, jnp.where(turn == 3, 2, turn))) % 4
-    at = jnp.where(core == 0, hg * 32 + hp * 8, hp * 32 + hg * 8)
+    turn, spot, hg, hw = here // 256, here // 32 % 8, here // 8 % 4, here % 8
+    turn = jnp.where(turn == 2, 3, jnp.where(turn == 3, 2, turn))
+    turn_here = (hg - p) % 4
+    turn_here = jnp.where(turn_here == 2, 3, jnp.where(turn_here == 3, 2, turn_here))
     there = lax.broadcasted_iota(jnp.int32, (1, QW), 1)
-    order = (here // 32 % 8 * 128 + at + here % 8 == there).astype(BF)
+    order = (turn_here * 256 + spot * 32 + (g + turn) % 4 * 8 + hw == there).astype(BF)
+    hp = (p + turn) % 4
+    hx, hy = jnp.where(core == 0, hg, hp), jnp.where(core == 0, hp, hg)
     there = lax.broadcasted_iota(jnp.int32, (1, QW // 2), 1) + core * (QW // 2)
-    final = (here // 8 % 16 * 64 + (z + here // 128) % NZ * 8 + here % 8 == there).astype(BF)
+    final = (hx * 256 + hy * 64 + (z + spot) % NZ * 8 + hw == there).astype(BF)
 
     away, own = dressed_first(blocks, [cyc, cb, cf])
-    wf, wb = after([wf, wb], own)
-    wf2, wb2 = shift_z(wf, 1), shift_z(wb, -1)
-    *away, own = dressed_last(blocks, far, away, own)
+    [win] = after([win], own)
+    wf, wb = shift_p(win, 1), shift_p(win, -1)
+    *away, total = dressed_last(blocks, far, away, own)
     back = [shift_g(away[d - 1], -d) for d in (1, 2, 3)]
-    wf2, wb2 = after([wf2, wb2], back[0])
-    wf3, wb3 = shift_z(wf2, 1), shift_z(wb2, -1)
-    total = group_sum(own, back, order)
-    inner = (total + swap_core(total)).astype(BF)
+    for value in back:
+        total = total + value.astype(F32)
+    inner = inner_call(total, swap_core(total), order)
     inners = [shift_g(inner, d) for d in (1, 2, 3)]
-    wf3, wb3 = after([wf3, wb3], inners[0])
-    half = win.shape[0] // 2
-    far = [shift_z(wb3[:half], -1), shift_z(wf3[half:], 1)]
-    rights = [win, wb, wb2, wb3, *far, wf3, wf2, wf]
+    rights = [win, wb, wf, shift_p(wb[:half], -1), shift_p(wf[half:], 1)]
     dressed = jnp.dot(inner, final, preferred_element_type=F32).astype(BF)
 
     outs = quadratic_blocks(inners, rights)

time: 148 us -> 142 us (0.959)
  starting transfers between devices: 60.4 us -> 48.3 us
  waiting for transfers between devices: 62.2 us -> 70.5 us
  local copies, waits for them, and re-layouts: 3.92 us -> 2.27 us
    ppermute x22 -> x23, waiting for transfers between devices: 38.5 us -> 53.9 us  [shift_plane(): return lax.ppermute(value, AX, pairs)]
    ppermute x16 -> x8, starting transfers between devices: 29.8 us -> 14.8 us  [shift_z(): lax.ppermute(value, AX, [(ident(x, y, z, c), ident(x, y, z + step, c)) fo...]
    ppermute x16 -> x8, waiting for transfers between devices: 23.7 us -> 16.6 us  [shift_z(): lax.ppermute(value, AX, [(ident(x, y, z, c), ident(x, y, z + step, c)) fo...]
    ppermute x22 -> x23, starting transfers between devices: 30.5 us -> 33.4 us  [shift_plane(): return lax.ppermute(value, AX, pairs)]
    unnamed x18 -> x14, local copies, waits for them, and re-layouts: 3.8 us -> 2.1 us
  transfers between devices with their start and end apart: 39 -> 32, of which waited for: 19 -> 18; matrix products, arithmetic and copies ran while one was open for 1% -> 1% of each run, Pallas kernels for 5% -> 5%
where the time goes in v5:
time: 142 us; the launch traced here: 140 us
  waiting for transfers between devices  70.5 us (50%)
  starting transfers between devices  48.3 us (34%)
  Pallas kernels  16.3 us (11%)
  local copies, waits for them, and re-layouts  2.27 us (2%)
    ppermute x23, waiting for transfers between devices, shift_plane(): return lax.ppermute(value, AX, pairs)  53.9 us
    ppermute x23, starting transfers between devices, shift_plane(): return lax.ppermute(value, AX, pairs)  33.4 us
    ppermute x8, waiting for transfers between devices, shift_z(): lax.ppermute(value, AX, [(ident(x, y, z, c), ident(x, y, z + step, c)) fo...  16.6 us
    ppermute x8, starting transfers between devices, shift_z(): lax.ppermute(value, AX, [(ident(x, y, z, c), ident(x, y, z + step, c)) fo...  14.8 us
    pallas_call x2, Pallas kernels, quadratic_blocks(): pl.pallas_call(functools.partial(quadratic_kernel, count), out_shape=[jax...  3.63 us
    pallas_call x1, Pallas kernels, place_blocks(): pl.pallas_call(place_kernel, out_shape=jax.ShapeDtypeStruct((ROWS, HALF),...  3.33 us
    pallas_call x1, Pallas kernels, small_shares(): pl.pallas_call(shares_kernel, out_shape=[jax.ShapeDtypeStruct((2 * WD, PA...  2.99 us
  transfers between devices with their start and end apart: 32, of which 18 were waited for; matrix products, arithmetic and copies ran while one was open for 1% of the time, Pallas kernels for 5%

profile of v5, /device:TPU:0, one launch (start us, length us, event | category | flops | bytes accessed | tf_op | source)
XLA Modules:
  0.0 140.3 jit_solution(1391561785245436435)
XLA Ops:
  0.7 3.0 %shard_map.59 = (bf16[16,2048]{1,0:T(8,128)(2,1)}, bf16[16,2048]{1,0:T(8,128)(2,1)}, bf16[16,2048]{1,0:T(8,128)(2,1)}, bf16[16,2048]{1,0:T(8,128)(2,1)}) custom-call(s32[128,128]{1,0:T(8,128)} %cyc_map.1, s32[1,64]{1,0:T(1,128)} %amp_map.3, bf16[8,8192]{1,0:T(8,128)(2,1)} %bitcast.6, bf16[128,8192]{1,0:T(8,128)(2,1)} %refs_3_), custom_call_target="tpu_custom_call" | custom-call | bytes 600000 | tf_op jit(solution)/shard_map/pallas_call | solution.py:84
  14.2 4.0 %collective-permute-start.8 = (bf16[64,2048]{1,0:T(8,128)(2,1)S(1)}, bf16[64,2048]{1,0:T(8,128)(2,1)S(1)}, u32[]{:S(2)}, u32[]{:S(2)}) collective-permute-start(bf16[64,2048]{1,0:T(8,128)(2,1)S(1)} %shard_map.61.refs_0_), channel_id=1, source_target_pairs={{0,14},{1,15},{2,0},{3,1},{4,2},{5,3},{6,4},{7,5},{8,6},{9,7},{10,... | collective-permute-start | bytes 786440 | tf_op jit(solution)/shard_map/ppermute | solution.py:32
  18.2 5.3 %collective-permute-done.3.refs_8_ = bf16[64,2048]{1,0:T(8,128)(2,1)S(1)} collective-permute-done((bf16[64,2048]{1,0:T(8,128)(2,1)S(1)}, bf16[64,2048]{1,0:T(8,128)(2,1)S(1)}, u32[]{:S(2)}, u32[]{:S(2)}) %collective-permute-start.3) | collective-permute-done | bytes 262176 | tf_op jit(solution)/shard_map/ppermute | solution.py:32
  23.6 3.2 %collective-permute-start.9 = (bf16[64,2048]{1,0:T(8,128)(2,1)S(1)}, bf16[64,2048]{1,0:T(8,128)(2,1)S(1)}, u32[]{:S(2)}, u32[]{:S(2)}) collective-permute-start(bf16[64,2048]{1,0:T(8,128)(2,1)S(1)} %collective-permute-done.8.refs_1_), channel_id=1, source_target_pairs={{0,14},{1,15},{2,0},{3,1},{4,2},{5,3},{6,4},{7,5},{8,6},{9,7},{10,... | collective-permute-start | bytes 786440 | tf_op jit(solution)/shard_map/ppermute | solution.py:32
  28.0 2.5 %collective-permute-start.5 = (bf16[128,2048]{1,0:T(8,128)(2,1)S(1)}, bf16[128,2048]{1,0:T(8,128)(2,1)S(1)}, u32[]{:S(2)}, u32[]{:S(2)}) collective-permute-start(bf16[128,2048]{1,0:T(8,128)(2,1)S(1)} %get-tuple-element.44), channel_id=1, source_target_pairs={{0,128},{1,33},{2,130},{3,35},{4,132},{5,37},{6,134},{7,39},{8,136... | collective-permute-start | bytes 1572872 | tf_op jit(solution)/shard_map/ppermute | solution.py:42
  31.3 3.9 %collective-permute-start.7 = (bf16[128,2048]{1,0:T(8,128)(2,1)S(1)}, bf16[128,2048]{1,0:T(8,128)(2,1)S(1)}, u32[]{:S(2)}, u32[]{:S(2)}) collective-permute-start(bf16[128,2048]{1,0:T(8,128)(2,1)S(1)} %get-tuple-element.46), channel_id=1, source_target_pairs={{0,192},{1,49},{2,194},{3,51},{4,196},{5,53},{6,198},{7,55},{8,200... | collective-permute-start | bytes 1572872 | tf_op jit(solution)/shard_map/ppermute | solution.py:42
  37.3 4.3 %collective-permute-done.10.refs_3_ = bf16[64,2048]{1,0:T(8,128)(2,1)S(1)} collective-permute-done((bf16[64,2048]{1,0:T(8,128)(2,1)S(1)}, bf16[64,2048]{1,0:T(8,128)(2,1)S(1)}, u32[]{:S(2)}, u32[]{:S(2)}) %collective-permute-start.10) | collective-permute-done | bytes 262176 | tf_op jit(solution)/shard_map/ppermute | solution.py:32
  41.6 3.4 %collective-permute-start.11 = (bf16[32,2048]{1,0:T(8,128)(2,1)S(1)}, bf16[32,2048]{1,0:T(8,128)(2,1)S(1)}, u32[]{:S(2)}, u32[]{:S(2)}) collective-permute-start(bf16[32,2048]{1,0:T(8,128)(2,1)S(1)} %slice.24), channel_id=1, source_target_pairs={{0,14},{1,15},{2,0},{3,1},{4,2},{5,3},{6,4},{7,5},{8,6},{9,7},{10,... | collective-permute-start | bytes 393224 | tf_op jit(solution)/shard_map/ppermute | solution.py:32
  45.2 2.4 %collective-permute-done.11.refs_4_ = bf16[32,2048]{1,0:T(8,128)(2,1)S(1)} collective-permute-done((bf16[32,2048]{1,0:T(8,128)(2,1)S(1)}, bf16[32,2048]{1,0:T(8,128)(2,1)S(1)}, u32[]{:S(2)}, u32[]{:S(2)}) %collective-permute-start.11) | collective-permute-done | bytes 131104 | tf_op jit(solution)/shard_map/ppermute | solution.py:32
  47.6 3.8 %collective-permute-done.13.refs_5_ = bf16[32,2048]{1,0:T(8,128)(2,1)S(1)} collective-permute-done((bf16[32,2048]{1,0:T(8,128)(2,1)S(1)}, bf16[32,2048]{1,0:T(8,128)(2,1)S(1)}, u32[]{:S(2)}, u32[]{:S(2)}) %collective-permute-start.13) | collective-permute-done | bytes 131104 | tf_op jit(solution)/shard_map/ppermute | solution.py:32
  51.5 3.7 %collective-permute-start.14 = (bf16[256,2048]{1,0:T(8,128)(2,1)S(1)}, bf16[256,2048]{1,0:T(8,128)(2,1)S(1)}, u32[]{:S(2)}, u32[]{:S(2)}) collective-permute-start(bf16[256,2048]{1,0:T(8,128)(2,1)S(1)} %get-tuple-element.48.refs_4_), channel_id=1, source_target_pairs={{0,48},{1,193},{2,50},{3,195},{4,52},{5,197},{6,54},{7,199},{8,56}... | collective-permute-start | bytes 3145736 | tf_op jit(solution)/shard_map/ppermute | solution.py:42
  55.2 12.3 %collective-permute-done.14.refs_5_ = bf16[256,2048]{1,0:T(8,128)(2,1)S(1)} collective-permute-done((bf16[256,2048]{1,0:T(8,128)(2,1)S(1)}, bf16[256,2048]{1,0:T(8,128)(2,1)S(1)}, u32[]{:S(2)}, u32[]{:S(2)}) %collective-permute-start.14) | collective-permute-done | bytes 1048608 | tf_op jit(solution)/shard_map/ppermute | solution.py:42
  67.5 3.8 %collective-permute-start.15 = (bf16[128,2048]{1,0:T(8,128)(2,1)S(1)}, bf16[128,2048]{1,0:T(8,128)(2,1)S(1)}, u32[]{:S(2)}, u32[]{:S(2)}) collective-permute-start(bf16[128,2048]{1,0:T(8,128)(2,1)S(1)} %slice.26), channel_id=1, source_target_pairs={{0,48},{1,193},{2,50},{3,195},{4,52},{5,197},{6,54},{7,199},{8,56}... | collective-permute-start | bytes 1572872 | tf_op jit(solution)/shard_map/ppermute | solution.py:42
  73.3 3.3 %collective-permute-start.22 = (bf16[256,2048]{1,0:T(8,128)(2,1)S(1)}, bf16[256,2048]{1,0:T(8,128)(2,1)S(1)}, u32[]{:S(2)}, u32[]{:S(2)}) collective-permute-start(bf16[256,2048]{1,0:T(8,128)(2,1)S(1)} %get-tuple-element.56.refs_1_.refs_3_), channel_id=1, source_target_pairs={{0,48},{1,193},{2,50},{3,195},{4,52},{5,197},{6,54},{7,199},{8,56}... | collective-permute-start | bytes 3145736 | tf_op jit(solution)/shard_map/ppermute | solution.py:42
  78.0 8.9 %collective-permute-done.17.refs_5_ = bf16[128,2048]{1,0:T(8,128)(2,1)S(1)} collective-permute-done((bf16[128,2048]{1,0:T(8,128)(2,1)S(1)}, bf16[128,2048]{1,0:T(8,128)(2,1)S(1)}, u32[]{:S(2)}, u32[]{:S(2)}) %collective-permute-start.17) | collective-permute-done | bytes 524320 | tf_op jit(solution)/shard_map/ppermute | solution.py:42
  87.8 3.1 %collective-permute-start.18 = (bf16[128,1024]{1,0:T(8,128)(2,1)S(1)}, bf16[128,1024]{1,0:T(8,128)(2,1)S(1)}, u32[]{:S(2)}, u32[]{:S(2)}) collective-permute-start(bf16[128,1024]{1,0:T(8,128)(2,1)S(1)} %get-tuple-element.52), channel_id=1, source_target_pairs={{0,192},{1,49},{2,194},{3,51},{4,196},{5,53},{6,198},{7,55},{8,200... | collective-permute-start | bytes 786440 | tf_op jit(solution)/shard_map/ppermute | solution.py:42
  91.0 7.2 %collective-permute-done.20 = bf16[128,1024]{1,0:T(8,128)(2,1)S(1)} collective-permute-done((bf16[128,1024]{1,0:T(8,128)(2,1)S(1)}, bf16[128,1024]{1,0:T(8,128)(2,1)S(1)}, u32[]{:S(2)}, u32[]{:S(2)}) %collective-permute-start.20) | collective-permute-done | bytes 262176 | tf_op jit(solution)/shard_map/ppermute | solution.py:42
  103.1 3.8 %collective-permute-start.27 = (bf16[128,1024]{1,0:T(8,128)(2,1)S(1)}, bf16[128,1024]{1,0:T(8,128)(2,1)S(1)}, u32[]{:S(2)}, u32[]{:S(2)}) collective-permute-start(bf16[128,1024]{1,0:T(8,128)(2,1)S(1)} %shard_map.65.refs_0_), channel_id=1, source_target_pairs={{0,128},{1,33},{2,130},{3,35},{4,132},{5,37},{6,134},{7,39},{8,136... | collective-permute-start | bytes 786440 | tf_op jit(solution)/shard_map/ppermute | solution.py:42
  109.2 6.1 %collective-permute-done.25.refs_5_.refs_7_ = bf16[128,2048]{1,0:T(8,128)(2,1)S(1)} collective-permute-done((bf16[128,2048]{1,0:T(8,128)(2,1)S(1)}, bf16[128,2048]{1,0:T(8,128)(2,1)S(1)}, u32[]{:S(2)}, u32[]{:S(2)}) %collective-permute-start.25) | collective-permute-done | bytes 524320 | tf_op jit(solution)/shard_map/ppermute | solution.py:42
  116.3 2.9 %shard_map.67 = (bf16[128,2048]{1,0:T(8,128)(2,1)}, bf16[128,2048]{1,0:T(8,128)(2,1)}, bf16[128,2048]{1,0:T(8,128)(2,1)}) custom-call(bf16[128,1024]{1,0:T(8,128)(2,1)S(1)} %collective-permute-done.26.refs_0_, bf16[128,1024]{1,0:T(8,128)(2,1)S(1)} %collective-permute-done.27.refs_1_, bf16[128,1024]{1,0:T(8,128)(2,1)S(1)} %collective-permute-done.28.refs_2_, ...), custom_call_target="tpu_custom_call" | custom-call | flops 1610612736 | bytes 5000000 | tf_op jit(solution)/shard_map/pallas_call | solution.py:256
  126.1 2.6 %collective-permute-done.29.refs_1_ = bf16[128,2048]{1,0:T(8,128)(2,1)} collective-permute-done((bf16[128,2048]{1,0:T(8,128)(2,1)}, bf16[128,2048]{1,0:T(8,128)(2,1)}, u32[]{:S(2)}, u32[]{:S(2)}) %collective-permute-start.29) | collective-permute-done | bytes 524320 | tf_op jit(solution)/shard_map/ppermute | solution.py:42
  128.7 2.6 %collective-permute-done.30.refs_2_ = bf16[128,2048]{1,0:T(8,128)(2,1)} collective-permute-done((bf16[128,2048]{1,0:T(8,128)(2,1)}, bf16[128,2048]{1,0:T(8,128)(2,1)}, u32[]{:S(2)}, u32[]{:S(2)}) %collective-permute-start.30) | collective-permute-done | bytes 524320 | tf_op jit(solution)/shard_map/ppermute | solution.py:42
  131.3 5.5 %collective-permute-done.31.refs_3_ = bf16[128,2048]{1,0:T(8,128)(2,1)} collective-permute-done((bf16[128,2048]{1,0:T(8,128)(2,1)}, bf16[128,2048]{1,0:T(8,128)(2,1)}, u32[]{:S(2)}, u32[]{:S(2)}) %collective-permute-start.31) | collective-permute-done | bytes 524320 | tf_op jit(solution)/shard_map/ppermute | solution.py:42
  136.8 3.3 %shard_map.68 = bf16[128,8192]{1,0:T(8,128)(2,1)} custom-call(s32[4]{0:T(128)S(1)} %pad_add_fusion.place, bf16[128,2048]{1,0:T(8,128)(2,1)S(1)} %shard_map.66.refs_0_, bf16[128,2048]{1,0:T(8,128)(2,1)} %collective-permute-done.29.refs_1_, bf16[128,2048]{1,0:T(8,128)(2,1)} %collective-permute-done.30.refs_2_, bf16[128,2048]{1,0:T(8,128)(2,1)} %collective-permute-done.31.refs_3_), custom_call_target="tpu_custom_call" | custom-call | bytes 4000000 | tf_op jit(solution)/shard_map/pallas_call | solution.py:283
  (77 shorter events, 34.2 us)
Async XLA Ops:
  12.2 11.4 %collective-permute-start.3 = (bf16[64,2048]{1,0:T(8,128)(2,1)S(1)}, bf16[64,2048]{1,0:T(8,128)(2,1)S(1)}, u32[]{:S(2)}, u32[]{:S(2)}) collective-permute-start(bf16[64,2048]{1,0:T(8,128)(2,1)S(1)} %shard_map.61.refs_0_), channel_id=1, source_target_pairs={{0,2},{1,3},{2,4},{3,5},{4,6},{5,7},{6,8},{7,9},{8,10},{9,11},{10,... | collective-permute-start | bytes 786440 | tf_op jit(solution)/shard_map/ppermute | solution.py:32
  14.2 9.4 %collective-permute-start.8 = (bf16[64,2048]{1,0:T(8,128)(2,1)S(1)}, bf16[64,2048]{1,0:T(8,128)(2,1)S(1)}, u32[]{:S(2)}, u32[]{:S(2)}) collective-permute-start(bf16[64,2048]{1,0:T(8,128)(2,1)S(1)} %shard_map.61.refs_0_), channel_id=1, source_target_pairs={{0,14},{1,15},{2,0},{3,1},{4,2},{5,3},{6,4},{7,5},{8,6},{9,7},{10,... | collective-permute-start | bytes 786440 | tf_op jit(solution)/shard_map/ppermute | solution.py:32
  23.6 11.7 %collective-permute-start.9 = (bf16[64,2048]{1,0:T(8,128)(2,1)S(1)}, bf16[64,2048]{1,0:T(8,128)(2,1)S(1)}, u32[]{:S(2)}, u32[]{:S(2)}) collective-permute-start(bf16[64,2048]{1,0:T(8,128)(2,1)S(1)} %collective-permute-done.8.refs_1_), channel_id=1, source_target_pairs={{0,14},{1,15},{2,0},{3,1},{4,2},{5,3},{6,4},{7,5},{8,6},{9,7},{10,... | collective-permute-start | bytes 786440 | tf_op jit(solution)/shard_map/ppermute | solution.py:32
  26.8 24.7 %collective-permute-start.4 = (bf16[128,2048]{1,0:T(8,128)(2,1)S(1)}, bf16[128,2048]{1,0:T(8,128)(2,1)S(1)}, u32[]{:S(2)}, u32[]{:S(2)}) collective-permute-start(bf16[128,2048]{1,0:T(8,128)(2,1)S(1)} %get-tuple-element.43), channel_id=1, source_target_pairs={{0,64},{1,17},{2,66},{3,19},{4,68},{5,21},{6,70},{7,23},{8,72},{9,... | collective-permute-start | bytes 1572872 | tf_op jit(solution)/shard_map/ppermute | solution.py:42
  28.0 23.5 %collective-permute-start.5 = (bf16[128,2048]{1,0:T(8,128)(2,1)S(1)}, bf16[128,2048]{1,0:T(8,128)(2,1)S(1)}, u32[]{:S(2)}, u32[]{:S(2)}) collective-permute-start(bf16[128,2048]{1,0:T(8,128)(2,1)S(1)} %get-tuple-element.44), channel_id=1, source_target_pairs={{0,128},{1,33},{2,130},{3,35},{4,132},{5,37},{6,134},{7,39},{8,136... | collective-permute-start | bytes 1572872 | tf_op jit(solution)/shard_map/ppermute | solution.py:42
  31.3 20.2 %collective-permute-start.7 = (bf16[128,2048]{1,0:T(8,128)(2,1)S(1)}, bf16[128,2048]{1,0:T(8,128)(2,1)S(1)}, u32[]{:S(2)}, u32[]{:S(2)}) collective-permute-start(bf16[128,2048]{1,0:T(8,128)(2,1)S(1)} %get-tuple-element.46), channel_id=1, source_target_pairs={{0,192},{1,49},{2,194},{3,51},{4,196},{5,53},{6,198},{7,55},{8,200... | collective-permute-start | bytes 1572872 | tf_op jit(solution)/shard_map/ppermute | solution.py:42
  36.0 9.1 %collective-permute-start.12 = (bf16[64,2048]{1,0:T(8,128)(2,1)S(1)}, bf16[64,2048]{1,0:T(8,128)(2,1)S(1)}, u32[]{:S(2)}, u32[]{:S(2)}) collective-permute-start(bf16[64,2048]{1,0:T(8,128)(2,1)S(1)} %collective-permute-done.6.refs_7_), channel_id=1, source_target_pairs={{0,2},{1,3},{2,4},{3,5},{4,6},{5,7},{6,8},{7,9},{8,10},{9,11},{10,... | collective-permute-start | bytes 786440 | tf_op jit(solution)/shard_map/ppermute | solution.py:32
  51.5 16.0 %collective-permute-start.14 = (bf16[256,2048]{1,0:T(8,128)(2,1)S(1)}, bf16[256,2048]{1,0:T(8,128)(2,1)S(1)}, u32[]{:S(2)}, u32[]{:S(2)}) collective-permute-start(bf16[256,2048]{1,0:T(8,128)(2,1)S(1)} %get-tuple-element.48.refs_4_), channel_id=1, source_target_pairs={{0,48},{1,193},{2,50},{3,195},{4,52},{5,197},{6,54},{7,199},{8,56}... | collective-permute-start | bytes 3145736 | tf_op jit(solution)/shard_map/ppermute | solution.py:42
  55.2 16.1 %collective-permute-start.16 = (bf16[256,2048]{1,0:T(8,128)(2,1)S(1)}, bf16[256,2048]{1,0:T(8,128)(2,1)S(1)}, u32[]{:S(2)}, u32[]{:S(2)}) collective-permute-start(bf16[256,2048]{1,0:T(8,128)(2,1)S(1)} %get-tuple-element.48.refs_4_), channel_id=1, source_target_pairs={{0,16},{1,65},{2,18},{3,67},{4,20},{5,69},{6,22},{7,71},{8,24},{9,... | collective-permute-start | bytes 3145736 | tf_op jit(solution)/shard_map/ppermute | solution.py:42
  67.5 10.5 %collective-permute-start.15 = (bf16[128,2048]{1,0:T(8,128)(2,1)S(1)}, bf16[128,2048]{1,0:T(8,128)(2,1)S(1)}, u32[]{:S(2)}, u32[]{:S(2)}) collective-permute-start(bf16[128,2048]{1,0:T(8,128)(2,1)S(1)} %slice.26), channel_id=1, source_target_pairs={{0,48},{1,193},{2,50},{3,195},{4,52},{5,197},{6,54},{7,199},{8,56}... | collective-permute-start | bytes 1572872 | tf_op jit(solution)/shard_map/ppermute | solution.py:42
  71.4 15.6 %collective-permute-start.17 = (bf16[128,2048]{1,0:T(8,128)(2,1)S(1)}, bf16[128,2048]{1,0:T(8,128)(2,1)S(1)}, u32[]{:S(2)}, u32[]{:S(2)}) collective-permute-start(bf16[128,2048]{1,0:T(8,128)(2,1)S(1)} %slice.27), channel_id=1, source_target_pairs={{0,16},{1,65},{2,18},{3,67},{4,20},{5,69},{6,22},{7,71},{8,24},{9,... | collective-permute-start | bytes 1572872 | tf_op jit(solution)/shard_map/ppermute | solution.py:42
  73.3 26.0 %collective-permute-start.22 = (bf16[256,2048]{1,0:T(8,128)(2,1)S(1)}, bf16[256,2048]{1,0:T(8,128)(2,1)S(1)}, u32[]{:S(2)}, u32[]{:S(2)}) collective-permute-start(bf16[256,2048]{1,0:T(8,128)(2,1)S(1)} %get-tuple-element.56.refs_1_.refs_3_), channel_id=1, source_target_pairs={{0,48},{1,193},{2,50},{3,195},{4,52},{5,197},{6,54},{7,199},{8,56}... | collective-permute-start | bytes 3145736 | tf_op jit(solution)/shard_map/ppermute | solution.py:42
  76.6 22.9 %collective-permute-start.23 = (bf16[256,2048]{1,0:T(8,128)(2,1)S(1)}, bf16[256,2048]{1,0:T(8,128)(2,1)S(1)}, u32[]{:S(2)}, u32[]{:S(2)}) collective-permute-start(bf16[256,2048]{1,0:T(8,128)(2,1)S(1)} %get-tuple-element.56.refs_1_.refs_3_), channel_id=1, source_target_pairs={{0,16},{1,65},{2,18},{3,67},{4,20},{5,69},{6,22},{7,71},{8,24},{9,... | collective-permute-start | bytes 3145736 | tf_op jit(solution)/shard_map/ppermute | solution.py:42
  87.7 10.5 %collective-permute-start.20 = (bf16[128,1024]{1,0:T(8,128)(2,1)S(1)}, bf16[128,1024]{1,0:T(8,128)(2,1)S(1)}, u32[]{:S(2)}, u32[]{:S(2)}) collective-permute-start(bf16[128,1024]{1,0:T(8,128)(2,1)S(1)} %get-tuple-element.54), channel_id=1, source_target_pairs={{0,64},{1,17},{2,66},{3,19},{4,68},{5,21},{6,70},{7,23},{8,72},{9,... | collective-permute-start | bytes 786440 | tf_op jit(solution)/shard_map/ppermute | solution.py:42
  87.7 10.4 %collective-permute-start.19 = (bf16[128,1024]{1,0:T(8,128)(2,1)S(1)}, bf16[128,1024]{1,0:T(8,128)(2,1)S(1)}, u32[]{:S(2)}, u32[]{:S(2)}) collective-permute-start(bf16[128,1024]{1,0:T(8,128)(2,1)S(1)} %get-tuple-element.53), channel_id=1, source_target_pairs={{0,128},{1,33},{2,130},{3,35},{4,132},{5,37},{6,134},{7,39},{8,136... | collective-permute-start | bytes 786440 | tf_op jit(solution)/shard_map/ppermute | solution.py:42
  87.8 11.2 %collective-permute-start.18 = (bf16[128,1024]{1,0:T(8,128)(2,1)S(1)}, bf16[128,1024]{1,0:T(8,128)(2,1)S(1)}, u32[]{:S(2)}, u32[]{:S(2)}) collective-permute-start(bf16[128,1024]{1,0:T(8,128)(2,1)S(1)} %get-tuple-element.52), channel_id=1, source_target_pairs={{0,192},{1,49},{2,194},{3,51},{4,196},{5,53},{6,198},{7,55},{8,200... | collective-permute-start | bytes 786440 | tf_op jit(solution)/shard_map/ppermute | solution.py:42
  99.3 9.8 %collective-permute-start.24 = (bf16[128,2048]{1,0:T(8,128)(2,1)S(1)}, bf16[128,2048]{1,0:T(8,128)(2,1)S(1)}, u32[]{:S(2)}, u32[]{:S(2)}) collective-permute-start(bf16[128,2048]{1,0:T(8,128)(2,1)S(1)} %slice.28), channel_id=1, source_target_pairs={{0,48},{1,193},{2,50},{3,195},{4,52},{5,197},{6,54},{7,199},{8,56}... | collective-permute-start | bytes 1572872 | tf_op jit(solution)/shard_map/ppermute | solution.py:42
  99.5 15.8 %collective-permute-start.25 = (bf16[128,2048]{1,0:T(8,128)(2,1)S(1)}, bf16[128,2048]{1,0:T(8,128)(2,1)S(1)}, u32[]{:S(2)}, u32[]{:S(2)}) collective-permute-start(bf16[128,2048]{1,0:T(8,128)(2,1)S(1)} %slice.29), channel_id=1, source_target_pairs={{0,16},{1,65},{2,18},{3,67},{4,20},{5,69},{6,22},{7,71},{8,24},{9,... | collective-permute-start | bytes 1572872 | tf_op jit(solution)/shard_map/ppermute | solution.py:42
  103.0 13.3 %collective-permute-start.26 = (bf16[128,1024]{1,0:T(8,128)(2,1)S(1)}, bf16[128,1024]{1,0:T(8,128)(2,1)S(1)}, u32[]{:S(2)}, u32[]{:S(2)}) collective-permute-start(bf16[128,1024]{1,0:T(8,128)(2,1)S(1)} %shard_map.65.refs_0_), channel_id=1, source_target_pairs={{0,64},{1,17},{2,66},{3,19},{4,68},{5,21},{6,70},{7,23},{8,72},{9,... | collective-permute-start | bytes 786440 | tf_op jit(solution)/shard_map/ppermute | solution.py:42
  103.1 13.3 %collective-permute-start.27 = (bf16[128,1024]{1,0:T(8,128)(2,1)S(1)}, bf16[128,1024]{1,0:T(8,128)(2,1)S(1)}, u32[]{:S(2)}, u32[]{:S(2)}) collective-permute-start(bf16[128,1024]{1,0:T(8,128)(2,1)S(1)} %shard_map.65.refs_0_), channel_id=1, source_target_pairs={{0,128},{1,33},{2,130},{3,35},{4,132},{5,37},{6,134},{7,39},{8,136... | collective-permute-start | bytes 786440 | tf_op jit(solution)/shard_map/ppermute | solution.py:42
  106.9 9.5 %collective-permute-start.28 = (bf16[128,1024]{1,0:T(8,128)(2,1)S(1)}, bf16[128,1024]{1,0:T(8,128)(2,1)S(1)}, u32[]{:S(2)}, u32[]{:S(2)}) collective-permute-start(bf16[128,1024]{1,0:T(8,128)(2,1)S(1)} %shard_map.65.refs_0_), channel_id=1, source_target_pairs={{0,192},{1,49},{2,194},{3,51},{4,196},{5,53},{6,198},{7,55},{8,200... | collective-permute-start | bytes 786440 | tf_op jit(solution)/shard_map/ppermute | solution.py:42
  119.2 9.5 %collective-permute-start.29 = (bf16[128,2048]{1,0:T(8,128)(2,1)}, bf16[128,2048]{1,0:T(8,128)(2,1)}, u32[]{:S(2)}, u32[]{:S(2)}) collective-permute-start(bf16[128,2048]{1,0:T(8,128)(2,1)} %get-tuple-element.57), channel_id=1, source_target_pairs={{0,192},{1,49},{2,194},{3,51},{4,196},{5,53},{6,198},{7,55},{8,200... | collective-permute-start | bytes 1572872 | tf_op jit(solution)/shard_map/ppermute | solution.py:42
  120.2 11.1 %collective-permute-start.30 = (bf16[128,2048]{1,0:T(8,128)(2,1)}, bf16[128,2048]{1,0:T(8,128)(2,1)}, u32[]{:S(2)}, u32[]{:S(2)}) collective-permute-start(bf16[128,2048]{1,0:T(8,128)(2,1)} %get-tuple-element.58), channel_id=1, source_target_pairs={{0,128},{1,33},{2,130},{3,35},{4,132},{5,37},{6,134},{7,39},{8,136... | collective-permute-start | bytes 1572872 | tf_op jit(solution)/shard_map/ppermute | solution.py:42
  120.7 16.1 %collective-permute-start.31 = (bf16[128,2048]{1,0:T(8,128)(2,1)}, bf16[128,2048]{1,0:T(8,128)(2,1)}, u32[]{:S(2)}, u32[]{:S(2)}) collective-permute-start(bf16[128,2048]{1,0:T(8,128)(2,1)} %get-tuple-element.59), channel_id=1, source_target_pairs={{0,64},{1,17},{2,66},{3,19},{4,68},{5,21},{6,70},{7,23},{8,72},{9,... | collective-permute-start | bytes 1572872 | tf_op jit(solution)/shard_map/ppermute | solution.py:42
  (15 other events, 78.6 us)

commit v6 on v5

--- a/solution.py
+++ b/solution.py
@@ -16,8 +16,11 @@
 HALF = 8192
 PART = HALF // 4
 QW = 1024
+EARLY = 5 * 32
+LATE = 3 * 32
 VMEM = pl.BlockSpec(memory_space=pltpu.VMEM)
-PARAMS = pltpu.CompilerParams(vmem_limit_bytes=24 * 2**20)
+PARAMS = pltpu.CompilerParams(vmem_limit_bytes=8 * 2**20)
+WIDE = pltpu.CompilerParams(vmem_limit_bytes=16 * 2**20)
 
 
 def ident(x, y, z, c):
@@ -58,18 +61,22 @@
     return pl.CostEstimate(flops=flops, bytes_accessed=moved, transcendentals=0)
 
 
-def shares_kernel(cyc_map, amp_map, cyc, amp, *refs):
-    outs, rows, both, sem = refs[:4], refs[4], refs[5], refs[6]
+def shares_kernel(cyc_map_in, amp_map_in, cyc_in, amp, *refs):
+    outs, rows, both, half_map, amp_map, cyc, sem = refs[:4], *refs[4:]
     row, col, core = (lax.axis_index(a) for a in AX)
     g = jnp.where(core == 0, row, col // NZ)
-    copy = pltpu.make_async_copy(amp.at[0:16, :], rows, sem)
-    copy.start()
     tiles = HALF // TB
-    half_map = cyc_map[pl.ds(pl.multiple_of(core * tiles, tiles), tiles), :].astype(F32)
+    mine = cyc_map_in.at[pl.ds(pl.multiple_of(core * tiles, tiles), tiles), :]
+    pairs = [(mine, half_map), (amp_map_in, amp_map), (cyc_in, cyc), (amp.at[0:16, :], rows)]
+    copies = [pltpu.make_async_copy(pairs[i][0], pairs[i][1], sem.at[i]) for i in range(4)]
+    for copy in copies:
+        copy.start()
+    for copy in copies:
+        copy.wait()
+    half_map = half_map[...].astype(F32)
     lane = lax.broadcasted_iota(jnp.int32, half_map.shape, 1)
     keep = jnp.sum(jnp.where(lane == row * NY * NZ + col, half_map, 0.0), axis=1, keepdims=True)
     keep_window = amp_map[...].astype(F32)
-    copy.wait()
     for t in range(tiles):
         at = slice(t * TB, (t + 1) * TB)
         top = cyc[:, at].astype(F32) * keep[t : t + 1, :]
@@ -84,12 +91,15 @@
     return pl.pallas_call(
         shares_kernel,
         out_shape=[jax.ShapeDtypeStruct((2 * WD, PART), BF)] * 4,
-        in_specs=[VMEM] * 3 + [pl.BlockSpec(memory_space=pl.ANY)],
+        in_specs=[pl.BlockSpec(memory_space=pl.ANY)] * 4,
         out_specs=[VMEM] * 4,
         scratch_shapes=[
             pltpu.VMEM((16, HALF), BF),
             pltpu.VMEM((16, HALF), BF),
-            pltpu.SemaphoreType.DMA,
+            pltpu.VMEM((HALF // TB, 128), jnp.int32),
+            pltpu.VMEM((1, HALF // TB), jnp.int32),
+            pltpu.VMEM((WD, HALF), BF),
+            pltpu.SemaphoreType.DMA((4,)),
         ],
         compiler_params=pltpu.CompilerParams(vmem_limit_bytes=60 * 2**20),
         cost_estimate=cost(0, 600_000),
@@ -120,20 +130,43 @@
     )(place, *pieces)
 
 
-def part_kernel(*refs):
-    pieces, outs = refs[:9], refs[9:]
+def late_kernel(*refs):
+    outs = refs[9:]
     at = 0
-    for ref in pieces:
+    for ref in refs[:9]:
         for rows in range(0, ref.shape[0], 32):
-            outs[0][at : at + 16, :] = ref[rows : rows + 16, :]
+            if at >= EARLY:
+                outs[0][at - EARLY : at - EARLY + 16, :] = ref[rows : rows + 16, :]
             outs[1][at : at + 16, :] = ref[rows + 16 : rows + 32, :]
             at += 16
 
 
-def part(pieces):
-    return pl.pallas_call(
-        part_kernel,
-        out_shape=[jax.ShapeDtypeStruct((32 * WD, PART), BF)] * 2,
+def early_kernel(*refs):
+    at = 0
+    for ref in refs[:5]:
+        for rows in range(0, ref.shape[0], 32):
+            refs[5][at : at + 16, :] = ref[rows : rows + 16, :]
+            at += 16
+
+
+def part_early(pieces):
+    return pl.pallas_call(
+        early_kernel,
+        out_shape=jax.ShapeDtypeStruct((EARLY, PART), BF),
+        in_specs=[VMEM] * 5,
+        out_specs=VMEM,
+        compiler_params=PARAMS,
+        cost_estimate=cost(0, 1_300_000),
+    )(*pieces)
+
+
+def part_late(pieces):
+    return pl.pallas_call(
+        late_kernel,
+        out_shape=[
+            jax.ShapeDtypeStruct((LATE, PART), BF),
+            jax.ShapeDtypeStruct((EARLY + LATE, PART), BF),
+        ],
         in_specs=[VMEM] * 9,
         out_specs=[VMEM] * 2,
         compiler_params=PARAMS,
@@ -170,52 +203,53 @@
     )(place, amp_map, *[amplitudes] * 4)
 
 
-def dressed_kernel(count, *refs):
-    blocks, cyc = refs[:4], refs[4 : 4 + count]
-    away, own = refs[-2:]
+def product(blocks, cyc):
     left = jnp.concatenate([blocks[d][...] for d in (1, 2, 3, 0)], 0)
-    for at in range(count):
-        value = lax.dot_general(left, cyc[at][...], (((1,), (1,)), ((), ())), preferred_element_type=F32)
-        where = slice(at * 256, at * 256 + 256)
-        away[:, where] = value[: 3 * ROWS].astype(BF)
-        own[:, where] = value[3 * ROWS :]
+    right = jnp.concatenate([ref[...] for ref in cyc], 0)
+    return lax.dot_general(left, right, (((1,), (1,)), ((), ())), preferred_element_type=F32)
+
+
+def dressed_first_kernel(*refs):
+    value = product(refs[:4], refs[4:9])
+    refs[9][...] = value[: 3 * ROWS].astype(BF)
+    refs[10][...] = value[3 * ROWS :]
 
 
 def dressed_first(blocks, cyc):
     return pl.pallas_call(
-        functools.partial(dressed_kernel, len(cyc)),
-        out_shape=[jax.ShapeDtypeStruct((3 * ROWS, QW), BF), jax.ShapeDtypeStruct((ROWS, QW), F32)],
-        in_specs=[VMEM] * (4 + len(cyc)),
+        dressed_first_kernel,
+        out_shape=[
+            jax.ShapeDtypeStruct((3 * ROWS, 4 * EARLY), BF),
+            jax.ShapeDtypeStruct((ROWS, 4 * EARLY), F32),
+        ],
+        in_specs=[VMEM] * 9,
         out_specs=[VMEM] * 2,
-        compiler_params=PARAMS,
-        cost_estimate=cost(2 * 512 * PART * 768, 8_000_000),
+        compiler_params=WIDE,
+        cost_estimate=cost(2 * 512 * PART * 4 * EARLY, 6_000_000),
     )(*blocks, *cyc)
 
 
 def dressed_last_kernel(*refs):
-    blocks, halves, away_in, own_in = refs[:4], refs[4:6], refs[6], refs[7]
-    outs, own = refs[8:11], refs[11]
-    edge = 3 * 256
-    left = jnp.concatenate([blocks[d][...] for d in (1, 2, 3, 0)], 0)
-    right = jnp.concatenate([ref[...] for ref in halves], 0)
-    value = lax.dot_general(left, right, (((1,), (1,)), ((), ())), preferred_element_type=F32)
+    away, early, outs, own = refs[9], refs[10], refs[11:14], refs[14]
+    edge = 4 * EARLY
+    value = product(refs[:4], refs[4:9])
     for d in range(3):
         rows = slice(d * ROWS, (d + 1) * ROWS)
-        outs[d][:, :edge] = away_in[rows, :edge]
+        outs[d][:, :edge] = away[rows, :]
         outs[d][:, edge:] = value[rows].astype(BF)
-    own[:, :edge] = own_in[:, :edge]
+    own[:, :edge] = early[...]
     own[:, edge:] = value[3 * ROWS :]
 
 
-def dressed_last(blocks, halves, away, own):
+def dressed_last(blocks, cyc, away, early):
     return pl.pallas_call(
         dressed_last_kernel,
         out_shape=[jax.ShapeDtypeStruct((ROWS, QW), BF)] * 3 + [jax.ShapeDtypeStruct((ROWS, QW), F32)],
-        in_specs=[VMEM] * 8,
+        in_specs=[VMEM] * 11,
         out_specs=[VMEM] * 4,
-        compiler_params=PARAMS,
-        cost_estimate=cost(2 * 512 * PART * 256, 5_000_000),
-    )(*blocks, *halves, away, own)
+        compiler_params=WIDE,
+        cost_estimate=cost(2 * 512 * PART * 4 * LATE, 6_000_000),
+    )(*blocks, *cyc, away, early)
 
 
 def inner_kernel(mine, other, order, out):
@@ -243,12 +277,17 @@
 def quadratic_kernel(count, *refs):
     lefts, rights, outs = refs[:count], refs[count : count + 5], refs[count + 5 :]
     left = jnp.concatenate([ref[...] for ref in lefts], 0)
+    mine, above, half, other, below = rights
+    middle = half.shape[0]
     wide = 512
     for n in range(0, PART, wide):
-        right = jnp.concatenate([ref[:, n : n + wide] for ref in rights], 0)
-        value = jnp.dot(left, right, preferred_element_type=F32).astype(BF)
+        cols = slice(n, n + wide)
+        right = [mine[:EARLY, cols], above[:EARLY, cols], half[:, cols], other[: EARLY - middle, cols]]
+        right += [below[:EARLY, cols], mine[EARLY:, cols], above[EARLY:, cols]]
+        right += [other[EARLY - middle :, cols], below[EARLY:, cols]]
+        value = jnp.dot(left, jnp.concatenate(right, 0), preferred_element_type=F32).astype(BF)
         for d in range(count):
-            outs[d][:, n : n + wide] = value[d * ROWS : (d + 1) * ROWS]
+            outs[d][:, cols] = value[d * ROWS : (d + 1) * ROWS]
 
 
 def quadratic_blocks(lefts, rights):
@@ -258,20 +297,20 @@
         out_shape=[jax.ShapeDtypeStruct((ROWS, PART), BF)] * count,
         in_specs=[VMEM] * (count + 5),
         out_specs=[VMEM] * count,
-        compiler_params=PARAMS,
+        compiler_params=WIDE,
         cost_estimate=cost(2 * count * ROWS * QW * PART, 5_000_000),
     )(*lefts, *rights)
 
 
-def place_kernel(place, *refs):
-    ins, out, sem = refs[:4], refs[4], refs[5]
+def place_kernel(ds, place, *refs):
+    ins, out, sem = refs[: len(ds)], refs[-2], refs[-1]
     copies = []
-    for d in range(4):
+    for k, d in enumerate(ds):
         at = pl.multiple_of(lax.rem(place[0] + d, 4) * PART, PART)
         for i in range(4):
             rows = slice(i * 32, i * 32 + 32)
             copies.append(
-                pltpu.make_async_copy(ins[d].at[rows, :], out.at[rows, pl.ds(at, PART)], sem.at[d * 4 + i])
+                pltpu.make_async_copy(ins[k].at[rows, :], out.at[rows, pl.ds(at, PART)], sem.at[k * 4 + i])
             )
     for copy in copies:
         copy.start()
@@ -279,20 +318,24 @@
         copy.wait()
 
 
-def place_blocks(place, blocks):
-    return pl.pallas_call(
-        place_kernel,
+def place_blocks(place, blocks, out=None):
+    anywhere = pl.BlockSpec(memory_space=pl.ANY)
+    ds = tuple(blocks)
+    operands = [place] + [blocks[d] for d in ds] + ([] if out is None else [out])
+    return pl.pallas_call(
+        functools.partial(place_kernel, ds),
         out_shape=jax.ShapeDtypeStruct((ROWS, HALF), BF),
         grid_spec=pltpu.PrefetchScalarGridSpec(
             num_scalar_prefetch=1,
             grid=(),
-            in_specs=[VMEM] * 4,
-            out_specs=pl.BlockSpec(memory_space=pl.ANY),
-            scratch_shapes=[pltpu.SemaphoreType.DMA((16,))],
+            in_specs=[VMEM] * len(ds) + ([] if out is None else [anywhere]),
+            out_specs=anywhere,
+            scratch_shapes=[pltpu.SemaphoreType.DMA((4 * len(ds),))],
         ),
-        compiler_params=PARAMS,
-        cost_estimate=cost(0, 4_000_000),
-    )(place, *blocks)
+        input_output_aliases={} if out is None else {len(operands) - 1: 0},
+        compiler_params=PARAMS,
+        cost_estimate=cost(0, 1_000_000 * len(ds)),
+    )(*operands)
 
 
 def after(values, *others):
@@ -314,48 +357,59 @@
     both = group_order(place, after(shares, mine))
 
     f, b = shift_z(both, 1), shift_z(both, -1)
+    sends = after(sends, both)
+    blocks = [mine] + [shift_g(sends[d - 1], d) for d in (1, 2, 3)]
     f2, b2 = shift_z(f, 1), shift_z(b, -1)
-    sends[:2] = after(sends[:2], f)
+    pieces = [both, b, f, b2, f2]
+    early = part_early(after(pieces, *blocks[1:]))
     f3, b3 = shift_z(f2, 1), shift_z(b2, -1)
-    sends[2:] = after(sends[2:], f2)
+    ef, eb = shift_p(early, 1), shift_p(early, -1)
     half = both.shape[0] // 2
-    far = [shift_z(b3[:half], -1), shift_z(f3[half:], 1)]
-    blocks = [mine] + [shift_g(sends[d - 1], d) for d in (1, 2, 3)]
-    cyc, win = part([both, b, b2, b3, *far, f3, f2, f])
-    [cyc] = after([cyc], *blocks)
-
-    cf, cb = shift_p(cyc, 1), shift_p(cyc, -1)
-    half = cyc.shape[0] // 2
-    far = [shift_p(cb[:half], -1), shift_p(cf[half:], 1)]
+    pieces += [b3, f3, shift_z(b3[:half], -1), shift_z(f3[half:], 1)]
+    late, win = part_late(pieces)
+    lf, lb = shift_p(late, 1), shift_p(late, -1)
+    half = EARLY // 2
+    early = [early, eb, shift_p(eb[:half], -1), shift_p(ef[half:], 1), ef]
+    half = LATE // 2
+    late = [late, lb, shift_p(lb[:half], -1), shift_p(lf[half:], 1), lf]
 
     here = lax.broadcasted_iota(jnp.int32, (QW, 1), 0)
-    turn, spot, hg, hw = here // 256, here // 32 % 8, here // 8 % 4, here % 8
-    turn = jnp.where(turn == 2, 3, jnp.where(turn == 3, 2, turn))
+    rest = here - 4 * EARLY
+    soon = rest < 0
+    turn = jnp.where(soon, here // EARLY, rest // LATE)
+    spot = jnp.where(soon, here % EARLY // 32, EARLY // 32 + rest % LATE // 32)
+    hg, hw = here // 8 % 4, here % 8
     turn_here = (hg - p) % 4
-    turn_here = jnp.where(turn_here == 2, 3, jnp.where(turn_here == 3, 2, turn_here))
+    at = jnp.where(soon, turn_here * EARLY, 4 * EARLY + turn_here * LATE - EARLY) + spot * 32
     there = lax.broadcasted_iota(jnp.int32, (1, QW), 1)
-    order = (turn_here * 256 + spot * 32 + (g + turn) % 4 * 8 + hw == there).astype(BF)
+    order = (at + (g + turn) % 4 * 8 + hw == there).astype(BF)
     hp = (p + turn) % 4
     hx, hy = jnp.where(core == 0, hg, hp), jnp.where(core == 0, hp, hg)
+    hz = (z + jnp.where(spot % 2 == 1, (spot + 1) // 2, 8 - spot // 2)) % NZ
     there = lax.broadcasted_iota(jnp.int32, (1, QW // 2), 1) + core * (QW // 2)
-    final = (hx * 256 + hy * 64 + (z + spot) % NZ * 8 + hw == there).astype(BF)
-
-    away, own = dressed_first(blocks, [cyc, cb, cf])
-    [win] = after([win], own)
+    final = (hx * 256 + hy * 64 + hz * 8 + hw == there).astype(BF)
+
+    away, own = dressed_first(blocks, early)
+    [win] = after([win], late[2])
     wf, wb = shift_p(win, 1), shift_p(win, -1)
-    *away, total = dressed_last(blocks, far, away, own)
+    *away, total = dressed_last(blocks, late, away, own)
     back = [shift_g(away[d - 1], -d) for d in (1, 2, 3)]
     for value in back:
         total = total + value.astype(F32)
     inner = inner_call(total, swap_core(total), order)
     inners = [shift_g(inner, d) for d in (1, 2, 3)]
-    rights = [win, wb, wf, shift_p(wb[:half], -1), shift_p(wf[half:], 1)]
+    half = win.shape[0] // 2
+    rights = [win, wb, shift_p(wb[:half], -1), shift_p(wf[half:], 1), wf]
     dressed = jnp.dot(inner, final, preferred_element_type=F32).astype(BF)
 
-    outs = quadratic_blocks(inners, rights)
-    outs = [shift_g(outs[d - 1], -d) for d in (1, 2, 3)]
-    outs = list(quadratic_blocks([inner], rights)) + outs
-    return (dressed, place_blocks(place, outs))
+    outs = {}
+    for d in (2, 1, 3):
+        [value] = quadratic_blocks([inners[d - 1]], rights)
+        outs[d] = shift_g(value, -d)
+    [outs[0]] = quadratic_blocks([inner], rights)
+    quadratic = place_blocks(place, {d: outs[d] for d in (0, 1, 2)})
+    quadratic = place_blocks(place, {3: outs[3]}, quadratic)
+    return (dressed, quadratic)
 
 
 def solution(mesh):

time: 142 us -> 135 us (0.951)
  waiting for transfers between devices: 70.5 us -> 45.9 us
  starting transfers between devices: 48.3 us -> 62.4 us
  Pallas kernels: 16.3 us -> 19.7 us
    ppermute x23 -> x27, waiting for transfers between devices: 53.9 us -> 35.2 us  [shift_plane(): return lax.ppermute(value, AX, pairs)]
    ppermute x23 -> x27, starting transfers between devices: 33.4 us -> 45.4 us  [shift_plane(): return lax.ppermute(value, AX, pairs)]
    ppermute x8, waiting for transfers between devices: 16.6 us -> 10.8 us  [shift_z(): lax.ppermute(value, AX, [(ident(x, y, z, c), ident(x, y, z + step, c)) fo...]
    ppermute x8, starting transfers between devices: 14.8 us -> 16.9 us  [shift_z(): lax.ppermute(value, AX, [(ident(x, y, z, c), ident(x, y, z + step, c)) fo...]
    pallas_call x3 -> x5, Pallas kernels: 5.3 us -> 7.34 us  [the longest x2 5.37 us: place_blocks(): pl.pallas_call(functools.partial(place_kernel, ds), out_shape=jax.ShapeDt...]
    pallas_call x2 -> x4, Pallas kernels: 3.63 us -> 5.31 us  [quadratic_blocks(): pl.pallas_call(functools.partial(quadratic_kernel, count), out_shape=[jax...]
  transfers between devices with their start and end apart: 32 -> 36, of which waited for: 18 -> 17; matrix products, arithmetic and copies ran while one was open for 1% -> 2% of each run, Pallas kernels for 5% -> 11%
where the time goes in v6:
time: 135 us; the launch traced here: 133 us
  starting transfers between devices  62.4 us (46%)
  waiting for transfers between devices  45.9 us (34%)
  Pallas kernels  19.7 us (15%)
  local copies, waits for them, and re-layouts  2.27 us (2%)
    ppermute x27, starting transfers between devices, shift_plane(): return lax.ppermute(value, AX, pairs)  45.4 us
    ppermute x27, waiting for transfers between devices, shift_plane(): return lax.ppermute(value, AX, pairs)  35.2 us
    ppermute x8, starting transfers between devices, shift_z(): lax.ppermute(value, AX, [(ident(x, y, z, c), ident(x, y, z + step, c)) fo...  16.9 us
    ppermute x8, waiting for transfers between devices, shift_z(): lax.ppermute(value, AX, [(ident(x, y, z, c), ident(x, y, z + step, c)) fo...  10.8 us
    pallas_call x2, Pallas kernels, place_blocks(): pl.pallas_call(functools.partial(place_kernel, ds), out_shape=jax.ShapeDt...  5.37 us
    pallas_call x4, Pallas kernels, quadratic_blocks(): pl.pallas_call(functools.partial(quadratic_kernel, count), out_shape=[jax...  5.31 us
  transfers between devices with their start and end apart: 36, of which 17 were waited for; matrix products, arithmetic and copies ran while one was open for 2% of the time, Pallas kernels for 11%

profile of v6, /device:TPU:0, one launch (start us, length us, event | category | flops | bytes accessed | tf_op | source)
XLA Modules:
  0.0 133.3 jit_solution(14276918290225714107)
XLA Ops:
  7.6 2.3 %collective-permute-done.1.refs_2_ = bf16[16,2048]{1,0:T(8,128)(2,1)S(1)} collective-permute-done((bf16[16,2048]{1,0:T(8,128)(2,1)}, bf16[16,2048]{1,0:T(8,128)(2,1)S(1)}, u32[]{:S(2)}, u32[]{:S(2)}) %collective-permute-start.1) | collective-permute-done | bytes 65568 | tf_op jit(solution)/shard_map/ppermute | solution.py:45
  11.4 5.9 %collective-permute-start.6 = (bf16[64,2048]{1,0:T(8,128)(2,1)S(1)}, bf16[64,2048]{1,0:T(8,128)(2,1)S(1)}, u32[]{:S(2)}, u32[]{:S(2)}) collective-permute-start(bf16[64,2048]{1,0:T(8,128)(2,1)S(1)} %shard_map.61.refs_0_), channel_id=1, source_target_pairs={{0,14},{1,15},{2,0},{3,1},{4,2},{5,3},{6,4},{7,5},{8,6},{9,7},{10,... | collective-permute-start | bytes 786440 | tf_op jit(solution)/shard_map/ppermute | solution.py:35
  22.0 3.7 %collective-permute-start.8 = (bf16[64,2048]{1,0:T(8,128)(2,1)S(1)}, bf16[64,2048]{1,0:T(8,128)(2,1)S(1)}, u32[]{:S(2)}, u32[]{:S(2)}) collective-permute-start(bf16[64,2048]{1,0:T(8,128)(2,1)S(1)} %collective-permute-done.6.refs_1_), channel_id=1, source_target_pairs={{0,14},{1,15},{2,0},{3,1},{4,2},{5,3},{6,4},{7,5},{8,6},{9,7},{10,... | collective-permute-start | bytes 786440 | tf_op jit(solution)/shard_map/ppermute | solution.py:35
  25.7 3.9 %collective-permute-done.8.refs_3_ = bf16[64,2048]{1,0:T(8,128)(2,1)S(1)} collective-permute-done((bf16[64,2048]{1,0:T(8,128)(2,1)S(1)}, bf16[64,2048]{1,0:T(8,128)(2,1)S(1)}, u32[]{:S(2)}, u32[]{:S(2)}) %collective-permute-start.8) | collective-permute-done | bytes 262176 | tf_op jit(solution)/shard_map/ppermute | solution.py:35
  29.6 3.7 %collective-permute-start.10 = (bf16[64,2048]{1,0:T(8,128)(2,1)S(1)}, bf16[64,2048]{1,0:T(8,128)(2,1)S(1)}, u32[]{:S(2)}, u32[]{:S(2)}) collective-permute-start(bf16[64,2048]{1,0:T(8,128)(2,1)S(1)} %collective-permute-done.8.refs_3_), channel_id=1, source_target_pairs={{0,14},{1,15},{2,0},{3,1},{4,2},{5,3},{6,4},{7,5},{8,6},{9,7},{10,... | collective-permute-start | bytes 786440 | tf_op jit(solution)/shard_map/ppermute | solution.py:35
  34.3 5.0 %collective-permute-start.18 = (bf16[160,2048]{1,0:T(8,128)(2,1)S(1)}, bf16[160,2048]{1,0:T(8,128)(2,1)S(1)}, u32[]{:S(2)}, u32[]{:S(2)}) collective-permute-start(bf16[160,2048]{1,0:T(8,128)(2,1)S(1)} %shard_map.63.refs_4_), channel_id=1, source_target_pairs={{0,48},{1,193},{2,50},{3,195},{4,52},{5,197},{6,54},{7,199},{8,56}... | collective-permute-start | bytes 1966088 | tf_op jit(solution)/shard_map/ppermute | solution.py:45
  39.3 3.3 %collective-permute-start.12 = (bf16[32,2048]{1,0:T(8,128)(2,1)S(1)}, bf16[32,2048]{1,0:T(8,128)(2,1)S(1)}, u32[]{:S(2)}, u32[]{:S(2)}) collective-permute-start(bf16[32,2048]{1,0:T(8,128)(2,1)S(1)} %slice.32), channel_id=1, source_target_pairs={{0,14},{1,15},{2,0},{3,1},{4,2},{5,3},{6,4},{7,5},{8,6},{9,7},{10,... | collective-permute-start | bytes 393224 | tf_op jit(solution)/shard_map/ppermute | solution.py:35
  42.9 2.2 %collective-permute-done.12.refs_7_ = bf16[32,2048]{1,0:T(8,128)(2,1)S(1)} collective-permute-done((bf16[32,2048]{1,0:T(8,128)(2,1)S(1)}, bf16[32,2048]{1,0:T(8,128)(2,1)S(1)}, u32[]{:S(2)}, u32[]{:S(2)}) %collective-permute-start.12) | collective-permute-done | bytes 131104 | tf_op jit(solution)/shard_map/ppermute | solution.py:35
  45.1 3.9 %collective-permute-done.13.refs_8_ = bf16[32,2048]{1,0:T(8,128)(2,1)S(1)} collective-permute-done((bf16[32,2048]{1,0:T(8,128)(2,1)S(1)}, bf16[32,2048]{1,0:T(8,128)(2,1)S(1)}, u32[]{:S(2)}, u32[]{:S(2)}) %collective-permute-start.13) | collective-permute-done | bytes 131104 | tf_op jit(solution)/shard_map/ppermute | solution.py:35
  49.1 5.3 %collective-permute-start.14 = (bf16[96,2048]{1,0:T(8,128)(2,1)S(1)}, bf16[96,2048]{1,0:T(8,128)(2,1)S(1)}, u32[]{:S(2)}, u32[]{:S(2)}) collective-permute-start(bf16[96,2048]{1,0:T(8,128)(2,1)S(1)} %get-tuple-element.48.refs_4_), channel_id=1, source_target_pairs={{0,48},{1,193},{2,50},{3,195},{4,52},{5,197},{6,54},{7,199},{8,56}... | collective-permute-start | bytes 1179656 | tf_op jit(solution)/shard_map/ppermute | solution.py:45
  54.4 3.3 %collective-permute-start.19 = (bf16[80,2048]{1,0:T(8,128)(2,1)S(1)}, bf16[80,2048]{1,0:T(8,128)(2,1)S(1)}, u32[]{:S(2)}, u32[]{:S(2)}) collective-permute-start(bf16[80,2048]{1,0:T(8,128)(2,1)S(1)} %slice.36), channel_id=1, source_target_pairs={{0,48},{1,193},{2,50},{3,195},{4,52},{5,197},{6,54},{7,199},{8,56}... | collective-permute-start | bytes 983048 | tf_op jit(solution)/shard_map/ppermute | solution.py:45
  59.7 3.8 %collective-permute-start.15 = (bf16[48,2048]{1,0:T(8,128)(2,1)S(1)}, bf16[48,2048]{1,0:T(8,128)(2,1)S(1)}, u32[]{:S(2)}, u32[]{:S(2)}) collective-permute-start(bf16[48,2048]{1,0:T(8,128)(2,1)S(1)} %slice.34), channel_id=1, source_target_pairs={{0,48},{1,193},{2,50},{3,195},{4,52},{5,197},{6,54},{7,199},{8,56}... | collective-permute-start | bytes 589832 | tf_op jit(solution)/shard_map/ppermute | solution.py:45
  63.6 3.1 %collective-permute-done.15.refs_6_ = bf16[48,2048]{1,0:T(8,128)(2,1)S(1)} collective-permute-done((bf16[48,2048]{1,0:T(8,128)(2,1)S(1)}, bf16[48,2048]{1,0:T(8,128)(2,1)S(1)}, u32[]{:S(2)}, u32[]{:S(2)}) %collective-permute-start.15) | collective-permute-done | bytes 196640 | tf_op jit(solution)/shard_map/ppermute | solution.py:45
  66.7 3.7 %collective-permute-start.27 = (bf16[256,2048]{1,0:T(8,128)(2,1)S(1)}, bf16[256,2048]{1,0:T(8,128)(2,1)S(1)}, u32[]{:S(2)}, u32[]{:S(2)}) collective-permute-start(bf16[256,2048]{1,0:T(8,128)(2,1)S(1)} %get-tuple-element.61.refs_1_), channel_id=1, source_target_pairs={{0,48},{1,193},{2,50},{3,195},{4,52},{5,197},{6,54},{7,199},{8,56}... | collective-permute-start | bytes 3145736 | tf_op jit(solution)/shard_map/ppermute | solution.py:45
  75.6 4.3 %collective-permute-done.22 = bf16[128,1024]{1,0:T(8,128)(2,1)S(1)} collective-permute-done((bf16[128,1024]{1,0:T(8,128)(2,1)S(1)}, bf16[128,1024]{1,0:T(8,128)(2,1)S(1)}, u32[]{:S(2)}, u32[]{:S(2)}) %collective-permute-start.22) | collective-permute-done | bytes 262176 | tf_op jit(solution)/shard_map/ppermute | solution.py:45
  81.7 2.9 %collective-permute-done.24 = bf16[128,1024]{1,0:T(8,128)(2,1)S(1)} collective-permute-done((bf16[128,1024]{1,0:T(8,128)(2,1)S(1)}, bf16[128,1024]{1,0:T(8,128)(2,1)S(1)}, u32[]{:S(2)}, u32[]{:S(2)}) %collective-permute-start.24) | collective-permute-done | bytes 262176 | tf_op jit(solution)/shard_map/ppermute | solution.py:45
  86.6 2.9 %collective-permute-start.28 = (bf16[128,2048]{1,0:T(8,128)(2,1)S(1)}, bf16[128,2048]{1,0:T(8,128)(2,1)S(1)}, u32[]{:S(2)}, u32[]{:S(2)}) collective-permute-start(bf16[128,2048]{1,0:T(8,128)(2,1)S(1)} %slice.38), channel_id=1, source_target_pairs={{0,48},{1,193},{2,50},{3,195},{4,52},{5,197},{6,54},{7,199},{8,56}... | collective-permute-start | bytes 1572872 | tf_op jit(solution)/shard_map/ppermute | solution.py:45
  94.8 4.3 %collective-permute-done.34.refs_0_ = bf16[128,1024]{1,0:T(8,128)(2,1)S(1)} collective-permute-done((bf16[128,1024]{1,0:T(8,128)(2,1)S(1)}, bf16[128,1024]{1,0:T(8,128)(2,1)S(1)}, u32[]{:S(2)}, u32[]{:S(2)}) %collective-permute-start.34) | collective-permute-done | bytes 262176 | tf_op jit(solution)/shard_map/ppermute | solution.py:45
  99.1 2.7 %collective-permute-done.28.refs_3_ = bf16[128,2048]{1,0:T(8,128)(2,1)S(1)} collective-permute-done((bf16[128,2048]{1,0:T(8,128)(2,1)S(1)}, bf16[128,2048]{1,0:T(8,128)(2,1)S(1)}, u32[]{:S(2)}, u32[]{:S(2)}) %collective-permute-start.28) | collective-permute-done | bytes 524320 | tf_op jit(solution)/shard_map/ppermute | solution.py:45
  101.8 2.6 %collective-permute-done.30.refs_4_ = bf16[128,2048]{1,0:T(8,128)(2,1)S(1)} collective-permute-done((bf16[128,2048]{1,0:T(8,128)(2,1)S(1)}, bf16[128,2048]{1,0:T(8,128)(2,1)S(1)}, u32[]{:S(2)}, u32[]{:S(2)}) %collective-permute-start.30) | collective-permute-done | bytes 524320 | tf_op jit(solution)/shard_map/ppermute | solution.py:45
  106.0 6.3 %collective-permute-start.35 = (bf16[128,2048]{1,0:T(8,128)(2,1)}, bf16[128,2048]{1,0:T(8,128)(2,1)}, u32[]{:S(2)}, u32[]{:S(2)}) collective-permute-start(bf16[128,2048]{1,0:T(8,128)(2,1)} %shard_map.70), channel_id=1, source_target_pairs={{0,128},{1,33},{2,130},{3,35},{4,132},{5,37},{6,134},{7,39},{8,136... | collective-permute-start | bytes 1572872 | tf_op jit(solution)/shard_map/ppermute | solution.py:45
  121.8 6.0 %collective-permute-done.33.refs_1_ = bf16[128,2048]{1,0:T(8,128)(2,1)} collective-permute-done((bf16[128,2048]{1,0:T(8,128)(2,1)}, bf16[128,2048]{1,0:T(8,128)(2,1)}, u32[]{:S(2)}, u32[]{:S(2)}) %collective-permute-start.33) | collective-permute-done | bytes 524320 | tf_op jit(solution)/shard_map/ppermute | solution.py:45
  127.7 3.0 %shard_map.71.refs_1_ = bf16[128,8192]{1,0:T(8,128)(2,1)} custom-call(s32[4]{0:T(128)S(1)} %pad_add_fusion.place, bf16[128,2048]{1,0:T(8,128)(2,1)S(1)} %shard_map.68.refs_0_, bf16[128,2048]{1,0:T(8,128)(2,1)} %collective-permute-done.33.refs_1_, bf16[128,2048]{1,0:T(8,128)(2,1)} %collective-permute-done.35.refs_2_), custom_call_target="tpu_custom_call" | custom-call | bytes 3000000 | tf_op jit(solution)/shard_map/pallas_call | solution.py:325
  130.7 2.4 %shard_map.72 = bf16[128,8192]{1,0:T(8,128)(2,1)} custom-call(s32[4]{0:T(128)S(1)} %pad_add_fusion.place, bf16[128,2048]{1,0:T(8,128)(2,1)} %collective-permute-done.31.refs_0_, bf16[128,8192]{1,0:T(8,128)(2,1)} %shard_map.71.refs_1_), custom_call_target="tpu_custom_call", output_to_operand_aliasing={{}: (2, {})} | custom-call | bytes 1000000 | tf_op jit(solution)/shard_map/pallas_call | solution.py:325
  (91 shorter events, 41.8 us)
Async XLA Ops:
  11.4 10.6 %collective-permute-start.6 = (bf16[64,2048]{1,0:T(8,128)(2,1)S(1)}, bf16[64,2048]{1,0:T(8,128)(2,1)S(1)}, u32[]{:S(2)}, u32[]{:S(2)}) collective-permute-start(bf16[64,2048]{1,0:T(8,128)(2,1)S(1)} %shard_map.61.refs_0_), channel_id=1, source_target_pairs={{0,14},{1,15},{2,0},{3,1},{4,2},{5,3},{6,4},{7,5},{8,6},{9,7},{10,... | collective-permute-start | bytes 786440 | tf_op jit(solution)/shard_map/ppermute | solution.py:35
  17.3 8.4 %collective-permute-start.7 = (bf16[64,2048]{1,0:T(8,128)(2,1)S(1)}, bf16[64,2048]{1,0:T(8,128)(2,1)S(1)}, u32[]{:S(2)}, u32[]{:S(2)}) collective-permute-start(bf16[64,2048]{1,0:T(8,128)(2,1)S(1)} %shard_map.61.refs_0_), channel_id=1, source_target_pairs={{0,2},{1,3},{2,4},{3,5},{4,6},{5,7},{6,8},{7,9},{8,10},{9,11},{10,... | collective-permute-start | bytes 786440 | tf_op jit(solution)/shard_map/ppermute | solution.py:35
  17.3 16.0 %collective-permute-start.3 = (bf16[128,2048]{1,0:T(8,128)(2,1)S(1)}, bf16[128,2048]{1,0:T(8,128)(2,1)S(1)}, u32[]{:S(2)}, u32[]{:S(2)}) collective-permute-start(bf16[128,2048]{1,0:T(8,128)(2,1)S(1)} %get-tuple-element.45), channel_id=1, source_target_pairs={{0,64},{1,17},{2,66},{3,19},{4,68},{5,21},{6,70},{7,23},{8,72},{9,... | collective-permute-start | bytes 1572872 | tf_op jit(solution)/shard_map/ppermute | solution.py:45
  17.3 16.0 %collective-permute-start.4 = (bf16[128,2048]{1,0:T(8,128)(2,1)S(1)}, bf16[128,2048]{1,0:T(8,128)(2,1)S(1)}, u32[]{:S(2)}, u32[]{:S(2)}) collective-permute-start(bf16[128,2048]{1,0:T(8,128)(2,1)S(1)} %get-tuple-element.46), channel_id=1, source_target_pairs={{0,128},{1,33},{2,130},{3,35},{4,132},{5,37},{6,134},{7,39},{8,136... | collective-permute-start | bytes 1572872 | tf_op jit(solution)/shard_map/ppermute | solution.py:45
  19.3 14.9 %collective-permute-start.5 = (bf16[128,2048]{1,0:T(8,128)(2,1)S(1)}, bf16[128,2048]{1,0:T(8,128)(2,1)S(1)}, u32[]{:S(2)}, u32[]{:S(2)}) collective-permute-start(bf16[128,2048]{1,0:T(8,128)(2,1)S(1)} %get-tuple-element.47), channel_id=1, source_target_pairs={{0,192},{1,49},{2,194},{3,51},{4,196},{5,53},{6,198},{7,55},{8,200... | collective-permute-start | bytes 1572872 | tf_op jit(solution)/shard_map/ppermute | solution.py:45
  29.6 9.7 %collective-permute-start.10 = (bf16[64,2048]{1,0:T(8,128)(2,1)S(1)}, bf16[64,2048]{1,0:T(8,128)(2,1)S(1)}, u32[]{:S(2)}, u32[]{:S(2)}) collective-permute-start(bf16[64,2048]{1,0:T(8,128)(2,1)S(1)} %collective-permute-done.8.refs_3_), channel_id=1, source_target_pairs={{0,14},{1,15},{2,0},{3,1},{4,2},{5,3},{6,4},{7,5},{8,6},{9,7},{10,... | collective-permute-start | bytes 786440 | tf_op jit(solution)/shard_map/ppermute | solution.py:35
  33.3 9.3 %collective-permute-start.11 = (bf16[64,2048]{1,0:T(8,128)(2,1)S(1)}, bf16[64,2048]{1,0:T(8,128)(2,1)S(1)}, u32[]{:S(2)}, u32[]{:S(2)}) collective-permute-start(bf16[64,2048]{1,0:T(8,128)(2,1)S(1)} %collective-permute-done.9.refs_4_), channel_id=1, source_target_pairs={{0,2},{1,3},{2,4},{3,5},{4,6},{5,7},{6,8},{7,9},{8,10},{9,11},{10,... | collective-permute-start | bytes 786440 | tf_op jit(solution)/shard_map/ppermute | solution.py:35
  34.3 20.1 %collective-permute-start.18 = (bf16[160,2048]{1,0:T(8,128)(2,1)S(1)}, bf16[160,2048]{1,0:T(8,128)(2,1)S(1)}, u32[]{:S(2)}, u32[]{:S(2)}) collective-permute-start(bf16[160,2048]{1,0:T(8,128)(2,1)S(1)} %shard_map.63.refs_4_), channel_id=1, source_target_pairs={{0,48},{1,193},{2,50},{3,195},{4,52},{5,197},{6,54},{7,199},{8,56}... | collective-permute-start | bytes 1966088 | tf_op jit(solution)/shard_map/ppermute | solution.py:45
  39.3 18.5 %collective-permute-start.20 = (bf16[160,2048]{1,0:T(8,128)(2,1)S(1)}, bf16[160,2048]{1,0:T(8,128)(2,1)S(1)}, u32[]{:S(2)}, u32[]{:S(2)}) collective-permute-start(bf16[160,2048]{1,0:T(8,128)(2,1)S(1)} %shard_map.63.refs_4_), channel_id=1, source_target_pairs={{0,16},{1,65},{2,18},{3,67},{4,20},{5,69},{6,22},{7,71},{8,24},{9,... | collective-permute-start | bytes 1966088 | tf_op jit(solution)/shard_map/ppermute | solution.py:45
  49.1 10.6 %collective-permute-start.14 = (bf16[96,2048]{1,0:T(8,128)(2,1)S(1)}, bf16[96,2048]{1,0:T(8,128)(2,1)S(1)}, u32[]{:S(2)}, u32[]{:S(2)}) collective-permute-start(bf16[96,2048]{1,0:T(8,128)(2,1)S(1)} %get-tuple-element.48.refs_4_), channel_id=1, source_target_pairs={{0,48},{1,193},{2,50},{3,195},{4,52},{5,197},{6,54},{7,199},{8,56}... | collective-permute-start | bytes 1179656 | tf_op jit(solution)/shard_map/ppermute | solution.py:45
  54.4 9.1 %collective-permute-start.16 = (bf16[96,2048]{1,0:T(8,128)(2,1)S(1)}, bf16[96,2048]{1,0:T(8,128)(2,1)S(1)}, u32[]{:S(2)}, u32[]{:S(2)}) collective-permute-start(bf16[96,2048]{1,0:T(8,128)(2,1)S(1)} %get-tuple-element.48.refs_4_), channel_id=1, source_target_pairs={{0,16},{1,65},{2,18},{3,67},{4,20},{5,69},{6,22},{7,71},{8,24},{9,... | collective-permute-start | bytes 1179656 | tf_op jit(solution)/shard_map/ppermute | solution.py:45
  54.4 15.9 %collective-permute-start.19 = (bf16[80,2048]{1,0:T(8,128)(2,1)S(1)}, bf16[80,2048]{1,0:T(8,128)(2,1)S(1)}, u32[]{:S(2)}, u32[]{:S(2)}) collective-permute-start(bf16[80,2048]{1,0:T(8,128)(2,1)S(1)} %slice.36), channel_id=1, source_target_pairs={{0,48},{1,193},{2,50},{3,195},{4,52},{5,197},{6,54},{7,199},{8,56}... | collective-permute-start | bytes 983048 | tf_op jit(solution)/shard_map/ppermute | solution.py:45
  57.8 12.6 %collective-permute-start.21 = (bf16[80,2048]{1,0:T(8,128)(2,1)S(1)}, bf16[80,2048]{1,0:T(8,128)(2,1)S(1)}, u32[]{:S(2)}, u32[]{:S(2)}) collective-permute-start(bf16[80,2048]{1,0:T(8,128)(2,1)S(1)} %slice.37), channel_id=1, source_target_pairs={{0,16},{1,65},{2,18},{3,67},{4,20},{5,69},{6,22},{7,71},{8,24},{9,... | collective-permute-start | bytes 983048 | tf_op jit(solution)/shard_map/ppermute | solution.py:45
  63.5 8.7 %collective-permute-start.17 = (bf16[48,2048]{1,0:T(8,128)(2,1)S(1)}, bf16[48,2048]{1,0:T(8,128)(2,1)S(1)}, u32[]{:S(2)}, u32[]{:S(2)}) collective-permute-start(bf16[48,2048]{1,0:T(8,128)(2,1)S(1)} %slice.35), channel_id=1, source_target_pairs={{0,16},{1,65},{2,18},{3,67},{4,20},{5,69},{6,22},{7,71},{8,24},{9,... | collective-permute-start | bytes 589832 | tf_op jit(solution)/shard_map/ppermute | solution.py:45
  66.7 19.9 %collective-permute-start.27 = (bf16[256,2048]{1,0:T(8,128)(2,1)S(1)}, bf16[256,2048]{1,0:T(8,128)(2,1)S(1)}, u32[]{:S(2)}, u32[]{:S(2)}) collective-permute-start(bf16[256,2048]{1,0:T(8,128)(2,1)S(1)} %get-tuple-element.61.refs_1_), channel_id=1, source_target_pairs={{0,48},{1,193},{2,50},{3,195},{4,52},{5,197},{6,54},{7,199},{8,56}... | collective-permute-start | bytes 3145736 | tf_op jit(solution)/shard_map/ppermute | solution.py:45
  70.4 19.2 %collective-permute-start.29 = (bf16[256,2048]{1,0:T(8,128)(2,1)S(1)}, bf16[256,2048]{1,0:T(8,128)(2,1)S(1)}, u32[]{:S(2)}, u32[]{:S(2)}) collective-permute-start(bf16[256,2048]{1,0:T(8,128)(2,1)S(1)} %get-tuple-element.61.refs_1_), channel_id=1, source_target_pairs={{0,16},{1,65},{2,18},{3,67},{4,20},{5,69},{6,22},{7,71},{8,24},{9,... | collective-permute-start | bytes 3145736 | tf_op jit(solution)/shard_map/ppermute | solution.py:45
  73.7 10.9 %collective-permute-start.24 = (bf16[128,1024]{1,0:T(8,128)(2,1)S(1)}, bf16[128,1024]{1,0:T(8,128)(2,1)S(1)}, u32[]{:S(2)}, u32[]{:S(2)}) collective-permute-start(bf16[128,1024]{1,0:T(8,128)(2,1)S(1)} %get-tuple-element.59), channel_id=1, source_target_pairs={{0,64},{1,17},{2,66},{3,19},{4,68},{5,21},{6,70},{7,23},{8,72},{9,... | collective-permute-start | bytes 786440 | tf_op jit(solution)/shard_map/ppermute | solution.py:45
  86.6 15.2 %collective-permute-start.28 = (bf16[128,2048]{1,0:T(8,128)(2,1)S(1)}, bf16[128,2048]{1,0:T(8,128)(2,1)S(1)}, u32[]{:S(2)}, u32[]{:S(2)}) collective-permute-start(bf16[128,2048]{1,0:T(8,128)(2,1)S(1)} %slice.38), channel_id=1, source_target_pairs={{0,48},{1,193},{2,50},{3,195},{4,52},{5,197},{6,54},{7,199},{8,56}... | collective-permute-start | bytes 1572872 | tf_op jit(solution)/shard_map/ppermute | solution.py:45
  89.6 14.9 %collective-permute-start.30 = (bf16[128,2048]{1,0:T(8,128)(2,1)S(1)}, bf16[128,2048]{1,0:T(8,128)(2,1)S(1)}, u32[]{:S(2)}, u32[]{:S(2)}) collective-permute-start(bf16[128,2048]{1,0:T(8,128)(2,1)S(1)} %slice.39), channel_id=1, source_target_pairs={{0,16},{1,65},{2,18},{3,67},{4,20},{5,69},{6,22},{7,71},{8,24},{9,... | collective-permute-start | bytes 1572872 | tf_op jit(solution)/shard_map/ppermute | solution.py:45
  91.6 20.7 %collective-permute-start.32 = (bf16[128,1024]{1,0:T(8,128)(2,1)S(1)}, bf16[128,1024]{1,0:T(8,128)(2,1)S(1)}, u32[]{:S(2)}, u32[]{:S(2)}) collective-permute-start(bf16[128,1024]{1,0:T(8,128)(2,1)S(1)} %shard_map.66.refs_0_), channel_id=1, source_target_pairs={{0,64},{1,17},{2,66},{3,19},{4,68},{5,21},{6,70},{7,23},{8,72},{9,... | collective-permute-start | bytes 786440 | tf_op jit(solution)/shard_map/ppermute | solution.py:45
  93.6 21.7 %collective-permute-start.26 = (bf16[128,1024]{1,0:T(8,128)(2,1)S(1)}, bf16[128,1024]{1,0:T(8,128)(2,1)S(1)}, u32[]{:S(2)}, u32[]{:S(2)}) collective-permute-start(bf16[128,1024]{1,0:T(8,128)(2,1)S(1)} %shard_map.66.refs_0_), channel_id=1, source_target_pairs={{0,192},{1,49},{2,194},{3,51},{4,196},{5,53},{6,198},{7,55},{8,200... | collective-permute-start | bytes 786440 | tf_op jit(solution)/shard_map/ppermute | solution.py:45
  106.0 15.8 %collective-permute-start.35 = (bf16[128,2048]{1,0:T(8,128)(2,1)}, bf16[128,2048]{1,0:T(8,128)(2,1)}, u32[]{:S(2)}, u32[]{:S(2)}) collective-permute-start(bf16[128,2048]{1,0:T(8,128)(2,1)} %shard_map.70), channel_id=1, source_target_pairs={{0,128},{1,33},{2,130},{3,35},{4,132},{5,37},{6,134},{7,39},{8,136... | collective-permute-start | bytes 1572872 | tf_op jit(solution)/shard_map/ppermute | solution.py:45
  113.8 14.0 %collective-permute-start.33 = (bf16[128,2048]{1,0:T(8,128)(2,1)}, bf16[128,2048]{1,0:T(8,128)(2,1)}, u32[]{:S(2)}, u32[]{:S(2)}) collective-permute-start(bf16[128,2048]{1,0:T(8,128)(2,1)} %shard_map.69), channel_id=1, source_target_pairs={{0,192},{1,49},{2,194},{3,51},{4,196},{5,53},{6,198},{7,55},{8,200... | collective-permute-start | bytes 1572872 | tf_op jit(solution)/shard_map/ppermute | solution.py:45
  116.8 13.9 %collective-permute-start.31 = (bf16[128,2048]{1,0:T(8,128)(2,1)}, bf16[128,2048]{1,0:T(8,128)(2,1)}, u32[]{:S(2)}, u32[]{:S(2)}) collective-permute-start(bf16[128,2048]{1,0:T(8,128)(2,1)} %shard_map.67), channel_id=1, source_target_pairs={{0,64},{1,17},{2,66},{3,19},{4,68},{5,21},{6,70},{7,23},{8,72},{9,... | collective-permute-start | bytes 1572872 | tf_op jit(solution)/shard_map/ppermute | solution.py:45
  (19 other events, 120.4 us)

commit v7 on v6

--- a/solution.py
+++ b/solution.py
@@ -303,18 +303,21 @@
 
 
 def place_kernel(ds, place, *refs):
-    ins, out, sem = refs[: len(ds)], refs[-2], refs[-1]
+    ins, out, held, sem = refs[: len(ds)], refs[-3], refs[-2], refs[-1]
+    chunks = [(k, slice(i * 32, i * 32 + 32)) for k in range(len(ds)) for i in range(4)]
     copies = []
-    for k, d in enumerate(ds):
-        at = pl.multiple_of(lax.rem(place[0] + d, 4) * PART, PART)
-        for i in range(4):
-            rows = slice(i * 32, i * 32 + 32)
-            copies.append(
-                pltpu.make_async_copy(ins[k].at[rows, :], out.at[rows, pl.ds(at, PART)], sem.at[k * 4 + i])
-            )
+    for n, (k, rows) in enumerate(chunks):
+        copies.append(pltpu.make_async_copy(ins[k].at[rows, :], held.at[k, rows, :], sem.at[n]))
     for copy in copies:
         copy.start()
-    for copy in copies:
+    later = []
+    for n, (k, rows) in enumerate(chunks):
+        at = pl.multiple_of(lax.rem(place[0] + ds[k], 4) * PART, PART)
+        copies[n].wait()
+        to = out.at[rows, pl.ds(at, PART)]
+        later.append(pltpu.make_async_copy(held.at[k, rows, :], to, sem.at[len(chunks) + n]))
+        later[-1].start()
+    for copy in later:
         copy.wait()
 
 
@@ -328,9 +331,12 @@
         grid_spec=pltpu.PrefetchScalarGridSpec(
             num_scalar_prefetch=1,
             grid=(),
-            in_specs=[VMEM] * len(ds) + ([] if out is None else [anywhere]),
+            in_specs=[anywhere] * (len(operands) - 1),
             out_specs=anywhere,
-            scratch_shapes=[pltpu.SemaphoreType.DMA((4 * len(ds),))],
+            scratch_shapes=[
+                pltpu.VMEM((len(ds), ROWS, PART), BF),
+                pltpu.SemaphoreType.DMA((8 * len(ds),)),
+            ],
         ),
         input_output_aliases={} if out is None else {len(operands) - 1: 0},
         compiler_params=PARAMS,
@@ -407,8 +413,9 @@
         [value] = quadratic_blocks([inners[d - 1]], rights)
         outs[d] = shift_g(value, -d)
     [outs[0]] = quadratic_blocks([inner], rights)
-    quadratic = place_blocks(place, {d: outs[d] for d in (0, 1, 2)})
-    quadratic = place_blocks(place, {3: outs[3]}, quadratic)
+    quadratic = place_blocks(place, {0: outs[0]})
+    quadratic = place_blocks(place, {2: outs[2]}, quadratic)
+    quadratic = place_blocks(place, {1: outs[1], 3: outs[3]}, quadratic)
     return (dressed, quadratic)
 
 

time: 135 us -> 130 us (0.963); the launches traced: 133 us -> 130 us
  waiting for transfers between devices: 45.9 us -> 43.2 us
  starting transfers between devices: 62.4 us -> 59.8 us
  Pallas kernels: 19.7 us -> 21.5 us
    ppermute x27, waiting for transfers between devices: 35.2 us -> 32.4 us  [shift_plane(): return lax.ppermute(value, AX, pairs)]
    ppermute x27, starting transfers between devices: 45.4 us -> 42.9 us  [shift_plane(): return lax.ppermute(value, AX, pairs)]
    pallas_call x2 -> x3, Pallas kernels: 5.37 us -> 7.06 us  [place_blocks(): pl.pallas_call(functools.partial(place_kernel, ds), out_shape=jax.ShapeDt...]
  transfers between devices with their start and end apart: 36 -> 36, of which waited for: 17 -> 18; matrix products, arithmetic and copies ran while one was open for 2% -> 2% of each run, Pallas kernels for 11% -> 12%
where the time goes in v7:
time: 130 us
  starting transfers between devices  59.8 us (46%)
  waiting for transfers between devices  43.2 us (33%)
  Pallas kernels  21.5 us (17%)
  local copies, waits for them, and re-layouts  2.27 us (2%)
    ppermute x27, starting transfers between devices, shift_plane(): return lax.ppermute(value, AX, pairs)  42.9 us
    ppermute x27, waiting for transfers between devices, shift_plane(): return lax.ppermute(value, AX, pairs)  32.4 us
    ppermute x8, starting transfers between devices, shift_z(): lax.ppermute(value, AX, [(ident(x, y, z, c), ident(x, y, z + step, c)) fo...  16.9 us
    ppermute x8, waiting for transfers between devices, shift_z(): lax.ppermute(value, AX, [(ident(x, y, z, c), ident(x, y, z + step, c)) fo...  10.8 us
    pallas_call x3, Pallas kernels, place_blocks(): pl.pallas_call(functools.partial(place_kernel, ds), out_shape=jax.ShapeDt...  7.06 us
    pallas_call x4, Pallas kernels, quadratic_blocks(): pl.pallas_call(functools.partial(quadratic_kernel, count), out_shape=[jax...  5.33 us
  transfers between devices with their start and end apart: 36, of which 18 were waited for; matrix products, arithmetic and copies ran while one was open for 2% of the time, Pallas kernels for 12%

profile of v7, /device:TPU:0, one launch (start us, length us, event | category | flops | bytes accessed | tf_op | source)
XLA Modules:
  0.0 129.8 jit_solution(4130278853326547664)
XLA Ops:
  0.7 2.2 %shard_map.59 = (bf16[16,2048]{1,0:T(8,128)(2,1)}, bf16[16,2048]{1,0:T(8,128)(2,1)}, bf16[16,2048]{1,0:T(8,128)(2,1)}, bf16[16,2048]{1,0:T(8,128)(2,1)}) custom-call(s32[128,128]{1,0:T(8,128)} %cyc_map_in.1, s32[1,64]{1,0:T(1,128)} %amp_map.1, bf16[8,8192]{1,0:T(8,128)(2,1)} %bitcast.6, bf16[128,8192]{1,0:T(8,128)(2,1)} %refs_3_), custom_call_target="tpu_custom_call" | custom-call | bytes 600000 | tf_op jit(solution)/shard_map/pallas_call | solution.py:91
  7.6 2.3 %collective-permute-done.1.refs_2_ = bf16[16,2048]{1,0:T(8,128)(2,1)S(1)} collective-permute-done((bf16[16,2048]{1,0:T(8,128)(2,1)}, bf16[16,2048]{1,0:T(8,128)(2,1)S(1)}, u32[]{:S(2)}, u32[]{:S(2)}) %collective-permute-start.1) | collective-permute-done | bytes 65568 | tf_op jit(solution)/shard_map/ppermute | solution.py:45
  11.4 5.9 %collective-permute-start.6 = (bf16[64,2048]{1,0:T(8,128)(2,1)S(1)}, bf16[64,2048]{1,0:T(8,128)(2,1)S(1)}, u32[]{:S(2)}, u32[]{:S(2)}) collective-permute-start(bf16[64,2048]{1,0:T(8,128)(2,1)S(1)} %shard_map.61.refs_0_), channel_id=1, source_target_pairs={{0,14},{1,15},{2,0},{3,1},{4,2},{5,3},{6,4},{7,5},{8,6},{9,7},{10,... | collective-permute-start | bytes 786440 | tf_op jit(solution)/shard_map/ppermute | solution.py:35
  22.0 3.7 %collective-permute-start.8 = (bf16[64,2048]{1,0:T(8,128)(2,1)S(1)}, bf16[64,2048]{1,0:T(8,128)(2,1)S(1)}, u32[]{:S(2)}, u32[]{:S(2)}) collective-permute-start(bf16[64,2048]{1,0:T(8,128)(2,1)S(1)} %collective-permute-done.6.refs_1_), channel_id=1, source_target_pairs={{0,14},{1,15},{2,0},{3,1},{4,2},{5,3},{6,4},{7,5},{8,6},{9,7},{10,... | collective-permute-start | bytes 786440 | tf_op jit(solution)/shard_map/ppermute | solution.py:35
  25.7 3.9 %collective-permute-done.8.refs_3_ = bf16[64,2048]{1,0:T(8,128)(2,1)S(1)} collective-permute-done((bf16[64,2048]{1,0:T(8,128)(2,1)S(1)}, bf16[64,2048]{1,0:T(8,128)(2,1)S(1)}, u32[]{:S(2)}, u32[]{:S(2)}) %collective-permute-start.8) | collective-permute-done | bytes 262176 | tf_op jit(solution)/shard_map/ppermute | solution.py:35
  29.6 3.7 %collective-permute-start.10 = (bf16[64,2048]{1,0:T(8,128)(2,1)S(1)}, bf16[64,2048]{1,0:T(8,128)(2,1)S(1)}, u32[]{:S(2)}, u32[]{:S(2)}) collective-permute-start(bf16[64,2048]{1,0:T(8,128)(2,1)S(1)} %collective-permute-done.8.refs_3_), channel_id=1, source_target_pairs={{0,14},{1,15},{2,0},{3,1},{4,2},{5,3},{6,4},{7,5},{8,6},{9,7},{10,... | collective-permute-start | bytes 786440 | tf_op jit(solution)/shard_map/ppermute | solution.py:35
  34.3 5.0 %collective-permute-start.18 = (bf16[160,2048]{1,0:T(8,128)(2,1)S(1)}, bf16[160,2048]{1,0:T(8,128)(2,1)S(1)}, u32[]{:S(2)}, u32[]{:S(2)}) collective-permute-start(bf16[160,2048]{1,0:T(8,128)(2,1)S(1)} %shard_map.63.refs_4_), channel_id=1, source_target_pairs={{0,48},{1,193},{2,50},{3,195},{4,52},{5,197},{6,54},{7,199},{8,56}... | collective-permute-start | bytes 1966088 | tf_op jit(solution)/shard_map/ppermute | solution.py:45
  39.3 3.3 %collective-permute-start.12 = (bf16[32,2048]{1,0:T(8,128)(2,1)S(1)}, bf16[32,2048]{1,0:T(8,128)(2,1)S(1)}, u32[]{:S(2)}, u32[]{:S(2)}) collective-permute-start(bf16[32,2048]{1,0:T(8,128)(2,1)S(1)} %slice.32), channel_id=1, source_target_pairs={{0,14},{1,15},{2,0},{3,1},{4,2},{5,3},{6,4},{7,5},{8,6},{9,7},{10,... | collective-permute-start | bytes 393224 | tf_op jit(solution)/shard_map/ppermute | solution.py:35
  42.9 2.2 %collective-permute-done.12.refs_7_ = bf16[32,2048]{1,0:T(8,128)(2,1)S(1)} collective-permute-done((bf16[32,2048]{1,0:T(8,128)(2,1)S(1)}, bf16[32,2048]{1,0:T(8,128)(2,1)S(1)}, u32[]{:S(2)}, u32[]{:S(2)}) %collective-permute-start.12) | collective-permute-done | bytes 131104 | tf_op jit(solution)/shard_map/ppermute | solution.py:35
  45.1 3.9 %collective-permute-done.13.refs_8_ = bf16[32,2048]{1,0:T(8,128)(2,1)S(1)} collective-permute-done((bf16[32,2048]{1,0:T(8,128)(2,1)S(1)}, bf16[32,2048]{1,0:T(8,128)(2,1)S(1)}, u32[]{:S(2)}, u32[]{:S(2)}) %collective-permute-start.13) | collective-permute-done | bytes 131104 | tf_op jit(solution)/shard_map/ppermute | solution.py:35
  49.1 5.3 %collective-permute-start.14 = (bf16[96,2048]{1,0:T(8,128)(2,1)S(1)}, bf16[96,2048]{1,0:T(8,128)(2,1)S(1)}, u32[]{:S(2)}, u32[]{:S(2)}) collective-permute-start(bf16[96,2048]{1,0:T(8,128)(2,1)S(1)} %get-tuple-element.48.refs_4_), channel_id=1, source_target_pairs={{0,48},{1,193},{2,50},{3,195},{4,52},{5,197},{6,54},{7,199},{8,56}... | collective-permute-start | bytes 1179656 | tf_op jit(solution)/shard_map/ppermute | solution.py:45
  54.4 3.3 %collective-permute-start.19 = (bf16[80,2048]{1,0:T(8,128)(2,1)S(1)}, bf16[80,2048]{1,0:T(8,128)(2,1)S(1)}, u32[]{:S(2)}, u32[]{:S(2)}) collective-permute-start(bf16[80,2048]{1,0:T(8,128)(2,1)S(1)} %slice.36), channel_id=1, source_target_pairs={{0,48},{1,193},{2,50},{3,195},{4,52},{5,197},{6,54},{7,199},{8,56}... | collective-permute-start | bytes 983048 | tf_op jit(solution)/shard_map/ppermute | solution.py:45
  59.7 3.8 %collective-permute-start.15 = (bf16[48,2048]{1,0:T(8,128)(2,1)S(1)}, bf16[48,2048]{1,0:T(8,128)(2,1)S(1)}, u32[]{:S(2)}, u32[]{:S(2)}) collective-permute-start(bf16[48,2048]{1,0:T(8,128)(2,1)S(1)} %slice.34), channel_id=1, source_target_pairs={{0,48},{1,193},{2,50},{3,195},{4,52},{5,197},{6,54},{7,199},{8,56}... | collective-permute-start | bytes 589832 | tf_op jit(solution)/shard_map/ppermute | solution.py:45
  63.6 3.1 %collective-permute-done.15.refs_6_ = bf16[48,2048]{1,0:T(8,128)(2,1)S(1)} collective-permute-done((bf16[48,2048]{1,0:T(8,128)(2,1)S(1)}, bf16[48,2048]{1,0:T(8,128)(2,1)S(1)}, u32[]{:S(2)}, u32[]{:S(2)}) %collective-permute-start.15) | collective-permute-done | bytes 196640 | tf_op jit(solution)/shard_map/ppermute | solution.py:45
  66.7 3.7 %collective-permute-start.27 = (bf16[256,2048]{1,0:T(8,128)(2,1)S(1)}, bf16[256,2048]{1,0:T(8,128)(2,1)S(1)}, u32[]{:S(2)}, u32[]{:S(2)}) collective-permute-start(bf16[256,2048]{1,0:T(8,128)(2,1)S(1)} %get-tuple-element.61.refs_1_), channel_id=1, source_target_pairs={{0,48},{1,193},{2,50},{3,195},{4,52},{5,197},{6,54},{7,199},{8,56}... | collective-permute-start | bytes 3145736 | tf_op jit(solution)/shard_map/ppermute | solution.py:45
  73.8 3.0 %collective-permute-start.22 = (bf16[128,1024]{1,0:T(8,128)(2,1)S(1)}, bf16[128,1024]{1,0:T(8,128)(2,1)S(1)}, u32[]{:S(2)}, u32[]{:S(2)}) collective-permute-start(bf16[128,1024]{1,0:T(8,128)(2,1)S(1)} %get-tuple-element.57), channel_id=1, source_target_pairs={{0,192},{1,49},{2,194},{3,51},{4,196},{5,53},{6,198},{7,55},{8,200... | collective-permute-start | bytes 786440 | tf_op jit(solution)/shard_map/ppermute | solution.py:45
  76.8 7.8 %collective-permute-done.24 = bf16[128,1024]{1,0:T(8,128)(2,1)S(1)} collective-permute-done((bf16[128,1024]{1,0:T(8,128)(2,1)S(1)}, bf16[128,1024]{1,0:T(8,128)(2,1)S(1)}, u32[]{:S(2)}, u32[]{:S(2)}) %collective-permute-start.24) | collective-permute-done | bytes 262176 | tf_op jit(solution)/shard_map/ppermute | solution.py:45
  87.1 4.0 %collective-permute-start.28 = (bf16[128,2048]{1,0:T(8,128)(2,1)S(1)}, bf16[128,2048]{1,0:T(8,128)(2,1)S(1)}, u32[]{:S(2)}, u32[]{:S(2)}) collective-permute-start(bf16[128,2048]{1,0:T(8,128)(2,1)S(1)} %slice.38), channel_id=1, source_target_pairs={{0,48},{1,193},{2,50},{3,195},{4,52},{5,197},{6,54},{7,199},{8,56}... | collective-permute-start | bytes 1572872 | tf_op jit(solution)/shard_map/ppermute | solution.py:45
  96.0 7.2 %collective-permute-done.26.refs_0_ = bf16[128,1024]{1,0:T(8,128)(2,1)S(1)} collective-permute-done((bf16[128,1024]{1,0:T(8,128)(2,1)S(1)}, bf16[128,1024]{1,0:T(8,128)(2,1)S(1)}, u32[]{:S(2)}, u32[]{:S(2)}) %collective-permute-start.26) | collective-permute-done | bytes 262176 | tf_op jit(solution)/shard_map/ppermute | solution.py:45
  105.4 3.4 %collective-permute-start.31 = (bf16[128,2048]{1,0:T(8,128)(2,1)}, bf16[128,2048]{1,0:T(8,128)(2,1)}, u32[]{:S(2)}, u32[]{:S(2)}) collective-permute-start(bf16[128,2048]{1,0:T(8,128)(2,1)} %shard_map.67), channel_id=1, source_target_pairs={{0,192},{1,49},{2,194},{3,51},{4,196},{5,53},{6,198},{7,55},{8,200... | collective-permute-start | bytes 1572872 | tf_op jit(solution)/shard_map/ppermute | solution.py:45
  118.9 2.6 %collective-permute-done.35.refs_0_ = bf16[128,2048]{1,0:T(8,128)(2,1)} collective-permute-done((bf16[128,2048]{1,0:T(8,128)(2,1)}, bf16[128,2048]{1,0:T(8,128)(2,1)}, u32[]{:S(2)}, u32[]{:S(2)}) %collective-permute-start.35) | collective-permute-done | bytes 524320 | tf_op jit(solution)/shard_map/ppermute | solution.py:45
  121.4 2.4 %shard_map.72.refs_2_ = bf16[128,8192]{1,0:T(8,128)(2,1)} custom-call(s32[4]{0:T(128)S(1)} %pad_add_fusion.place, bf16[128,2048]{1,0:T(8,128)(2,1)} %collective-permute-done.35.refs_0_, bf16[128,8192]{1,0:T(8,128)(2,1)} %shard_map.71.refs_1_), custom_call_target="tpu_custom_call", output_to_operand_aliasing={{}: (2, {})} | custom-call | bytes 1000000 | tf_op jit(solution)/shard_map/pallas_call | solution.py:328
  123.8 3.1 %collective-permute-done.33.refs_1_ = bf16[128,2048]{1,0:T(8,128)(2,1)} collective-permute-done((bf16[128,2048]{1,0:T(8,128)(2,1)}, bf16[128,2048]{1,0:T(8,128)(2,1)}, u32[]{:S(2)}, u32[]{:S(2)}) %collective-permute-start.33) | collective-permute-done | bytes 524320 | tf_op jit(solution)/shard_map/ppermute | solution.py:45
  127.0 2.6 %shard_map.73 = bf16[128,8192]{1,0:T(8,128)(2,1)} custom-call(s32[4]{0:T(128)S(1)} %pad_add_fusion.place, bf16[128,2048]{1,0:T(8,128)(2,1)} %collective-permute-done.31.refs_0_, bf16[128,2048]{1,0:T(8,128)(2,1)} %collective-permute-done.33.refs_1_, bf16[128,8192]{1,0:T(8,128)(2,1)} %shard_map.72.refs_2_), custom_call_target="tpu_custom_call", output_to_operand_aliasing={{}: (3, {})} | custom-call | bytes 2000000 | tf_op jit(solution)/shard_map/pallas_call | solution.py:328
  (92 shorter events, 37.4 us)
Async XLA Ops:
  11.4 10.6 %collective-permute-start.6 = (bf16[64,2048]{1,0:T(8,128)(2,1)S(1)}, bf16[64,2048]{1,0:T(8,128)(2,1)S(1)}, u32[]{:S(2)}, u32[]{:S(2)}) collective-permute-start(bf16[64,2048]{1,0:T(8,128)(2,1)S(1)} %shard_map.61.refs_0_), channel_id=1, source_target_pairs={{0,14},{1,15},{2,0},{3,1},{4,2},{5,3},{6,4},{7,5},{8,6},{9,7},{10,... | collective-permute-start | bytes 786440 | tf_op jit(solution)/shard_map/ppermute | solution.py:35
  17.3 16.0 %collective-permute-start.3 = (bf16[128,2048]{1,0:T(8,128)(2,1)S(1)}, bf16[128,2048]{1,0:T(8,128)(2,1)S(1)}, u32[]{:S(2)}, u32[]{:S(2)}) collective-permute-start(bf16[128,2048]{1,0:T(8,128)(2,1)S(1)} %get-tuple-element.45), channel_id=1, source_target_pairs={{0,64},{1,17},{2,66},{3,19},{4,68},{5,21},{6,70},{7,23},{8,72},{9,... | collective-permute-start | bytes 1572872 | tf_op jit(solution)/shard_map/ppermute | solution.py:45
  17.3 16.0 %collective-permute-start.4 = (bf16[128,2048]{1,0:T(8,128)(2,1)S(1)}, bf16[128,2048]{1,0:T(8,128)(2,1)S(1)}, u32[]{:S(2)}, u32[]{:S(2)}) collective-permute-start(bf16[128,2048]{1,0:T(8,128)(2,1)S(1)} %get-tuple-element.46), channel_id=1, source_target_pairs={{0,128},{1,33},{2,130},{3,35},{4,132},{5,37},{6,134},{7,39},{8,136... | collective-permute-start | bytes 1572872 | tf_op jit(solution)/shard_map/ppermute | solution.py:45
  19.4 14.9 %collective-permute-start.5 = (bf16[128,2048]{1,0:T(8,128)(2,1)S(1)}, bf16[128,2048]{1,0:T(8,128)(2,1)S(1)}, u32[]{:S(2)}, u32[]{:S(2)}) collective-permute-start(bf16[128,2048]{1,0:T(8,128)(2,1)S(1)} %get-tuple-element.47), channel_id=1, source_target_pairs={{0,192},{1,49},{2,194},{3,51},{4,196},{5,53},{6,198},{7,55},{8,200... | collective-permute-start | bytes 1572872 | tf_op jit(solution)/shard_map/ppermute | solution.py:45
  29.6 9.7 %collective-permute-start.10 = (bf16[64,2048]{1,0:T(8,128)(2,1)S(1)}, bf16[64,2048]{1,0:T(8,128)(2,1)S(1)}, u32[]{:S(2)}, u32[]{:S(2)}) collective-permute-start(bf16[64,2048]{1,0:T(8,128)(2,1)S(1)} %collective-permute-done.8.refs_3_), channel_id=1, source_target_pairs={{0,14},{1,15},{2,0},{3,1},{4,2},{5,3},{6,4},{7,5},{8,6},{9,7},{10,... | collective-permute-start | bytes 786440 | tf_op jit(solution)/shard_map/ppermute | solution.py:35
  33.3 9.3 %collective-permute-start.11 = (bf16[64,2048]{1,0:T(8,128)(2,1)S(1)}, bf16[64,2048]{1,0:T(8,128)(2,1)S(1)}, u32[]{:S(2)}, u32[]{:S(2)}) collective-permute-start(bf16[64,2048]{1,0:T(8,128)(2,1)S(1)} %collective-permute-done.9.refs_4_), channel_id=1, source_target_pairs={{0,2},{1,3},{2,4},{3,5},{4,6},{5,7},{6,8},{7,9},{8,10},{9,11},{10,... | collective-permute-start | bytes 786440 | tf_op jit(solution)/shard_map/ppermute | solution.py:35
  34.3 20.1 %collective-permute-start.18 = (bf16[160,2048]{1,0:T(8,128)(2,1)S(1)}, bf16[160,2048]{1,0:T(8,128)(2,1)S(1)}, u32[]{:S(2)}, u32[]{:S(2)}) collective-permute-start(bf16[160,2048]{1,0:T(8,128)(2,1)S(1)} %shard_map.63.refs_4_), channel_id=1, source_target_pairs={{0,48},{1,193},{2,50},{3,195},{4,52},{5,197},{6,54},{7,199},{8,56}... | collective-permute-start | bytes 1966088 | tf_op jit(solution)/shard_map/ppermute | solution.py:45
  39.3 18.5 %collective-permute-start.20 = (bf16[160,2048]{1,0:T(8,128)(2,1)S(1)}, bf16[160,2048]{1,0:T(8,128)(2,1)S(1)}, u32[]{:S(2)}, u32[]{:S(2)}) collective-permute-start(bf16[160,2048]{1,0:T(8,128)(2,1)S(1)} %shard_map.63.refs_4_), channel_id=1, source_target_pairs={{0,16},{1,65},{2,18},{3,67},{4,20},{5,69},{6,22},{7,71},{8,24},{9,... | collective-permute-start | bytes 1966088 | tf_op jit(solution)/shard_map/ppermute | solution.py:45
  49.1 10.6 %collective-permute-start.14 = (bf16[96,2048]{1,0:T(8,128)(2,1)S(1)}, bf16[96,2048]{1,0:T(8,128)(2,1)S(1)}, u32[]{:S(2)}, u32[]{:S(2)}) collective-permute-start(bf16[96,2048]{1,0:T(8,128)(2,1)S(1)} %get-tuple-element.48.refs_4_), channel_id=1, source_target_pairs={{0,48},{1,193},{2,50},{3,195},{4,52},{5,197},{6,54},{7,199},{8,56}... | collective-permute-start | bytes 1179656 | tf_op jit(solution)/shard_map/ppermute | solution.py:45
  54.4 15.9 %collective-permute-start.19 = (bf16[80,2048]{1,0:T(8,128)(2,1)S(1)}, bf16[80,2048]{1,0:T(8,128)(2,1)S(1)}, u32[]{:S(2)}, u32[]{:S(2)}) collective-permute-start(bf16[80,2048]{1,0:T(8,128)(2,1)S(1)} %slice.36), channel_id=1, source_target_pairs={{0,48},{1,193},{2,50},{3,195},{4,52},{5,197},{6,54},{7,199},{8,56}... | collective-permute-start | bytes 983048 | tf_op jit(solution)/shard_map/ppermute | solution.py:45
  57.8 12.6 %collective-permute-start.21 = (bf16[80,2048]{1,0:T(8,128)(2,1)S(1)}, bf16[80,2048]{1,0:T(8,128)(2,1)S(1)}, u32[]{:S(2)}, u32[]{:S(2)}) collective-permute-start(bf16[80,2048]{1,0:T(8,128)(2,1)S(1)} %slice.37), channel_id=1, source_target_pairs={{0,16},{1,65},{2,18},{3,67},{4,20},{5,69},{6,22},{7,71},{8,24},{9,... | collective-permute-start | bytes 983048 | tf_op jit(solution)/shard_map/ppermute | solution.py:45
  66.7 20.4 %collective-permute-start.27 = (bf16[256,2048]{1,0:T(8,128)(2,1)S(1)}, bf16[256,2048]{1,0:T(8,128)(2,1)S(1)}, u32[]{:S(2)}, u32[]{:S(2)}) collective-permute-start(bf16[256,2048]{1,0:T(8,128)(2,1)S(1)} %get-tuple-element.61.refs_1_), channel_id=1, source_target_pairs={{0,48},{1,193},{2,50},{3,195},{4,52},{5,197},{6,54},{7,199},{8,56}... | collective-permute-start | bytes 3145736 | tf_op jit(solution)/shard_map/ppermute | solution.py:45
  70.4 20.7 %collective-permute-start.29 = (bf16[256,2048]{1,0:T(8,128)(2,1)S(1)}, bf16[256,2048]{1,0:T(8,128)(2,1)S(1)}, u32[]{:S(2)}, u32[]{:S(2)}) collective-permute-start(bf16[256,2048]{1,0:T(8,128)(2,1)S(1)} %get-tuple-element.61.refs_1_), channel_id=1, source_target_pairs={{0,16},{1,65},{2,18},{3,67},{4,20},{5,69},{6,22},{7,71},{8,24},{9,... | collective-permute-start | bytes 3145736 | tf_op jit(solution)/shard_map/ppermute | solution.py:45
  73.5 11.1 %collective-permute-start.24 = (bf16[128,1024]{1,0:T(8,128)(2,1)S(1)}, bf16[128,1024]{1,0:T(8,128)(2,1)S(1)}, u32[]{:S(2)}, u32[]{:S(2)}) collective-permute-start(bf16[128,1024]{1,0:T(8,128)(2,1)S(1)} %get-tuple-element.59), channel_id=1, source_target_pairs={{0,64},{1,17},{2,66},{3,19},{4,68},{5,21},{6,70},{7,23},{8,72},{9,... | collective-permute-start | bytes 786440 | tf_op jit(solution)/shard_map/ppermute | solution.py:45
  73.6 11.0 %collective-permute-start.23 = (bf16[128,1024]{1,0:T(8,128)(2,1)S(1)}, bf16[128,1024]{1,0:T(8,128)(2,1)S(1)}, u32[]{:S(2)}, u32[]{:S(2)}) collective-permute-start(bf16[128,1024]{1,0:T(8,128)(2,1)S(1)} %get-tuple-element.58), channel_id=1, source_target_pairs={{0,128},{1,33},{2,130},{3,35},{4,132},{5,37},{6,134},{7,39},{8,136... | collective-permute-start | bytes 786440 | tf_op jit(solution)/shard_map/ppermute | solution.py:45
  73.8 11.0 %collective-permute-start.22 = (bf16[128,1024]{1,0:T(8,128)(2,1)S(1)}, bf16[128,1024]{1,0:T(8,128)(2,1)S(1)}, u32[]{:S(2)}, u32[]{:S(2)}) collective-permute-start(bf16[128,1024]{1,0:T(8,128)(2,1)S(1)} %get-tuple-element.57), channel_id=1, source_target_pairs={{0,192},{1,49},{2,194},{3,51},{4,196},{5,53},{6,198},{7,55},{8,200... | collective-permute-start | bytes 786440 | tf_op jit(solution)/shard_map/ppermute | solution.py:45
  87.1 16.6 %collective-permute-start.28 = (bf16[128,2048]{1,0:T(8,128)(2,1)S(1)}, bf16[128,2048]{1,0:T(8,128)(2,1)S(1)}, u32[]{:S(2)}, u32[]{:S(2)}) collective-permute-start(bf16[128,2048]{1,0:T(8,128)(2,1)S(1)} %slice.38), channel_id=1, source_target_pairs={{0,48},{1,193},{2,50},{3,195},{4,52},{5,197},{6,54},{7,199},{8,56}... | collective-permute-start | bytes 1572872 | tf_op jit(solution)/shard_map/ppermute | solution.py:45
  91.2 12.7 %collective-permute-start.30 = (bf16[128,2048]{1,0:T(8,128)(2,1)S(1)}, bf16[128,2048]{1,0:T(8,128)(2,1)S(1)}, u32[]{:S(2)}, u32[]{:S(2)}) collective-permute-start(bf16[128,2048]{1,0:T(8,128)(2,1)S(1)} %slice.39), channel_id=1, source_target_pairs={{0,16},{1,65},{2,18},{3,67},{4,20},{5,69},{6,22},{7,71},{8,24},{9,... | collective-permute-start | bytes 1572872 | tf_op jit(solution)/shard_map/ppermute | solution.py:45
  92.7 10.6 %collective-permute-start.26 = (bf16[128,1024]{1,0:T(8,128)(2,1)S(1)}, bf16[128,1024]{1,0:T(8,128)(2,1)S(1)}, u32[]{:S(2)}, u32[]{:S(2)}) collective-permute-start(bf16[128,1024]{1,0:T(8,128)(2,1)S(1)} %shard_map.66.refs_0_), channel_id=1, source_target_pairs={{0,64},{1,17},{2,66},{3,19},{4,68},{5,21},{6,70},{7,23},{8,72},{9,... | collective-permute-start | bytes 786440 | tf_op jit(solution)/shard_map/ppermute | solution.py:45
  92.7 16.1 %collective-permute-start.34 = (bf16[128,1024]{1,0:T(8,128)(2,1)S(1)}, bf16[128,1024]{1,0:T(8,128)(2,1)S(1)}, u32[]{:S(2)}, u32[]{:S(2)}) collective-permute-start(bf16[128,1024]{1,0:T(8,128)(2,1)S(1)} %shard_map.66.refs_0_), channel_id=1, source_target_pairs={{0,128},{1,33},{2,130},{3,35},{4,132},{5,37},{6,134},{7,39},{8,136... | collective-permute-start | bytes 786440 | tf_op jit(solution)/shard_map/ppermute | solution.py:45
  94.2 16.1 %collective-permute-start.32 = (bf16[128,1024]{1,0:T(8,128)(2,1)S(1)}, bf16[128,1024]{1,0:T(8,128)(2,1)S(1)}, u32[]{:S(2)}, u32[]{:S(2)}) collective-permute-start(bf16[128,1024]{1,0:T(8,128)(2,1)S(1)} %shard_map.66.refs_0_), channel_id=1, source_target_pairs={{0,192},{1,49},{2,194},{3,51},{4,196},{5,53},{6,198},{7,55},{8,200... | collective-permute-start | bytes 786440 | tf_op jit(solution)/shard_map/ppermute | solution.py:45
  105.4 18.4 %collective-permute-start.31 = (bf16[128,2048]{1,0:T(8,128)(2,1)}, bf16[128,2048]{1,0:T(8,128)(2,1)}, u32[]{:S(2)}, u32[]{:S(2)}) collective-permute-start(bf16[128,2048]{1,0:T(8,128)(2,1)} %shard_map.67), channel_id=1, source_target_pairs={{0,192},{1,49},{2,194},{3,51},{4,196},{5,53},{6,198},{7,55},{8,200... | collective-permute-start | bytes 1572872 | tf_op jit(solution)/shard_map/ppermute | solution.py:45
  110.3 11.1 %collective-permute-start.35 = (bf16[128,2048]{1,0:T(8,128)(2,1)}, bf16[128,2048]{1,0:T(8,128)(2,1)}, u32[]{:S(2)}, u32[]{:S(2)}) collective-permute-start(bf16[128,2048]{1,0:T(8,128)(2,1)} %shard_map.69), channel_id=1, source_target_pairs={{0,128},{1,33},{2,130},{3,35},{4,132},{5,37},{6,134},{7,39},{8,136... | collective-permute-start | bytes 1572872 | tf_op jit(solution)/shard_map/ppermute | solution.py:45
  111.9 15.1 %collective-permute-start.33 = (bf16[128,2048]{1,0:T(8,128)(2,1)}, bf16[128,2048]{1,0:T(8,128)(2,1)}, u32[]{:S(2)}, u32[]{:S(2)}) collective-permute-start(bf16[128,2048]{1,0:T(8,128)(2,1)} %shard_map.68), channel_id=1, source_target_pairs={{0,64},{1,17},{2,66},{3,19},{4,68},{5,21},{6,70},{7,23},{8,72},{9,... | collective-permute-start | bytes 1572872 | tf_op jit(solution)/shard_map/ppermute | solution.py:45
  (19 other events, 114.2 us)

commit v8 on v7

--- a/solution.py
+++ b/solution.py
@@ -275,19 +275,23 @@
 
 
 def quadratic_kernel(count, *refs):
-    lefts, rights, outs = refs[:count], refs[count : count + 5], refs[count + 5 :]
+    lefts, rights, out, held, sem = refs[:count], refs[count : count + 5], *refs[count + 5 :]
     left = jnp.concatenate([ref[...] for ref in lefts], 0)
     mine, above, half, other, below = rights
     middle = half.shape[0]
     wide = 512
+    copies = []
     for n in range(0, PART, wide):
         cols = slice(n, n + wide)
         right = [mine[:EARLY, cols], above[:EARLY, cols], half[:, cols], other[: EARLY - middle, cols]]
         right += [below[:EARLY, cols], mine[EARLY:, cols], above[EARLY:, cols]]
         right += [other[EARLY - middle :, cols], below[EARLY:, cols]]
         value = jnp.dot(left, jnp.concatenate(right, 0), preferred_element_type=F32).astype(BF)
-        for d in range(count):
-            outs[d][:, cols] = value[d * ROWS : (d + 1) * ROWS]
+        held[:, cols] = value
+        copies.append(pltpu.make_async_copy(held.at[:, cols], out.at[:, cols], sem.at[n // wide]))
+        copies[-1].start()
+    for copy in copies:
+        copy.wait()
 
 
 def quadratic_blocks(lefts, rights):
@@ -296,7 +300,8 @@
         functools.partial(quadratic_kernel, count),
         out_shape=[jax.ShapeDtypeStruct((ROWS, PART), BF)] * count,
         in_specs=[VMEM] * (count + 5),
-        out_specs=[VMEM] * count,
+        out_specs=[pl.BlockSpec(memory_space=pl.ANY)] * count,
+        scratch_shapes=[pltpu.VMEM((ROWS, PART), BF), pltpu.SemaphoreType.DMA((4,))],
         compiler_params=WIDE,
         cost_estimate=cost(2 * count * ROWS * QW * PART, 5_000_000),
     )(*lefts, *rights)

time: 130 us -> 130 us (level)
  transfers between devices with their start and end apart: 36 -> 36, of which waited for: 18 -> 18; matrix products, arithmetic and copies ran while one was open for 2% -> 2% of each run, Pallas kernels for 12% -> 13%
where the time goes in v8:
time: 130 us
  starting transfers between devices  60.1 us (46%)
  waiting for transfers between devices  42.5 us (33%)
  Pallas kernels  21.9 us (17%)
  local copies, waits for them, and re-layouts  2.27 us (2%)
    ppermute x27, starting transfers between devices, shift_plane(): return lax.ppermute(value, AX, pairs)  43.1 us
    ppermute x27, waiting for transfers between devices, shift_plane(): return lax.ppermute(value, AX, pairs)  31.7 us
    ppermute x8, starting transfers between devices, shift_z(): lax.ppermute(value, AX, [(ident(x, y, z, c), ident(x, y, z + step, c)) fo...  16.9 us
    ppermute x8, waiting for transfers between devices, shift_z(): lax.ppermute(value, AX, [(ident(x, y, z, c), ident(x, y, z + step, c)) fo...  10.8 us
    pallas_call x3, Pallas kernels, place_blocks(): pl.pallas_call(functools.partial(place_kernel, ds), out_shape=jax.ShapeDt...  7.06 us
    pallas_call x4, Pallas kernels, quadratic_blocks(): pl.pallas_call(functools.partial(quadratic_kernel, count), out_shape=[jax...  5.75 us
  transfers between devices with their start and end apart: 36, of which 18 were waited for; matrix products, arithmetic and copies ran while one was open for 2% of the time, Pallas kernels for 13%

profile of v8, /device:TPU:0, one launch (start us, length us, event | category | flops | bytes accessed | tf_op | source)
XLA Modules:
  0.0 129.8 jit_solution(5950794710860122903)
XLA Ops:
  0.7 2.2 %shard_map.59 = (bf16[16,2048]{1,0:T(8,128)(2,1)}, bf16[16,2048]{1,0:T(8,128)(2,1)}, bf16[16,2048]{1,0:T(8,128)(2,1)}, bf16[16,2048]{1,0:T(8,128)(2,1)}) custom-call(s32[128,128]{1,0:T(8,128)} %cyc_map_in.1, s32[1,64]{1,0:T(1,128)} %amp_map.1, bf16[8,8192]{1,0:T(8,128)(2,1)} %bitcast.6, bf16[128,8192]{1,0:T(8,128)(2,1)} %refs_3_), custom_call_target="tpu_custom_call" | custom-call | bytes 600000 | tf_op jit(solution)/shard_map/pallas_call | solution.py:91
  7.6 2.3 %collective-permute-done.1.refs_2_ = bf16[16,2048]{1,0:T(8,128)(2,1)S(1)} collective-permute-done((bf16[16,2048]{1,0:T(8,128)(2,1)}, bf16[16,2048]{1,0:T(8,128)(2,1)S(1)}, u32[]{:S(2)}, u32[]{:S(2)}) %collective-permute-start.1) | collective-permute-done | bytes 65568 | tf_op jit(solution)/shard_map/ppermute | solution.py:45
  11.4 5.9 %collective-permute-start.6 = (bf16[64,2048]{1,0:T(8,128)(2,1)S(1)}, bf16[64,2048]{1,0:T(8,128)(2,1)S(1)}, u32[]{:S(2)}, u32[]{:S(2)}) collective-permute-start(bf16[64,2048]{1,0:T(8,128)(2,1)S(1)} %shard_map.61.refs_0_), channel_id=1, source_target_pairs={{0,14},{1,15},{2,0},{3,1},{4,2},{5,3},{6,4},{7,5},{8,6},{9,7},{10,... | collective-permute-start | bytes 786440 | tf_op jit(solution)/shard_map/ppermute | solution.py:35
  22.0 3.7 %collective-permute-start.8 = (bf16[64,2048]{1,0:T(8,128)(2,1)S(1)}, bf16[64,2048]{1,0:T(8,128)(2,1)S(1)}, u32[]{:S(2)}, u32[]{:S(2)}) collective-permute-start(bf16[64,2048]{1,0:T(8,128)(2,1)S(1)} %collective-permute-done.6.refs_1_), channel_id=1, source_target_pairs={{0,14},{1,15},{2,0},{3,1},{4,2},{5,3},{6,4},{7,5},{8,6},{9,7},{10,... | collective-permute-start | bytes 786440 | tf_op jit(solution)/shard_map/ppermute | solution.py:35
  25.7 3.9 %collective-permute-done.8.refs_3_ = bf16[64,2048]{1,0:T(8,128)(2,1)S(1)} collective-permute-done((bf16[64,2048]{1,0:T(8,128)(2,1)S(1)}, bf16[64,2048]{1,0:T(8,128)(2,1)S(1)}, u32[]{:S(2)}, u32[]{:S(2)}) %collective-permute-start.8) | collective-permute-done | bytes 262176 | tf_op jit(solution)/shard_map/ppermute | solution.py:35
  29.6 3.7 %collective-permute-start.10 = (bf16[64,2048]{1,0:T(8,128)(2,1)S(1)}, bf16[64,2048]{1,0:T(8,128)(2,1)S(1)}, u32[]{:S(2)}, u32[]{:S(2)}) collective-permute-start(bf16[64,2048]{1,0:T(8,128)(2,1)S(1)} %collective-permute-done.8.refs_3_), channel_id=1, source_target_pairs={{0,14},{1,15},{2,0},{3,1},{4,2},{5,3},{6,4},{7,5},{8,6},{9,7},{10,... | collective-permute-start | bytes 786440 | tf_op jit(solution)/shard_map/ppermute | solution.py:35
  34.3 5.0 %collective-permute-start.18 = (bf16[160,2048]{1,0:T(8,128)(2,1)S(1)}, bf16[160,2048]{1,0:T(8,128)(2,1)S(1)}, u32[]{:S(2)}, u32[]{:S(2)}) collective-permute-start(bf16[160,2048]{1,0:T(8,128)(2,1)S(1)} %shard_map.63.refs_4_), channel_id=1, source_target_pairs={{0,48},{1,193},{2,50},{3,195},{4,52},{5,197},{6,54},{7,199},{8,56}... | collective-permute-start | bytes 1966088 | tf_op jit(solution)/shard_map/ppermute | solution.py:45
  39.3 3.3 %collective-permute-start.12 = (bf16[32,2048]{1,0:T(8,128)(2,1)S(1)}, bf16[32,2048]{1,0:T(8,128)(2,1)S(1)}, u32[]{:S(2)}, u32[]{:S(2)}) collective-permute-start(bf16[32,2048]{1,0:T(8,128)(2,1)S(1)} %slice.32), channel_id=1, source_target_pairs={{0,14},{1,15},{2,0},{3,1},{4,2},{5,3},{6,4},{7,5},{8,6},{9,7},{10,... | collective-permute-start | bytes 393224 | tf_op jit(solution)/shard_map/ppermute | solution.py:35
  42.9 2.2 %collective-permute-done.12.refs_7_ = bf16[32,2048]{1,0:T(8,128)(2,1)S(1)} collective-permute-done((bf16[32,2048]{1,0:T(8,128)(2,1)S(1)}, bf16[32,2048]{1,0:T(8,128)(2,1)S(1)}, u32[]{:S(2)}, u32[]{:S(2)}) %collective-permute-start.12) | collective-permute-done | bytes 131104 | tf_op jit(solution)/shard_map/ppermute | solution.py:35
  45.1 3.9 %collective-permute-done.13.refs_8_ = bf16[32,2048]{1,0:T(8,128)(2,1)S(1)} collective-permute-done((bf16[32,2048]{1,0:T(8,128)(2,1)S(1)}, bf16[32,2048]{1,0:T(8,128)(2,1)S(1)}, u32[]{:S(2)}, u32[]{:S(2)}) %collective-permute-start.13) | collective-permute-done | bytes 131104 | tf_op jit(solution)/shard_map/ppermute | solution.py:35
  49.1 5.3 %collective-permute-start.14 = (bf16[96,2048]{1,0:T(8,128)(2,1)S(1)}, bf16[96,2048]{1,0:T(8,128)(2,1)S(1)}, u32[]{:S(2)}, u32[]{:S(2)}) collective-permute-start(bf16[96,2048]{1,0:T(8,128)(2,1)S(1)} %get-tuple-element.48.refs_4_), channel_id=1, source_target_pairs={{0,48},{1,193},{2,50},{3,195},{4,52},{5,197},{6,54},{7,199},{8,56}... | collective-permute-start | bytes 1179656 | tf_op jit(solution)/shard_map/ppermute | solution.py:45
  54.4 3.3 %collective-permute-start.19 = (bf16[80,2048]{1,0:T(8,128)(2,1)S(1)}, bf16[80,2048]{1,0:T(8,128)(2,1)S(1)}, u32[]{:S(2)}, u32[]{:S(2)}) collective-permute-start(bf16[80,2048]{1,0:T(8,128)(2,1)S(1)} %slice.36), channel_id=1, source_target_pairs={{0,48},{1,193},{2,50},{3,195},{4,52},{5,197},{6,54},{7,199},{8,56}... | collective-permute-start | bytes 983048 | tf_op jit(solution)/shard_map/ppermute | solution.py:45
  59.7 3.8 %collective-permute-start.15 = (bf16[48,2048]{1,0:T(8,128)(2,1)S(1)}, bf16[48,2048]{1,0:T(8,128)(2,1)S(1)}, u32[]{:S(2)}, u32[]{:S(2)}) collective-permute-start(bf16[48,2048]{1,0:T(8,128)(2,1)S(1)} %slice.34), channel_id=1, source_target_pairs={{0,48},{1,193},{2,50},{3,195},{4,52},{5,197},{6,54},{7,199},{8,56}... | collective-permute-start | bytes 589832 | tf_op jit(solution)/shard_map/ppermute | solution.py:45
  63.6 3.1 %collective-permute-done.15.refs_6_ = bf16[48,2048]{1,0:T(8,128)(2,1)S(1)} collective-permute-done((bf16[48,2048]{1,0:T(8,128)(2,1)S(1)}, bf16[48,2048]{1,0:T(8,128)(2,1)S(1)}, u32[]{:S(2)}, u32[]{:S(2)}) %collective-permute-start.15) | collective-permute-done | bytes 196640 | tf_op jit(solution)/shard_map/ppermute | solution.py:45
  66.7 3.7 %collective-permute-start.27 = (bf16[256,2048]{1,0:T(8,128)(2,1)S(1)}, bf16[256,2048]{1,0:T(8,128)(2,1)S(1)}, u32[]{:S(2)}, u32[]{:S(2)}) collective-permute-start(bf16[256,2048]{1,0:T(8,128)(2,1)S(1)} %get-tuple-element.61.refs_1_), channel_id=1, source_target_pairs={{0,48},{1,193},{2,50},{3,195},{4,52},{5,197},{6,54},{7,199},{8,56}... | collective-permute-start | bytes 3145736 | tf_op jit(solution)/shard_map/ppermute | solution.py:45
  73.8 3.0 %collective-permute-start.22 = (bf16[128,1024]{1,0:T(8,128)(2,1)S(1)}, bf16[128,1024]{1,0:T(8,128)(2,1)S(1)}, u32[]{:S(2)}, u32[]{:S(2)}) collective-permute-start(bf16[128,1024]{1,0:T(8,128)(2,1)S(1)} %get-tuple-element.57), channel_id=1, source_target_pairs={{0,192},{1,49},{2,194},{3,51},{4,196},{5,53},{6,198},{7,55},{8,200... | collective-permute-start | bytes 786440 | tf_op jit(solution)/shard_map/ppermute | solution.py:45
  76.8 7.8 %collective-permute-done.24 = bf16[128,1024]{1,0:T(8,128)(2,1)S(1)} collective-permute-done((bf16[128,1024]{1,0:T(8,128)(2,1)S(1)}, bf16[128,1024]{1,0:T(8,128)(2,1)S(1)}, u32[]{:S(2)}, u32[]{:S(2)}) %collective-permute-start.24) | collective-permute-done | bytes 262176 | tf_op jit(solution)/shard_map/ppermute | solution.py:45
  87.1 4.0 %collective-permute-start.28 = (bf16[128,2048]{1,0:T(8,128)(2,1)S(1)}, bf16[128,2048]{1,0:T(8,128)(2,1)S(1)}, u32[]{:S(2)}, u32[]{:S(2)}) collective-permute-start(bf16[128,2048]{1,0:T(8,128)(2,1)S(1)} %slice.38), channel_id=1, source_target_pairs={{0,48},{1,193},{2,50},{3,195},{4,52},{5,197},{6,54},{7,199},{8,56}... | collective-permute-start | bytes 1572872 | tf_op jit(solution)/shard_map/ppermute | solution.py:45
  96.0 7.2 %collective-permute-done.26.refs_0_ = bf16[128,1024]{1,0:T(8,128)(2,1)S(1)} collective-permute-done((bf16[128,1024]{1,0:T(8,128)(2,1)S(1)}, bf16[128,1024]{1,0:T(8,128)(2,1)S(1)}, u32[]{:S(2)}, u32[]{:S(2)}) %collective-permute-start.26) | collective-permute-done | bytes 262176 | tf_op jit(solution)/shard_map/ppermute | solution.py:45
  105.3 3.5 %collective-permute-start.31 = (bf16[128,2048]{1,0:T(8,128)(2,1)}, bf16[128,2048]{1,0:T(8,128)(2,1)}, u32[]{:S(2)}, u32[]{:S(2)}) collective-permute-start(bf16[128,2048]{1,0:T(8,128)(2,1)} %shard_map.67), channel_id=1, source_target_pairs={{0,192},{1,49},{2,194},{3,51},{4,196},{5,53},{6,198},{7,55},{8,200... | collective-permute-start | bytes 1572872 | tf_op jit(solution)/shard_map/ppermute | solution.py:45
  117.5 2.1 %shard_map.71.refs_1_ = bf16[128,8192]{1,0:T(8,128)(2,1)} custom-call(s32[4]{0:T(128)S(1)} %pad_add_fusion.place, bf16[128,2048]{1,0:T(8,128)(2,1)S(1)} %shard_map.70.refs_0_), custom_call_target="tpu_custom_call" | custom-call | bytes 1000000 | tf_op jit(solution)/shard_map/pallas_call | solution.py:333
  121.5 2.4 %shard_map.72.refs_2_ = bf16[128,8192]{1,0:T(8,128)(2,1)} custom-call(s32[4]{0:T(128)S(1)} %pad_add_fusion.place, bf16[128,2048]{1,0:T(8,128)(2,1)} %collective-permute-done.35.refs_0_, bf16[128,8192]{1,0:T(8,128)(2,1)} %shard_map.71.refs_1_), custom_call_target="tpu_custom_call", output_to_operand_aliasing={{}: (2, {})} | custom-call | bytes 1000000 | tf_op jit(solution)/shard_map/pallas_call | solution.py:333
  123.8 3.1 %collective-permute-done.33.refs_1_ = bf16[128,2048]{1,0:T(8,128)(2,1)} collective-permute-done((bf16[128,2048]{1,0:T(8,128)(2,1)}, bf16[128,2048]{1,0:T(8,128)(2,1)}, u32[]{:S(2)}, u32[]{:S(2)}) %collective-permute-start.33) | collective-permute-done | bytes 524320 | tf_op jit(solution)/shard_map/ppermute | solution.py:45
  127.0 2.6 %shard_map.73 = bf16[128,8192]{1,0:T(8,128)(2,1)} custom-call(s32[4]{0:T(128)S(1)} %pad_add_fusion.place, bf16[128,2048]{1,0:T(8,128)(2,1)} %collective-permute-done.31.refs_0_, bf16[128,2048]{1,0:T(8,128)(2,1)} %collective-permute-done.33.refs_1_, bf16[128,8192]{1,0:T(8,128)(2,1)} %shard_map.72.refs_2_), custom_call_target="tpu_custom_call", output_to_operand_aliasing={{}: (3, {})} | custom-call | bytes 2000000 | tf_op jit(solution)/shard_map/pallas_call | solution.py:333
  (92 shorter events, 37.8 us)
Async XLA Ops:
  11.4 10.6 %collective-permute-start.6 = (bf16[64,2048]{1,0:T(8,128)(2,1)S(1)}, bf16[64,2048]{1,0:T(8,128)(2,1)S(1)}, u32[]{:S(2)}, u32[]{:S(2)}) collective-permute-start(bf16[64,2048]{1,0:T(8,128)(2,1)S(1)} %shard_map.61.refs_0_), channel_id=1, source_target_pairs={{0,14},{1,15},{2,0},{3,1},{4,2},{5,3},{6,4},{7,5},{8,6},{9,7},{10,... | collective-permute-start | bytes 786440 | tf_op jit(solution)/shard_map/ppermute | solution.py:35
  17.3 16.0 %collective-permute-start.3 = (bf16[128,2048]{1,0:T(8,128)(2,1)S(1)}, bf16[128,2048]{1,0:T(8,128)(2,1)S(1)}, u32[]{:S(2)}, u32[]{:S(2)}) collective-permute-start(bf16[128,2048]{1,0:T(8,128)(2,1)S(1)} %get-tuple-element.45), channel_id=1, source_target_pairs={{0,64},{1,17},{2,66},{3,19},{4,68},{5,21},{6,70},{7,23},{8,72},{9,... | collective-permute-start | bytes 1572872 | tf_op jit(solution)/shard_map/ppermute | solution.py:45
  17.3 16.0 %collective-permute-start.4 = (bf16[128,2048]{1,0:T(8,128)(2,1)S(1)}, bf16[128,2048]{1,0:T(8,128)(2,1)S(1)}, u32[]{:S(2)}, u32[]{:S(2)}) collective-permute-start(bf16[128,2048]{1,0:T(8,128)(2,1)S(1)} %get-tuple-element.46), channel_id=1, source_target_pairs={{0,128},{1,33},{2,130},{3,35},{4,132},{5,37},{6,134},{7,39},{8,136... | collective-permute-start | bytes 1572872 | tf_op jit(solution)/shard_map/ppermute | solution.py:45
  19.4 14.9 %collective-permute-start.5 = (bf16[128,2048]{1,0:T(8,128)(2,1)S(1)}, bf16[128,2048]{1,0:T(8,128)(2,1)S(1)}, u32[]{:S(2)}, u32[]{:S(2)}) collective-permute-start(bf16[128,2048]{1,0:T(8,128)(2,1)S(1)} %get-tuple-element.47), channel_id=1, source_target_pairs={{0,192},{1,49},{2,194},{3,51},{4,196},{5,53},{6,198},{7,55},{8,200... | collective-permute-start | bytes 1572872 | tf_op jit(solution)/shard_map/ppermute | solution.py:45
  29.6 9.7 %collective-permute-start.10 = (bf16[64,2048]{1,0:T(8,128)(2,1)S(1)}, bf16[64,2048]{1,0:T(8,128)(2,1)S(1)}, u32[]{:S(2)}, u32[]{:S(2)}) collective-permute-start(bf16[64,2048]{1,0:T(8,128)(2,1)S(1)} %collective-permute-done.8.refs_3_), channel_id=1, source_target_pairs={{0,14},{1,15},{2,0},{3,1},{4,2},{5,3},{6,4},{7,5},{8,6},{9,7},{10,... | collective-permute-start | bytes 786440 | tf_op jit(solution)/shard_map/ppermute | solution.py:35
  33.3 9.3 %collective-permute-start.11 = (bf16[64,2048]{1,0:T(8,128)(2,1)S(1)}, bf16[64,2048]{1,0:T(8,128)(2,1)S(1)}, u32[]{:S(2)}, u32[]{:S(2)}) collective-permute-start(bf16[64,2048]{1,0:T(8,128)(2,1)S(1)} %collective-permute-done.9.refs_4_), channel_id=1, source_target_pairs={{0,2},{1,3},{2,4},{3,5},{4,6},{5,7},{6,8},{7,9},{8,10},{9,11},{10,... | collective-permute-start | bytes 786440 | tf_op jit(solution)/shard_map/ppermute | solution.py:35
  34.3 20.1 %collective-permute-start.18 = (bf16[160,2048]{1,0:T(8,128)(2,1)S(1)}, bf16[160,2048]{1,0:T(8,128)(2,1)S(1)}, u32[]{:S(2)}, u32[]{:S(2)}) collective-permute-start(bf16[160,2048]{1,0:T(8,128)(2,1)S(1)} %shard_map.63.refs_4_), channel_id=1, source_target_pairs={{0,48},{1,193},{2,50},{3,195},{4,52},{5,197},{6,54},{7,199},{8,56}... | collective-permute-start | bytes 1966088 | tf_op jit(solution)/shard_map/ppermute | solution.py:45
  39.3 18.5 %collective-permute-start.20 = (bf16[160,2048]{1,0:T(8,128)(2,1)S(1)}, bf16[160,2048]{1,0:T(8,128)(2,1)S(1)}, u32[]{:S(2)}, u32[]{:S(2)}) collective-permute-start(bf16[160,2048]{1,0:T(8,128)(2,1)S(1)} %shard_map.63.refs_4_), channel_id=1, source_target_pairs={{0,16},{1,65},{2,18},{3,67},{4,20},{5,69},{6,22},{7,71},{8,24},{9,... | collective-permute-start | bytes 1966088 | tf_op jit(solution)/shard_map/ppermute | solution.py:45
  49.1 10.6 %collective-permute-start.14 = (bf16[96,2048]{1,0:T(8,128)(2,1)S(1)}, bf16[96,2048]{1,0:T(8,128)(2,1)S(1)}, u32[]{:S(2)}, u32[]{:S(2)}) collective-permute-start(bf16[96,2048]{1,0:T(8,128)(2,1)S(1)} %get-tuple-element.48.refs_4_), channel_id=1, source_target_pairs={{0,48},{1,193},{2,50},{3,195},{4,52},{5,197},{6,54},{7,199},{8,56}... | collective-permute-start | bytes 1179656 | tf_op jit(solution)/shard_map/ppermute | solution.py:45
  54.4 15.9 %collective-permute-start.19 = (bf16[80,2048]{1,0:T(8,128)(2,1)S(1)}, bf16[80,2048]{1,0:T(8,128)(2,1)S(1)}, u32[]{:S(2)}, u32[]{:S(2)}) collective-permute-start(bf16[80,2048]{1,0:T(8,128)(2,1)S(1)} %slice.36), channel_id=1, source_target_pairs={{0,48},{1,193},{2,50},{3,195},{4,52},{5,197},{6,54},{7,199},{8,56}... | collective-permute-start | bytes 983048 | tf_op jit(solution)/shard_map/ppermute | solution.py:45
  57.8 12.6 %collective-permute-start.21 = (bf16[80,2048]{1,0:T(8,128)(2,1)S(1)}, bf16[80,2048]{1,0:T(8,128)(2,1)S(1)}, u32[]{:S(2)}, u32[]{:S(2)}) collective-permute-start(bf16[80,2048]{1,0:T(8,128)(2,1)S(1)} %slice.37), channel_id=1, source_target_pairs={{0,16},{1,65},{2,18},{3,67},{4,20},{5,69},{6,22},{7,71},{8,24},{9,... | collective-permute-start | bytes 983048 | tf_op jit(solution)/shard_map/ppermute | solution.py:45
  66.7 20.4 %collective-permute-start.27 = (bf16[256,2048]{1,0:T(8,128)(2,1)S(1)}, bf16[256,2048]{1,0:T(8,128)(2,1)S(1)}, u32[]{:S(2)}, u32[]{:S(2)}) collective-permute-start(bf16[256,2048]{1,0:T(8,128)(2,1)S(1)} %get-tuple-element.61.refs_1_), channel_id=1, source_target_pairs={{0,48},{1,193},{2,50},{3,195},{4,52},{5,197},{6,54},{7,199},{8,56}... | collective-permute-start | bytes 3145736 | tf_op jit(solution)/shard_map/ppermute | solution.py:45
  70.4 20.7 %collective-permute-start.29 = (bf16[256,2048]{1,0:T(8,128)(2,1)S(1)}, bf16[256,2048]{1,0:T(8,128)(2,1)S(1)}, u32[]{:S(2)}, u32[]{:S(2)}) collective-permute-start(bf16[256,2048]{1,0:T(8,128)(2,1)S(1)} %get-tuple-element.61.refs_1_), channel_id=1, source_target_pairs={{0,16},{1,65},{2,18},{3,67},{4,20},{5,69},{6,22},{7,71},{8,24},{9,... | collective-permute-start | bytes 3145736 | tf_op jit(solution)/shard_map/ppermute | solution.py:45
  73.5 11.1 %collective-permute-start.24 = (bf16[128,1024]{1,0:T(8,128)(2,1)S(1)}, bf16[128,1024]{1,0:T(8,128)(2,1)S(1)}, u32[]{:S(2)}, u32[]{:S(2)}) collective-permute-start(bf16[128,1024]{1,0:T(8,128)(2,1)S(1)} %get-tuple-element.59), channel_id=1, source_target_pairs={{0,64},{1,17},{2,66},{3,19},{4,68},{5,21},{6,70},{7,23},{8,72},{9,... | collective-permute-start | bytes 786440 | tf_op jit(solution)/shard_map/ppermute | solution.py:45
  73.6 11.0 %collective-permute-start.23 = (bf16[128,1024]{1,0:T(8,128)(2,1)S(1)}, bf16[128,1024]{1,0:T(8,128)(2,1)S(1)}, u32[]{:S(2)}, u32[]{:S(2)}) collective-permute-start(bf16[128,1024]{1,0:T(8,128)(2,1)S(1)} %get-tuple-element.58), channel_id=1, source_target_pairs={{0,128},{1,33},{2,130},{3,35},{4,132},{5,37},{6,134},{7,39},{8,136... | collective-permute-start | bytes 786440 | tf_op jit(solution)/shard_map/ppermute | solution.py:45
  73.8 11.0 %collective-permute-start.22 = (bf16[128,1024]{1,0:T(8,128)(2,1)S(1)}, bf16[128,1024]{1,0:T(8,128)(2,1)S(1)}, u32[]{:S(2)}, u32[]{:S(2)}) collective-permute-start(bf16[128,1024]{1,0:T(8,128)(2,1)S(1)} %get-tuple-element.57), channel_id=1, source_target_pairs={{0,192},{1,49},{2,194},{3,51},{4,196},{5,53},{6,198},{7,55},{8,200... | collective-permute-start | bytes 786440 | tf_op jit(solution)/shard_map/ppermute | solution.py:45
  87.1 16.6 %collective-permute-start.28 = (bf16[128,2048]{1,0:T(8,128)(2,1)S(1)}, bf16[128,2048]{1,0:T(8,128)(2,1)S(1)}, u32[]{:S(2)}, u32[]{:S(2)}) collective-permute-start(bf16[128,2048]{1,0:T(8,128)(2,1)S(1)} %slice.38), channel_id=1, source_target_pairs={{0,48},{1,193},{2,50},{3,195},{4,52},{5,197},{6,54},{7,199},{8,56}... | collective-permute-start | bytes 1572872 | tf_op jit(solution)/shard_map/ppermute | solution.py:45
  91.2 12.7 %collective-permute-start.30 = (bf16[128,2048]{1,0:T(8,128)(2,1)S(1)}, bf16[128,2048]{1,0:T(8,128)(2,1)S(1)}, u32[]{:S(2)}, u32[]{:S(2)}) collective-permute-start(bf16[128,2048]{1,0:T(8,128)(2,1)S(1)} %slice.39), channel_id=1, source_target_pairs={{0,16},{1,65},{2,18},{3,67},{4,20},{5,69},{6,22},{7,71},{8,24},{9,... | collective-permute-start | bytes 1572872 | tf_op jit(solution)/shard_map/ppermute | solution.py:45
  92.7 10.6 %collective-permute-start.26 = (bf16[128,1024]{1,0:T(8,128)(2,1)S(1)}, bf16[128,1024]{1,0:T(8,128)(2,1)S(1)}, u32[]{:S(2)}, u32[]{:S(2)}) collective-permute-start(bf16[128,1024]{1,0:T(8,128)(2,1)S(1)} %shard_map.66.refs_0_), channel_id=1, source_target_pairs={{0,64},{1,17},{2,66},{3,19},{4,68},{5,21},{6,70},{7,23},{8,72},{9,... | collective-permute-start | bytes 786440 | tf_op jit(solution)/shard_map/ppermute | solution.py:45
  92.7 16.0 %collective-permute-start.34 = (bf16[128,1024]{1,0:T(8,128)(2,1)S(1)}, bf16[128,1024]{1,0:T(8,128)(2,1)S(1)}, u32[]{:S(2)}, u32[]{:S(2)}) collective-permute-start(bf16[128,1024]{1,0:T(8,128)(2,1)S(1)} %shard_map.66.refs_0_), channel_id=1, source_target_pairs={{0,128},{1,33},{2,130},{3,35},{4,132},{5,37},{6,134},{7,39},{8,136... | collective-permute-start | bytes 786440 | tf_op jit(solution)/shard_map/ppermute | solution.py:45
  94.2 16.1 %collective-permute-start.32 = (bf16[128,1024]{1,0:T(8,128)(2,1)S(1)}, bf16[128,1024]{1,0:T(8,128)(2,1)S(1)}, u32[]{:S(2)}, u32[]{:S(2)}) collective-permute-start(bf16[128,1024]{1,0:T(8,128)(2,1)S(1)} %shard_map.66.refs_0_), channel_id=1, source_target_pairs={{0,192},{1,49},{2,194},{3,51},{4,196},{5,53},{6,198},{7,55},{8,200... | collective-permute-start | bytes 786440 | tf_op jit(solution)/shard_map/ppermute | solution.py:45
  105.3 18.5 %collective-permute-start.31 = (bf16[128,2048]{1,0:T(8,128)(2,1)}, bf16[128,2048]{1,0:T(8,128)(2,1)}, u32[]{:S(2)}, u32[]{:S(2)}) collective-permute-start(bf16[128,2048]{1,0:T(8,128)(2,1)} %shard_map.67), channel_id=1, source_target_pairs={{0,192},{1,49},{2,194},{3,51},{4,196},{5,53},{6,198},{7,55},{8,200... | collective-permute-start | bytes 1572872 | tf_op jit(solution)/shard_map/ppermute | solution.py:45
  110.3 11.2 %collective-permute-start.35 = (bf16[128,2048]{1,0:T(8,128)(2,1)}, bf16[128,2048]{1,0:T(8,128)(2,1)}, u32[]{:S(2)}, u32[]{:S(2)}) collective-permute-start(bf16[128,2048]{1,0:T(8,128)(2,1)} %shard_map.69), channel_id=1, source_target_pairs={{0,128},{1,33},{2,130},{3,35},{4,132},{5,37},{6,134},{7,39},{8,136... | collective-permute-start | bytes 1572872 | tf_op jit(solution)/shard_map/ppermute | solution.py:45
  111.8 15.1 %collective-permute-start.33 = (bf16[128,2048]{1,0:T(8,128)(2,1)}, bf16[128,2048]{1,0:T(8,128)(2,1)}, u32[]{:S(2)}, u32[]{:S(2)}) collective-permute-start(bf16[128,2048]{1,0:T(8,128)(2,1)} %shard_map.68), channel_id=1, source_target_pairs={{0,64},{1,17},{2,66},{3,19},{4,68},{5,21},{6,70},{7,23},{8,72},{9,... | collective-permute-start | bytes 1572872 | tf_op jit(solution)/shard_map/ppermute | solution.py:45
  (19 other events, 114.2 us)
